TPU v7x, 128 devices: a whole 4x4x4 slice. The times are simulated.
128 devices in a mesh: tx: 16 (over x, z), ty: 8 (over y, core).
Axes of the slice: x: 4, y: 4, z: 4, core: 2. Of those that a mesh axis runs over, the one named last changes fastest.
Arguments:
- innovation: float32 [16384, 128], P(('tx', 'ty')), may hold values from -6 to 6
- obs_weight: float32 [16384, 128], P(('tx', 'ty')), may hold values from 0.5 to 4
- obs_operator: float32 [16384, 128, 128], P(('tx', 'ty')), may hold values from -0.5 to 0.5
- block_tile: int32 [16384, 1], P(('tx', 'ty')), may hold values from 0 to 15; in each aligned block of 128 rows (0 to 127, 128 to 255, ...) at most 24 rows name the same one
- owner_counts: int32 [128], P(('tx', 'ty')), may hold values from 64 to 128, as said below
- block_column: int32 [16384], P(('tx', 'ty')), may hold values from 0 to 255
- sea_mask: int32 [4, 1024, 1024], P(None, 'tx', 'ty'), may hold values 0 or 1
- diffusivity: float32 [4, 1024, 1024], P(None, 'tx', 'ty'), may hold values from 0.03 to 0.12
- background_std: float32 [4, 1024, 1024], P(None, 'tx', 'ty'), may hold values from 0.4 to 10.5
- step_counts: int32 [4], replicated, may hold values from 5 to 10, as said below
Outputs:
- control_field: float32 [4, 1024, 1024], P(None, 'tx', 'ty')
- residual: float32 [4, 1024, 1024], P(None, 'tx', 'ty')
Inputs may be any that keep to these rules, and one draw needn't show every extreme that they name: `owner_counts`: at least one owner has all 128 blocks live. `step_counts`: at least one level takes 10 sweeps. `block_tile`: among the 128 blocks of one owner no tile index appears more than 24 times.
All inputs are finite; a program needn't handle non-finite values. No bound on the sum of `sea_mask` on one device may be relied on, other than what follows from the above.
Results may differ from a plain program's by a relative error of at most 0.04.
Values sent between devices are 32-bit elements; how exact they have to be, the bound alone decides.
No kernel may reach another device: no remote copies, remote signals or barrier semaphores. Data moves between devices by JAX's collectives and lax.ppermute only.
A program may use at most 192 MiB of HBM per device.

v0:
```python
import jax
import jax.numpy as jnp
from jax import lax
from jax.sharding import PartitionSpec as P

NSTEP = 10
ITERS = 2


def extended(cells, sides, width):
    for axis, dim in sides:
        count = lax.axis_size(axis)
        ends = count - 1
        head = lax.slice_in_dim(cells, 0, width, axis=dim)
        tail = lax.slice_in_dim(cells, cells.shape[dim] - width, cells.shape[dim], axis=dim)
        cells = jnp.concatenate(
            [
                lax.ppermute(tail, axis, [(i, (i + 1) % count) for i in range(ends)]),
                cells,
                lax.ppermute(head, axis, [((i + 1) % count, i) for i in range(ends)]),
            ],
            axis=dim,
        )
    return cells


def face_weights(mask_pad, kappa_pad):
    centre_m = mask_pad[:, 1:-1, 1:-1]
    centre_k = kappa_pad[:, 1:-1, 1:-1]
    east_face = 0.5 * (centre_m * kappa_pad[:, 2:, 1:-1] + centre_k * mask_pad[:, 2:, 1:-1])
    west_face = 0.5 * (mask_pad[:, :-2, 1:-1] * centre_k + kappa_pad[:, :-2, 1:-1] * centre_m)
    north_face = 0.5 * (centre_m * kappa_pad[:, 1:-1, 2:] + centre_k * mask_pad[:, 1:-1, 2:])
    south_face = 0.5 * (mask_pad[:, 1:-1, :-2] * centre_k + kappa_pad[:, 1:-1, :-2] * centre_m)
    return (east_face, west_face, north_face, south_face)


def diffusion_update(field_in, padded, face_set):
    east_face, west_face, north_face, south_face = face_set
    change = east_face * (padded[:, 2:, 1:-1] - field_in)
    change = change + west_face * (padded[:, :-2, 1:-1] - field_in)
    change = change + north_face * (padded[:, 1:-1, 2:] - field_in)
    change = change + south_face * (padded[:, 1:-1, :-2] - field_in)
    return field_in + change


def spread_field(field_in, mask_float, wide_faces, step_counts):
    margin = NSTEP
    face_set = tuple((face[:, margin:-margin, margin:-margin] for face in wide_faces))

    def one_sweep(sweep_no, current):
        padded = extended(current, (("tx", 1), ("ty", 2)), 1)
        updated = diffusion_update(current, padded, face_set)
        return jnp.where((sweep_no < step_counts)[:, None, None], updated, current)

    return lax.fori_loop(0, NSTEP, one_sweep, field_in * mask_float)


def squares(residual):
    return lax.psum(jnp.sum(residual * residual), ("tx", "ty"))


def body(
    innovation,
    obs_weight,
    obs_operator,
    block_tile,
    owner_counts,
    block_column,
    sea_mask,
    diffusivity,
    background_std,
    step_counts,
):
    tiles_x = lax.axis_size("tx")
    own_blocks = innovation.shape[0]
    capacity = 3 * own_blocks // tiles_x
    slot_total = tiles_x * capacity
    segment_total = sea_mask.size // 128
    mask_float = sea_mask.astype(jnp.float32)
    kappa_masked = diffusivity * mask_float
    stacked = jnp.stack([mask_float, kappa_masked])
    padded_both = extended(stacked, (("tx", 2), ("ty", 3)), NSTEP + 1)
    wide_faces = face_weights(padded_both[0], padded_both[1])

    def spread_op(values):
        return spread_field(values, mask_float, wide_faces, step_counts)

    target = block_tile[:, 0]
    onehot = (target[:, None] == jnp.arange(tiles_x, dtype=jnp.int32)[None, :]).astype(jnp.int32)
    earlier = jnp.cumsum(onehot, axis=0) - onehot
    position = jnp.sum(earlier * onehot, axis=1)
    slot_index = target * capacity + position
    is_live = jnp.arange(own_blocks, dtype=jnp.int32) < owner_counts[0]
    column_buffer = jnp.zeros((slot_total,), jnp.int32).at[slot_index].set(block_column)
    wanted = lax.all_to_all(
        column_buffer.reshape(tiles_x, capacity), "tx", split_axis=0, concat_axis=0, tiled=True
    ).reshape(-1)

    def scatter_segments(values):
        segments = (
            jnp.zeros((segment_total, 128), jnp.float32).at[wanted].add(values.reshape(-1, 128))
        )
        return segments.reshape(sea_mask.shape)

    def send_back(adjoint_cells):
        buffer = jnp.zeros((slot_total, 128), jnp.float32).at[slot_index].set(adjoint_cells)
        arrived = lax.all_to_all(
            buffer.reshape(tiles_x, capacity, 128), "tx", split_axis=0, concat_axis=0, tiled=True
        )
        return scatter_segments(arrived)

    start_weighted = jnp.where(is_live[:, None], obs_weight * innovation, 0.0)
    first_term = send_back(
        jnp.einsum("bij,bi->bj", obs_operator, start_weighted, precision=lax.Precision.HIGHEST)
    )
    right_side = spread_op(background_std * first_term)
    control_field = jnp.zeros_like(right_side)
    residual = right_side
    direction = right_side
    norm_now = squares(residual)
    for iter_no in range(ITERS):
        hessian_spread = background_std * spread_op(direction)
        picked = hessian_spread.reshape(-1, 128)[wanted].reshape(tiles_x, capacity, 128)
        returned = lax.all_to_all(picked, "tx", split_axis=0, concat_axis=0, tiled=True).reshape(
            -1, 128
        )[slot_index]
        observed = jnp.einsum("bij,bj->bi", obs_operator, returned, precision=lax.Precision.HIGHEST)
        weighted = jnp.where(is_live[:, None], obs_weight * observed, 0.0)
        curved = direction + spread_op(
            background_std
            * send_back(
                jnp.einsum("bij,bi->bj", obs_operator, weighted, precision=lax.Precision.HIGHEST)
            )
        )
        step_length = norm_now / lax.psum(jnp.sum(direction * curved), ("tx", "ty"))
        control_field = control_field + step_length * direction
        residual = residual - step_length * curved
        norm_next = squares(residual)
        direction = residual + norm_next / norm_now * direction
        norm_now = norm_next
    return (control_field, residual)


def solution(mesh):
    placed = (
        P(("tx", "ty"), None),
        P(("tx", "ty"), None),
        P(("tx", "ty"), None, None),
        P(("tx", "ty"), None),
        P(("tx", "ty")),
        P(("tx", "ty")),
        P(None, "tx", "ty"),
        P(None, "tx", "ty"),
        P(None, "tx", "ty"),
        P(),
    )
    return jax.shard_map(
        body,
        mesh=mesh,
        in_specs=placed,
        out_specs=(P(None, "tx", "ty"), P(None, "tx", "ty")),
        check_vma=False,
    )
```

profile of v0, /device:TPU:1, one launch (start us, length us, event | category | flops | bytes accessed | tf_op | source)
XLA Modules:
  0.0 1297.8 jit_solution(10174392890755845567)
XLA Ops:
  4.9 8.4 all-to-all-start
  15.0 9.4 fusion.93
  25.9 6.7 all-to-all-start.1
  49.3 7.3 collective-permute-start.22
  67.1 174.3 %while.65 = (s32[]{:T(128)}, f32[4,64,128]{2,1,0:T(8,128)S(1)}, s32[4]{0:T(128)S(1)}, f32[4,64,128]{2,1,0:T(8,128)S(1)}, f32[4,64,128]{2,1,0:T(8,128)S(1)}, /*in...) while((s32[]{:T(128)}, f32[4,64,128]{2,1,0:T(8,128)S(1)}, s32[4]{0:T(128)S(1)}, ...), condition=%wide.region_6.7_spmd, body=%wide.region_5.6_spmd.sunk | while | flops 755718 | bytes 1362641 | solution.py:55
  241.4 181.1 %while.66 = (s32[]{:T(128)}, f32[4,64,128]{2,1,0:T(8,128)S(1)}, s32[4]{0:T(128)S(1)}, f32[4,64,128]{2,1,0:T(8,128)S(1)}, f32[4,64,128]{2,1,0:T(8,128)S(1)}, /*in...) while((s32[]{:T(128)}, f32[4,64,128]{2,1,0:T(8,128)S(1)}, s32[4]{0:T(128)S(1)}, ...), condition=%wide.region_10.11_spmd, body=%wide.region_9.10_spmd.sunk | while | flops 755718 | bytes 1362641 | solution.py:55
  424.2 15.7 %all-to-all-start.2 = ((f32[16,24,128]{2,1,0:T(8,128)}), f32[16,24,128]{2,1,0:T(8,128)S(1)}, u32[]{:S(2)}, u32[]{:S(2)}) async-start(f32[16,24,128]{2,1,0:T(8,128)} %bitcast.16), calls=%async_computation.2 | async-start | bytes 393216 | tf_op jit(solution)/shard_map/all_to_all | solution.py:124
  440.0 6.9 all-to-all-done.2
  447.5 15.4 %fusion.94 = f32[128,1,128]{2,1,0:T(1,128)S(1)} fusion(f32[128,128,1]{1,2,0:T(1,128)S(1)} %bitcast.82, f32[128,128,128]{2,1,0:T(8,128)} %param.22), kind=kOutput, calls=%fused_computation.200 | convolution fusion | flops 25165824 | bytes 8519680 | tf_op jit(solution)/shard_map/bij,bj->bi/dot_general | solution.py:127
  463.0 9.4 fusion.95
  477.4 7.0 all-to-all-done.3
  487.2 173.8 %while.67 = (s32[]{:T(128)}, f32[4,64,128]{2,1,0:T(8,128)S(1)}, s32[4]{0:T(128)S(1)}, f32[4,64,128]{2,1,0:T(8,128)S(1)}, f32[4,64,128]{2,1,0:T(8,128)S(1)}, /*in...) while((s32[]{:T(128)}, f32[4,64,128]{2,1,0:T(8,128)S(1)}, s32[4]{0:T(128)S(1)}, ...), condition=%wide.region_14.15_spmd, body=%wide.region_13.14_spmd.sunk | while | flops 755718 | bytes 1362641 | solution.py:55
  661.7 74.6 %all-reduce = (f32[]{:T(128)}, f32[]{:T(128)}) all-reduce(f32[]{:T(128)} %get-tuple-element.628, f32[]{:T(128)} %get-tuple-element.627), channel_id=1, replica_groups=mesh['tx'=16,'ty'=8] {'tx','ty'}, use_global_device_ids=true, to_apply=%region_8.9 | all-reduce | flops 2 | bytes 16 | tf_op jit(solution)/shard_map/psum | solution.py:59
  738.2 63.1 %psum.30 = f32[]{:T(128)} all-reduce(f32[]{:T(128)} %multiply_reduce_fusion.1), channel_id=1, replica_groups=mesh['tx'=16,'ty'=8] {'tx','ty'}, use_global_device_ids=true, to_apply=%region_18.19 | all-reduce | flops 1 | bytes 8 | tf_op jit(solution)/shard_map/psum | solution.py:59
  802.6 171.6 %while.68 = (s32[]{:T(128)}, f32[4,64,128]{2,1,0:T(8,128)S(1)}, s32[4]{0:T(128)S(1)}, f32[4,64,128]{2,1,0:T(8,128)S(1)}, f32[4,64,128]{2,1,0:T(8,128)S(1)}, /*in...) while((s32[]{:T(128)}, f32[4,64,128]{2,1,0:T(8,128)S(1)}, s32[4]{0:T(128)S(1)}, ...), condition=%wide.region_20.21_spmd, body=%wide.region_19.20_spmd.sunk | while | flops 755718 | bytes 1362641 | solution.py:55
  975.3 31.5 %all_to_all.34 = f32[16,24,128]{2,1,0:T(8,128)S(1)} all-to-all(f32[16,24,128]{2,1,0:T(8,128)S(1)} %bitcast.72), channel_id=1, replica_groups=mesh['tx'=16,'ty'=8] {'tx'}, dimensions={0} | all-to-all | bytes 393216 | tf_op jit(solution)/shard_map/all_to_all | solution.py:124
  1007.5 15.4 %fusion.96 = f32[128,1,128]{2,1,0:T(1,128)S(1)} fusion(f32[128,128,1]{1,2,0:T(1,128)S(1)} %bitcast.81, f32[128,128,128]{2,1,0:T(8,128)} %param.22), kind=kOutput, calls=%fused_computation.202 | convolution fusion | flops 25165824 | bytes 8519680 | tf_op jit(solution)/shard_map/bij,bj->bi/dot_general | solution.py:127
  1023.0 9.4 fusion.97
  1033.3 10.4 all_to_all.35
  1046.3 174.1 %while.69 = (s32[]{:T(128)}, f32[4,64,128]{2,1,0:T(8,128)S(1)}, s32[4]{0:T(128)S(1)}, f32[4,64,128]{2,1,0:T(8,128)S(1)}, f32[4,64,128]{2,1,0:T(8,128)S(1)}, /*in...) while((s32[]{:T(128)}, f32[4,64,128]{2,1,0:T(8,128)S(1)}, s32[4]{0:T(128)S(1)}, ...), condition=%wide.region_24.25_spmd, body=%wide.region_23.24_spmd.sunk | while | flops 755718 | bytes 1362641 | solution.py:55
  1052.5 6.7 collective-permute-start.18
  1149.3 6.6 collective-permute-start.17
  1167.4 6.7 collective-permute-start.17
  1221.1 74.5 %psum.31 = f32[]{:T(128)} all-reduce(f32[]{:T(128)} %get-tuple-element.701), channel_id=1, replica_groups=mesh['tx'=16,'ty'=8] {'tx','ty'}, use_global_device_ids=true, to_apply=%region_26.27 | all-reduce | flops 1 | bytes 8 | tf_op jit(solution)/shard_map/psum | solution.py:135
  (762 shorter events, 902.3 us)
Async XLA Ops:
  4.9 21.0 %all-to-all-start = ((s32[16,1,24]{2,1,0:T(1,128)}), s32[16,1,24]{2,1,0:T(1,128)S(1)}, u32[]{:S(2)}, u32[]{:S(2)}) async-start(s32[16,1,24]{2,1,0:T(1,128)} %all_to_all.21), calls=%async_computation | async-start | bytes 16384 | tf_op jit(solution)/shard_map/all_to_all | solution.py:95
  25.9 13.6 %all-to-all-start.1 = ((f32[16,24,128]{2,1,0:T(8,128)}), f32[16,24,128]{2,1,0:T(8,128)S(1)}, u32[]{:S(2)}, u32[]{:S(2)}) async-start(f32[16,24,128]{2,1,0:T(8,128)} %bitcast.8), calls=%async_computation.1 | async-start | bytes 393216 | tf_op jit(solution)/shard_map/all_to_all | solution.py:107
  49.3 11.6 collective-permute-start.22
  56.6 8.7 collective-permute-start.23
  132.8 7.9 collective-permute-start
  150.9 7.9 collective-permute-start
  169.0 7.9 collective-permute-start
  187.1 7.9 collective-permute-start
  205.2 7.9 collective-permute-start
  223.3 7.9 collective-permute-start
  241.5 7.9 collective-permute-start.4
  259.6 7.9 collective-permute-start.4
  313.9 7.9 collective-permute-start.4
  332.0 7.9 collective-permute-start.4
  424.2 22.6 %all-to-all-start.2 = ((f32[16,24,128]{2,1,0:T(8,128)}), f32[16,24,128]{2,1,0:T(8,128)S(1)}, u32[]{:S(2)}, u32[]{:S(2)}) async-start(f32[16,24,128]{2,1,0:T(8,128)} %bitcast.16), calls=%async_computation.2 | async-start | bytes 393216 | tf_op jit(solution)/shard_map/all_to_all | solution.py:124
  473.9 10.6 all-to-all-start.3
  493.3 8.6 collective-permute-start.10
  588.6 7.9 collective-permute-start.8
  919.9 7.9 collective-permute-start.12
  938.0 7.9 collective-permute-start.12
  1052.5 8.8 collective-permute-start.18
  1148.0 8.0 collective-permute-start.16
  1166.1 8.0 collective-permute-start.16
  1184.2 7.9 collective-permute-start.16
  (189 other events, 1313.7 us)
where the time goes:
time: 1310 us; the launch traced here: 1300 us
  starting transfers between devices  639 us (49%)
  waiting for transfers between devices  292 us (22%)
  blocking collectives  254 us (19%)
  matrix products  58.9 us (4%)
  other arithmetic  26.5 us (2%)
  local copies, waits for them, and re-layouts  17 us (1%)
    ppermute x102, starting transfers between devices, extended(): lax.ppermute(tail, axis, [(i, (i + 1) % count) for i in range(ends)])  441 us
    ppermute x102, waiting for transfers between devices, extended(): lax.ppermute(head, axis, [((i + 1) % count, i) for i in range(ends)])  227 us
    ppermute x102, starting transfers between devices, extended(): lax.ppermute(head, axis, [((i + 1) % count, i) for i in range(ends)])  164 us
    psum x2, blocking collectives, squares(): return lax.psum(jnp.sum(residual * residual), ('tx', 'ty'))  138 us
    psum x1, blocking collectives, body(): step_length = norm_now / lax.psum(jnp.sum(direction * curved), ('tx', 'ty'))  74.5 us
    ppermute x102, waiting for transfers between devices, extended(): lax.ppermute(tail, axis, [(i, (i + 1) % count) for i in range(ends)])  44.7 us
    all_to_all x1, blocking collectives, body(): lax.all_to_all(picked, 'tx', split_axis=0, concat_axis=0, tiled=True)  31.5 us
    dot_general x2, matrix products, body(): jnp.einsum('bij,bj->bi', obs_operator, returned, precision=lax.Precision....  30.8 us
  transfers between devices with their start and end apart: 208, of which 156 were waited for; matrix products, arithmetic and copies ran while one was open for 1% of the time, Pallas kernels for 0%

commit v1 on v0

v1 whole, which is shorter than its diff:
```python
import jax
import jax.numpy as jnp
from jax import lax
from jax.experimental import pallas as pl
from jax.experimental.pallas import tpu as pltpu
from jax.sharding import PartitionSpec as P

F32 = jnp.float32
BF16 = jnp.bfloat16

LEV = 4
CX = 64
CY = 128
NSTEP = 10
MIN_STEPS = 5
HALO = 2 * NSTEP
SIDE = 24
EXT = CX + 2 * SIDE
ROWS = LEV * EXT
OWN = 128
TX = 16
TY = 8
CAP = 24
SLOTS = TX * CAP
LISTED = 3 * CAP
PART = 80
GROUP = 16
WIDE = 16
STRIP = 48
LAST = STRIP + 8


def iota(shape, dim):
    return lax.broadcasted_iota(jnp.int32, shape, dim)


def thirds(values):
    high = values.astype(BF16)
    rest = values - high.astype(F32)
    middle = rest.astype(BF16)
    low = (rest - middle.astype(F32)).astype(BF16)
    return high, middle, low


def pick(onehot, values):
    high, middle, low = thirds(values)
    total = jnp.dot(onehot, high, preferred_element_type=F32)
    total = total + jnp.dot(onehot, middle, preferred_element_type=F32)
    return total + jnp.dot(onehot, low, preferred_element_type=F32)


def as_onehot(hit):
    return jnp.where(hit, 1.0, 0.0).astype(BF16)


def slot_tables(tile_ref):
    down = iota((OWN, OWN), 0)
    across = iota((OWN, OWN), 1)
    tile_row = tile_ref[...].astype(F32)
    spread = jnp.broadcast_to(tile_row, (OWN, OWN))
    tile_col = jnp.sum(jnp.where(down == across, spread, 0.0), axis=1, keepdims=True)
    same = spread == tile_col
    rank_row = jnp.sum(jnp.where(same & (down < across), 1.0, 0.0), axis=0, keepdims=True)
    rank_col = jnp.sum(jnp.where(same & (across < down), 1.0, 0.0), axis=1, keepdims=True)
    return tile_row, rank_row, tile_col, rank_col


def write_parts(parts_ref, slots):
    for tile in range(TX):
        for side in (-1, 0, 1):
            source = tile + side
            rows = pl.ds((side + 1) * CAP, CAP)
            if 0 <= source < TX:
                parts_ref[tile, rows, :] = slots[source * CAP : (source + 1) * CAP]
            else:
                parts_ref[tile, rows, :] = jnp.zeros((CAP, 128), F32)


def to_slots(tables, adjoint):
    tile_row, rank_row, _, _ = tables
    slot_row = (tile_row * CAP + rank_row).astype(jnp.int32)
    return pick(as_onehot(iota((SLOTS, OWN), 0) == slot_row), adjoint)


def from_slots(tables, returned):
    _, _, tile_col, rank_col = tables
    slot_col = (tile_col * CAP + rank_col).astype(jnp.int32)
    return pick(as_onehot(iota((OWN, SLOTS), 1) == slot_col), returned)


def listed_columns(tables, column_ref):
    tile_row, _, _, rank_col = tables
    column_row = column_ref[...].astype(F32)
    tile_no = iota((TX, OWN), 0).astype(F32)
    lane = iota((OWN, 128), 1)
    rank = rank_col.astype(jnp.int32)
    total = jnp.zeros((TX, 128), F32)
    for side in (-1, 0, 1):
        mine = jnp.where(tile_row == tile_no + side, column_row, 0.0).astype(BF16)
        place = as_onehot(rank + (side + 1) * CAP == lane)
        total = total + jnp.dot(mine, place, preferred_element_type=F32)
    return total


def live_columns(count_ref, weighted):
    return jnp.where(iota((OWN, OWN), 1) < count_ref[0], weighted.T, 0.0)


def group_columns(columns_ref, step):
    turned = pltpu.roll(columns_ref[...], lax.rem(OWN - step * GROUP, OWN), 1)
    return turned[:, :GROUP]


def first_kernel(
    count_ref, tile_ref, column_ref, innovation_ref, weight_ref, operator_ref,
    parts_ref, adjoint_ref, columns_ref,
):
    step = pl.program_id(0)

    @pl.when(step == 0)
    def _():
        columns_ref[...] = live_columns(count_ref, weight_ref[...] * innovation_ref[...])

    columns = group_columns(columns_ref, step)
    rows = []
    for k in range(GROUP):
        rows.append(jnp.sum(operator_ref[k] * columns[:, k : k + 1], axis=0, keepdims=True))
    adjoint_ref[pl.ds(pl.multiple_of(step * GROUP, GROUP), GROUP), :] = jnp.concatenate(rows, axis=0)

    @pl.when(step == pl.num_programs(0) - 1)
    def _():
        tables = slot_tables(tile_ref)
        write_parts(parts_ref, to_slots(tables, adjoint_ref[...]))
        listed = listed_columns(tables, column_ref)
        for tile in range(TX):
            parts_ref[tile, pl.ds(LISTED, 8), :] = jnp.broadcast_to(listed[tile : tile + 1], (8, 128))


def middle_kernel(
    count_ref, tile_ref, weight_ref, returned_ref, earlier_ref, sums_in_ref, operator_ref,
    parts_ref, adjoint_ref, sums_ref, columns_ref, segments_ref,
):
    step = pl.program_id(0)

    @pl.when(step == 0)
    def _():
        columns_ref[...] = live_columns(count_ref, weight_ref[...])
        segments_ref[...] = from_slots(slot_tables(tile_ref), returned_ref[...])

    columns = group_columns(columns_ref, step)
    here = pl.ds(pl.multiple_of(step * GROUP, GROUP), GROUP)
    segments = segments_ref[here, :]
    rows = []
    for k in range(GROUP):
        block = operator_ref[k]
        observed = jnp.sum(block * segments[k : k + 1], axis=1, keepdims=True)
        rows.append(jnp.sum(block * (observed * columns[:, k : k + 1]), axis=0, keepdims=True))
    adjoint_ref[here, :] = jnp.concatenate(rows, axis=0)

    @pl.when(step == pl.num_programs(0) - 1)
    def _():
        adjoint = adjoint_ref[...]
        segments = segments_ref[...]
        write_parts(parts_ref, to_slots(slot_tables(tile_ref), adjoint))
        known = jnp.sum(earlier_ref[...] * segments, axis=0, keepdims=True)
        new = jnp.sum(adjoint * segments, axis=0, keepdims=True)
        sums = jnp.concatenate([sums_in_ref[2:4], known, new, jnp.zeros((4, 128), F32)], axis=0)
        sums_ref[...] = sums
        for tile in range(TX):
            parts_ref[tile, pl.ds(LISTED, 8), :] = sums
        adjoint_ref[...] = adjoint + earlier_ref[...]


def whole(shape):
    return pl.BlockSpec(shape, lambda i: (0,) * len(shape))


SCALARS = pl.BlockSpec(memory_space=pltpu.SMEM)
OPERATORS = pl.BlockSpec((GROUP, 128, 128), lambda i: (i, 0, 0))
PARTS = jax.ShapeDtypeStruct((TX, PART, 128), F32)
SQUARE = jax.ShapeDtypeStruct((OWN, 128), F32)
SUMS = jax.ShapeDtypeStruct((8, 128), F32)


def run_first(counts, tile, column, innovation, weight, operator):
    return pl.pallas_call(
        first_kernel,
        grid=(OWN // GROUP,),
        in_specs=[
            SCALARS, whole((1, OWN)), whole((1, OWN)), whole((OWN, 128)), whole((OWN, 128)), OPERATORS,
        ],
        out_specs=[whole((TX, PART, 128)), whole((OWN, 128))],
        out_shape=[PARTS, SQUARE],
        scratch_shapes=[pltpu.VMEM((OWN, OWN), F32)],
        cost_estimate=pl.CostEstimate(flops=4 * 128**3, bytes_accessed=9 << 20, transcendentals=0),
        name="first_adjoint",
    )(counts, tile, column, innovation, weight, operator)


def run_middle(counts, tile, weight, returned, earlier, sums, operator):
    return pl.pallas_call(
        middle_kernel,
        grid=(OWN // GROUP,),
        in_specs=[
            SCALARS, whole((1, OWN)), whole((OWN, 128)), whole((SLOTS, 128)), whole((OWN, 128)),
            whole((8, 128)), OPERATORS,
        ],
        out_specs=[whole((TX, PART, 128)), whole((OWN, 128)), whole((8, 128))],
        out_shape=[PARTS, SQUARE, SUMS],
        scratch_shapes=[pltpu.VMEM((OWN, OWN), F32), pltpu.VMEM((OWN, 128), F32)],
        cost_estimate=pl.CostEstimate(flops=8 * 128**3, bytes_accessed=10 << 20, transcendentals=0),
        name="observe",
    )(counts, tile, weight, returned, earlier, sums, operator)


def scatter(parts_ref, listed):
    column = listed.astype(jnp.int32)
    level = column >> 6
    cell = column & (CX - 1)
    lane = iota((TX, 128), 1)
    left = lane < CAP
    right = lane >= 2 * CAP
    place = jnp.where(left, cell - (CX - SIDE), jnp.where(right, cell + CX + SIDE, cell + SIDE))
    good = (lane < LISTED) & (place >= 0) & (place < EXT)
    row = jnp.where(good, level * EXT + place, -1)
    turned = pltpu.roll(row, PART, 1)
    one = jnp.where(lane < PART, row, turned)
    two = jnp.where(
        lane < 2 * PART - 128,
        turned,
        jnp.where(lane < 3 * PART - 128, pltpu.roll(row, 2 * PART - 128, 1), -1),
    )
    triple = jnp.concatenate([one, two], axis=1)
    down = iota((ROWS, 256), 0)
    total = jnp.zeros((ROWS, 128), F32)
    blank = jnp.zeros((256 - 3 * PART, 128), BF16)
    for source in range(TX):
        onehot = as_onehot(down == triple[source : source + 1])
        stacked = jnp.concatenate([*thirds(parts_ref[source]), blank], axis=0)
        total = total + jnp.dot(onehot, stacked, preferred_element_type=F32)
    return total


def edges(field, even):
    lane = iota((EXT, 128), 1)
    west = jnp.zeros((EXT, 128), F32)
    east = jnp.zeros((EXT, 128), F32)
    for level in range(LEV):
        part = field[level * EXT : (level + 1) * EXT]
        here = (lane >= 32 * level) & (lane < 32 * level + HALO)
        low = pltpu.roll(part, 32 * level, 1) if level else part
        west = jnp.where(here, low, west)
        east = jnp.where(here, pltpu.roll(part, (32 * level + HALO) % 128, 1), east)
    return jnp.where(even, east, west), jnp.where(even, west, east)


def parity(axis):
    return lax.axis_index(axis) % 2 == 0


def open_kernel(
    where_ref, parts_ref, sigma_ref, mask_ref, diffusivity_ref, near_ref, far_ref,
    field_ref, sigma_ext_ref, kappa_ext_ref, pair_ref, other_ref, listed_ref,
):
    row_no = where_ref[0]
    even_row = row_no % 2 == 0
    even = where_ref[1] % 2 == 0
    not_first = jnp.where(row_no > 0, 1.0, 0.0)
    not_last = jnp.where(row_no < TX - 1, 1.0, 0.0)
    for level in range(LEV):
        base = level * EXT
        near_k, far_k = near_ref[0, level], far_ref[0, level]
        near_s, far_s = near_ref[1, level], far_ref[1, level]
        kappa_ext_ref[pl.ds(base, SIDE), :] = jnp.where(even_row, far_k, near_k) * not_first
        kappa_ext_ref[pl.ds(base + SIDE, CX), :] = diffusivity_ref[level] * mask_ref[level].astype(F32)
        kappa_ext_ref[pl.ds(base + SIDE + CX, SIDE), :] = jnp.where(even_row, near_k, far_k) * not_last
        sigma_ext_ref[pl.ds(base, SIDE), :] = jnp.where(even_row, far_s, near_s)
        sigma_ext_ref[pl.ds(base + SIDE, CX), :] = sigma_ref[level]
        sigma_ext_ref[pl.ds(base + SIDE + CX, SIDE), :] = jnp.where(even_row, near_s, far_s)
    sigma_ext_ref[...] = jnp.where(kappa_ext_ref[...] > 0.0, sigma_ext_ref[...], 0.0)
    listed = jnp.concatenate([parts_ref[k, pl.ds(LISTED, 1), :] for k in range(TX)], axis=0)
    listed_ref[...] = listed
    field = scatter(parts_ref, listed) * sigma_ext_ref[...]
    field_ref[...] = field
    pair_ref[0], other_ref[0] = edges(field, even)
    pair_ref[1], other_ref[1] = edges(kappa_ext_ref[...], even)


def gather_kernel(where_ref, parts_ref, sigma_ext_ref, listed_ref, field_ref, pair_ref, other_ref):
    field = scatter(parts_ref, listed_ref[...]) * sigma_ext_ref[...]
    field_ref[...] = field
    pair_ref[0], other_ref[0] = edges(field, where_ref[1] % 2 == 0)


FIRST_ROW = SIDE - NSTEP - 6


def last_gather_kernel(where_ref, parts_ref, sigma_ext_ref, listed_ref, field_ref, message_ref):
    field = scatter(parts_ref, listed_ref[...]) * sigma_ext_ref[...]
    field_ref[...] = field
    lane = iota((STRIP, 128), 1)
    west = jnp.zeros((STRIP, 128), F32)
    east = jnp.zeros((STRIP, 128), F32)
    for level in range(LEV):
        for half in range(2):
            start = level * EXT + FIRST_ROW + half * STRIP
            part = field[start : start + STRIP]
            at = WIDE * (2 * level + half)
            here = (lane >= at) & (lane < at + NSTEP)
            west = jnp.where(here, pltpu.roll(part, at, 1) if at else part, west)
            east = jnp.where(here, pltpu.roll(part, (at + NSTEP) % 128, 1), east)
    sums = parts_ref[0, pl.ds(LISTED, 8), :]
    for source in range(1, TX):
        sums = sums + parts_ref[source, pl.ds(LISTED, 8), :]
    me = where_ref[1]
    for band in range(TY):
        message_ref[band, pl.ds(0, STRIP), :] = jnp.where(band == me + 1, east, west)
        message_ref[band, pl.ds(STRIP, 8), :] = sums


def widen(work_ref, field_ref, west_of, east_of, reach):
    lane = iota((EXT, 128), 1)
    for level in range(LEV):
        part = field_ref[pl.ds(level * EXT, EXT), :]
        first = jnp.where(
            (lane >= HALO - reach) & (lane < HALO), west_of(level), pltpu.roll(part, HALO, 1)
        )
        second = jnp.where(
            (lane >= 128 - HALO) & (lane < 128 - HALO + reach),
            east_of(level),
            pltpu.roll(part, 128 - HALO, 1),
        )
        work_ref[pl.ds(level, EXT, stride=8), :] = first
        work_ref[pl.ds(LEV + level, EXT, stride=8), :] = second


def tile_part(work_ref, level):
    lane = iota((CX, 128), 1)
    first = work_ref[pl.ds(SIDE * 8 + level, CX, stride=8), :]
    second = work_ref[pl.ds(SIDE * 8 + LEV + level, CX, stride=8), :]
    return jnp.where(lane < CY // 2, pltpu.roll(first, 128 - HALO, 1), pltpu.roll(second, HALO, 1))


def level_counts(count_ref):
    level = iota((8, 128), 0) % LEV
    counts = jnp.full((8, 128), count_ref[0], jnp.int32)
    for k in range(1, LEV):
        counts = jnp.where(level == k, count_ref[k], counts)
    return counts


def sweeps(work_ref, along_ref, across_ref, counts, first_row, end_row):
    def one(number, masked):
        active = counts > number
        flux = None
        now = work_ref[pl.ds(first_row * 8, 8), :]
        for row in range(first_row, end_row):
            here = pl.ds(row * 8, 8)
            side = across_ref[here, :] * (pltpu.roll(now, 127, 1) - now)
            change = side - pltpu.roll(side, 1, 1)
            if flux is not None:
                change = change - flux
            after = None
            if row + 1 < end_row:
                after = work_ref[pl.ds((row + 1) * 8, 8), :]
                flux = along_ref[here, :] * (after - now)
                change = change + flux
            if masked:
                change = jnp.where(active, change, 0.0)
            work_ref[here, :] = now + change
            now = after

    lax.fori_loop(0, MIN_STEPS, lambda n, c: (one(n, False), c)[1], 0)
    lax.fori_loop(MIN_STEPS, NSTEP, lambda n, c: (one(n, True), c)[1], 0)


def faces(work_ref, along_ref, across_ref):
    def mask_of(kappa):
        return jnp.where(kappa > 0.0, 1.0, 0.0)

    for row in range(EXT):
        here = pl.ds(row * 8, 8)
        kappa = work_ref[here, :]
        mask = mask_of(kappa)
        if row + 1 < EXT:
            after = work_ref[pl.ds((row + 1) * 8, 8), :]
            along_ref[here, :] = 0.5 * (mask * after + kappa * mask_of(after))
        else:
            along_ref[here, :] = jnp.zeros((8, 128), F32)
        beside = pltpu.roll(kappa, 127, 1)
        across_ref[here, :] = 0.5 * (mask * beside + kappa * mask_of(beside))


def strips(packed):
    west, east = packed

    def west_of(level):
        return pltpu.roll(west, 128 - 32 * level, 1) if level else west

    def east_of(level):
        return pltpu.roll(east, (2 * 128 - HALO - 32 * level) % 128, 1)

    return west_of, east_of


def from_pairs(near_ref, far_ref, which, even):
    near, far = near_ref[which], far_ref[which]
    return jnp.where(even, far, near), jnp.where(even, near, far)


def send_segments(picked_ref, listed_ref, segments):
    listed = jnp.concatenate([listed_ref[...], jnp.zeros((128 - TX, 128), F32)], axis=0).T
    mine = listed[CAP : 2 * CAP].astype(jnp.int32)
    lane = iota((CAP, LEV * CX), 1)
    hits = [
        jnp.where(mine[:, source : source + 1] == lane, 1.0, 0.0) for source in range(TX)
    ]
    onehot = jnp.concatenate(hits, axis=0).astype(BF16)
    picked_ref[...] = pick(onehot, segments)


INNER = (SIDE - NSTEP, SIDE + CX + NSTEP)
OUTER = (SIDE - HALO, SIDE + CX + HALO)


def spread_first_kernel(
    where_ref, count_ref, field_ref, kappa_ext_ref, near_ref, far_ref, sigma_ref, listed_ref,
    picked_ref, once_ref, twice_ref, along_ref, across_ref, work_ref,
):
    band = where_ref[1]
    even = band % 2 == 0
    west, east = from_pairs(near_ref, far_ref, 1, even)
    west = west * jnp.where(band > 0, 1.0, 0.0)
    east = east * jnp.where(band < TY - 1, 1.0, 0.0)
    widen(work_ref, kappa_ext_ref, *strips((west, east)), HALO)
    faces(work_ref, along_ref, across_ref)
    widen(work_ref, field_ref, *strips(from_pairs(near_ref, far_ref, 0, even)), HALO)
    counts = level_counts(count_ref)
    sweeps(work_ref, along_ref, across_ref, counts, *OUTER)
    for level in range(LEV):
        once_ref[level] = tile_part(work_ref, level)
    sweeps(work_ref, along_ref, across_ref, counts, *INNER)
    parts = []
    for level in range(LEV):
        part = tile_part(work_ref, level)
        twice_ref[level] = part
        parts.append(part * sigma_ref[level])
    send_segments(picked_ref, listed_ref, jnp.concatenate(parts, axis=0))


def spread_next_kernel(
    where_ref, count_ref, field_ref, near_ref, far_ref, sigma_ref, listed_ref, along_ref, across_ref,
    once_ref, twice_ref,
    picked_ref, image_ref, work_ref,
):
    even = where_ref[1] % 2 == 0
    widen(work_ref, field_ref, *strips(from_pairs(near_ref, far_ref, 0, even)), HALO)
    counts = level_counts(count_ref)
    sweeps(work_ref, along_ref, across_ref, counts, *OUTER)
    for level in range(LEV):
        image_ref[level] = once_ref[level] + tile_part(work_ref, level)
    sweeps(work_ref, along_ref, across_ref, counts, *INNER)
    parts = []
    for level in range(LEV):
        parts.append((twice_ref[level] + tile_part(work_ref, level)) * sigma_ref[level])
    send_segments(picked_ref, listed_ref, jnp.concatenate(parts, axis=0))


def spread_last_kernel(
    where_ref, count_ref, field_ref, message_ref, along_ref, across_ref, start_ref, image_ref,
    control_ref, residual_ref, work_ref,
):
    band = where_ref[1]
    west = message_ref[jnp.maximum(band - 1, 0), pl.ds(0, STRIP), :]
    east = message_ref[jnp.minimum(band + 1, TY - 1), pl.ds(0, STRIP), :]
    blank = jnp.zeros((FIRST_ROW, 128), F32)

    def side_of(packed, shift):
        def of(level):
            halves = [
                pltpu.roll(packed, (2 * 128 + shift - WIDE * (2 * level + half)) % 128, 1)
                for half in range(2)
            ]
            return jnp.concatenate([blank, *halves, blank], axis=0)

        return of

    widen(work_ref, field_ref, side_of(west, HALO - NSTEP), side_of(east, 128 - HALO), NSTEP)
    counts = level_counts(count_ref)
    sweeps(work_ref, along_ref, across_ref, counts, *INNER)

    sums = message_ref[0, pl.ds(STRIP, 8), :]
    for source in range(1, TY):
        sums = sums + message_ref[source, pl.ds(STRIP, 8), :]
    sums = jnp.sum(sums, axis=1, keepdims=True)
    start_start = sums[0:1]
    start_image = sums[0:1] + sums[1:2]
    image_image = sums[2:3]
    image_second = sums[2:3] + sums[3:4]
    step = start_start / start_image
    norm = step * step * image_image - 2.0 * step * start_image + start_start
    ratio = norm / start_start
    next_next = start_image - 2.0 * step * image_image + step * step * image_second
    next_start = start_image - step * image_image
    curvature = next_next + 2.0 * ratio * next_start + ratio * ratio * start_image
    second = norm / curvature
    for level in range(LEV):
        start = start_ref[level]
        image = image_ref[level]
        twice = image + tile_part(work_ref, level)
        remainder = start - step * image
        direction = remainder + ratio * start
        curved = (1.0 + ratio) * image - step * twice
        control_ref[level] = step * start + second * direction
        residual_ref[level] = remainder - second * curved


WORK = [pltpu.VMEM((EXT * 8, 128), F32)]
TILE = jax.ShapeDtypeStruct((LEV, CX, CY), F32)
WIDENED = jax.ShapeDtypeStruct((ROWS, 128), F32)
LAID = jax.ShapeDtypeStruct((EXT * 8, 128), F32)
LISTS = jax.ShapeDtypeStruct((TX, 128), F32)
PICKED = jax.ShapeDtypeStruct((SLOTS, 128), F32)


def edge_shape(number):
    return jax.ShapeDtypeStruct((number, EXT, 128), F32)


def tile_call(kernel, out_shape, scalars, arrays, name, scratch=()):
    vmem = pl.BlockSpec(memory_space=pltpu.VMEM)
    return pl.pallas_call(
        kernel,
        in_specs=[SCALARS] * len(scalars) + [vmem] * len(arrays),
        out_specs=[vmem] * len(out_shape),
        out_shape=list(out_shape),
        scratch_shapes=list(scratch),
        compiler_params=pltpu.CompilerParams(vmem_limit_bytes=32 << 20),
        name=name,
    )(*scalars, *arrays)


def swap_neighbours(for_pair, for_other, axis):
    count = lax.axis_size(axis)
    pairs = [(i, i ^ 1) for i in range(count)]
    others = [(i, (i + (1 if i % 2 else -1)) % count) for i in range(count)]
    return lax.ppermute(for_pair, axis, pairs), lax.ppermute(for_other, axis, others)


def exchange(parts):
    return lax.all_to_all(parts, "tx", split_axis=0, concat_axis=0, tiled=True)


def body(
    innovation,
    obs_weight,
    obs_operator,
    block_tile,
    owner_counts,
    block_column,
    sea_mask,
    diffusivity,
    background_std,
    step_counts,
):
    where = jnp.stack([lax.axis_index("tx"), lax.axis_index("ty")]).astype(jnp.int32)
    tile = block_tile.reshape(1, OWN)
    column = block_column.reshape(1, OWN)

    masked = diffusivity * sea_mask.astype(F32)
    low = jnp.stack([masked[:, :SIDE], background_std[:, :SIDE]])
    high = jnp.stack([masked[:, CX - SIDE :], background_std[:, CX - SIDE :]])
    even = parity("tx")
    near_x, far_x = swap_neighbours(jnp.where(even, high, low), jnp.where(even, low, high), "tx")

    parts, adjoint = run_first(owner_counts, tile, column, innovation, obs_weight, obs_operator)
    parts = exchange(parts)
    field, sigma_ext, kappa_ext, pair, other, listed = tile_call(
        open_kernel,
        (WIDENED, WIDENED, WIDENED, edge_shape(2), edge_shape(2), LISTS),
        (where,),
        (parts, background_std, sea_mask, diffusivity, near_x, far_x),
        "open_tile",
    )
    near, far = swap_neighbours(pair, other, "ty")
    picked, once, twice, along, across = tile_call(
        spread_first_kernel,
        (PICKED, TILE, TILE, LAID, LAID),
        (where, step_counts),
        (field, kappa_ext, near, far, background_std, listed),
        "spread_first",
        WORK,
    )
    returned = exchange(picked.reshape(TX, CAP, 128)).reshape(SLOTS, 128)
    sums = jnp.zeros((8, 128), F32)
    parts, adjoint, sums = run_middle(
        owner_counts, tile, obs_weight, returned, adjoint, sums, obs_operator
    )
    parts = exchange(parts)
    field, pair, other = tile_call(
        gather_kernel,
        (WIDENED, edge_shape(1), edge_shape(1)),
        (where,),
        (parts, sigma_ext, listed),
        "gather_tile",
    )
    near, far = swap_neighbours(pair, other, "ty")
    picked, image = tile_call(
        spread_next_kernel,
        (PICKED, TILE),
        (where, step_counts),
        (field, near, far, background_std, listed, along, across, once, twice),
        "spread_next",
        WORK,
    )
    returned = exchange(picked.reshape(TX, CAP, 128)).reshape(SLOTS, 128)
    parts, adjoint, sums = run_middle(
        owner_counts, tile, obs_weight, returned, adjoint, sums, obs_operator
    )
    parts = exchange(parts)
    field, message = tile_call(
        last_gather_kernel,
        (WIDENED, jax.ShapeDtypeStruct((TY, LAST, 128), F32)),
        (where,),
        (parts, sigma_ext, listed),
        "gather_last",
    )
    message = lax.all_to_all(message, "ty", split_axis=0, concat_axis=0, tiled=True)
    control_field, residual = tile_call(
        spread_last_kernel,
        (TILE, TILE),
        (where, step_counts),
        (field, message, along, across, once, image),
        "spread_last",
        WORK,
    )
    return control_field, residual


def solution(mesh):
    placed = (
        P(("tx", "ty"), None),
        P(("tx", "ty"), None),
        P(("tx", "ty"), None, None),
        P(("tx", "ty"), None),
        P(("tx", "ty")),
        P(("tx", "ty")),
        P(None, "tx", "ty"),
        P(None, "tx", "ty"),
        P(None, "tx", "ty"),
        P(),
    )
    return jax.shard_map(
        body,
        mesh=mesh,
        in_specs=placed,
        out_specs=(P(None, "tx", "ty"), P(None, "tx", "ty")),
        check_vma=False,
    )
```

time: 1310 us -> 179 us (0.14)
  starting transfers between devices: 639 us -> 20.8 us
  waiting for transfers between devices: 292 us -> 15 us
  blocking collectives: 254 us -> 64.9 us
  Pallas kernels: 0 us -> 74.9 us
  matrix products: 58.9 us -> 0 us
  other arithmetic: 26.5 us -> 0.11 us
  local copies, waits for them, and re-layouts: 17 us -> 0.63 us
    ppermute x204 -> x6, starting transfers between devices: 605 us -> 12.4 us  [the longest x3 7.3 us: swap_neighbours(): lax.ppermute(for_other, axis, others)]
    ppermute x204 -> x6, waiting for transfers between devices: 272 us -> 15 us  [the longest x3 15 us: swap_neighbours(): lax.ppermute(for_other, axis, others)]
    psum x3 -> x0, blocking collectives: 212 us -> none  [the longest x2 138 us: squares(): return lax.psum(jnp.sum(residual * residual), ('tx', 'ty'))]
    pallas_call x0 -> x9, Pallas kernels: none -> 74.9 us  [the longest x2 37.4 us: run_middle(): pl.pallas_call(middle_kernel, grid=(OWN // GROUP,), in_specs=[SCALARS, wh...]
    dot_general x5 -> x0, matrix products: 58.9 us -> none  [the longest x2 30.8 us: body(): jnp.einsum('bij,bj->bi', obs_operator, returned, precision=lax.Precision....]
    all_to_all x4 -> x1, starting transfers between devices: 34.3 us -> 8.43 us  [exchange(): return lax.all_to_all(parts, 'tx', split_axis=0, concat_axis=0, tiled=True)]
    all_to_all x2 -> x5, blocking collectives: 41.9 us -> 64.9 us  [the longest x4 47.3 us: exchange(): return lax.all_to_all(parts, 'tx', split_axis=0, concat_axis=0, tiled=True)]
    all_to_all x4 -> x1, waiting for transfers between devices: 19.5 us -> 0.01 us  [exchange(): return lax.all_to_all(parts, 'tx', split_axis=0, concat_axis=0, tiled=True)]
  transfers between devices with their start and end apart: 208 -> 7, of which waited for: 156 -> 3; matrix products, arithmetic and copies ran while one was open for 1% -> 0% of each run, Pallas kernels for 0% -> 0%
where the time goes in v1:
time: 179 us; the launch traced here: 178 us
  Pallas kernels  74.9 us (42%)
  blocking collectives  64.9 us (36%)
  starting transfers between devices  20.8 us (12%)
  waiting for transfers between devices  15 us (8%)
    all_to_all x4, blocking collectives, exchange(): return lax.all_to_all(parts, 'tx', split_axis=0, concat_axis=0, tiled=True)  47.3 us
    pallas_call x2, Pallas kernels, run_middle(): pl.pallas_call(middle_kernel, grid=(OWN // GROUP,), in_specs=[SCALARS, wh...  37.4 us
    pallas_call x6, Pallas kernels, tile_call(): pl.pallas_call(kernel, in_specs=[SCALARS] * len(scalars) + [vmem] * len(a...  28.7 us
    all_to_all x1, blocking collectives, body(): lax.all_to_all(message, 'ty', split_axis=0, concat_axis=0, tiled=True)  17.6 us
    ppermute x3, waiting for transfers between devices, swap_neighbours(): lax.ppermute(for_other, axis, others)  15 us
    pallas_call x1, Pallas kernels, run_first(): pl.pallas_call(first_kernel, grid=(OWN // GROUP,), in_specs=[SCALARS, who...  8.8 us
    all_to_all x1, starting transfers between devices, exchange(): return lax.all_to_all(parts, 'tx', split_axis=0, concat_axis=0, tiled=True)  8.43 us
    ppermute x3, starting transfers between devices, swap_neighbours(): lax.ppermute(for_other, axis, others)  7.3 us
  transfers between devices with their start and end apart: 7, of which 3 were waited for; matrix products, arithmetic and copies ran while one was open for 0% of the time, Pallas kernels for 0%

profile of v1, /device:TPU:1, one launch (start us, length us, event | category | flops | bytes accessed | tf_op | source)
XLA Modules:
  0.0 177.9 jit_solution(8218401735802211236)
XLA Ops:
  1.4 8.8 %first_adjoint.1 = (f32[16,80,128]{2,1,0:T(8,128)}, f32[128,128]{1,0:T(8,128)}) custom-call(s32[1]{0:T(128)S(6)} %copy.12.count_ref, s32[1,128]{1,0:T(1,128)} %bitcast.20, s32[1,128]{1,0:T(1,128)} %bitcast.23, f32[128,128]{1,0:T(8,128)} %innovation_ref.1, f32[128,128]{1,0:T(8,128)} %weight_ref.5, f32[128,128,128]{2,1,0:T(8,128)} %operator_ref.5), custom_call_target="tpu_custom_call" | custom-call | flops 8388608 | bytes 9437184 | tf_op jit(solution)/shard_map/first_adjoint/pallas_call | solution.py:186
  10.2 8.4 %all-to-all-start = ((f32[16,80,128]{2,1,0:T(8,128)}), f32[16,80,128]{2,1,0:T(8,128)S(1)}, u32[]{:S(2)}, u32[]{:S(2)}) async-start(f32[16,80,128]{2,1,0:T(8,128)} %get-tuple-element.26), calls=%async_computation | async-start | bytes 1310720 | tf_op jit(solution)/shard_map/all_to_all | solution.py:551
  18.7 4.8 %collective-permute-start.1 = (f32[2,4,24,128]{3,2,1,0:T(8,128)S(1)}, f32[2,4,24,128]{3,2,1,0:T(8,128)S(1)}, u32[]{:S(2)}, u32[]{:S(2)}) collective-permute-start(f32[2,4,24,128]{3,2,1,0:T(8,128)S(1)} %get-tuple-element.50), channel_id=1, source_target_pairs={{0,120},{8,16},{16,8},{24,32},{32,24},{40,48},{48,40},{56,64},{64,... | collective-permute-start | bytes 294920 | tf_op jit(solution)/shard_map/ppermute | solution.py:547
  23.6 9.4 %collective-permute-done.1.far_ref = f32[2,4,24,128]{3,2,1,0:T(8,128)S(1)} collective-permute-done((f32[2,4,24,128]{3,2,1,0:T(8,128)S(1)}, f32[2,4,24,128]{3,2,1,0:T(8,128)S(1)}, u32[]{:S(2)}, u32[]{:S(2)}) %collective-permute-start.1) | collective-permute-done | bytes 98336 | tf_op jit(solution)/shard_map/ppermute | solution.py:547
  33.0 1.8 %open_tile.1 = (f32[448,128]{1,0:T(8,128)S(1)}, f32[448,128]{1,0:T(8,128)S(1)}, f32[448,128]{1,0:T(8,128)S(1)}, f32[2,112,128]{2,1,0:T(8,128)S(1)}, f32[2,112,128]{2,1,0:T(8,128)S(1)}, /*index=5*/f32[16,128]{1,0:T(8,128)S(1)}) custom-call(s32[2]{0:T(128)S(1)} %pad_add_fusion.where_ref, f32[16,80,128]{2,1,0:T(8,128)S(1)} %all-to-all-done.parts_ref, ...), custom_call_target="tpu_custom_call" | custom-call | tf_op jit(solution)/shard_map/open_tile/pallas_call | solution.py:532
  34.8 1.4 collective-permute-start.2
  36.2 1.3 collective-permute-start.3
  37.4 3.2 %collective-permute-done.3.far_ref = f32[2,112,128]{2,1,0:T(8,128)S(1)} collective-permute-done((f32[2,112,128]{2,1,0:T(8,128)S(1)}, f32[2,112,128]{2,1,0:T(8,128)S(1)}, u32[]{:S(2)}, u32[]{:S(2)}) %collective-permute-start.3) | collective-permute-done | bytes 114720 | tf_op jit(solution)/shard_map/ppermute | solution.py:547
  40.7 9.3 %spread_first.1 = (f32[384,128]{1,0:T(8,128)S(1)}, f32[4,64,128]{2,1,0:T(8,128)S(1)}, f32[4,64,128]{2,1,0:T(8,128)S(1)}, f32[896,128]{1,0:T(8,128)S(1)}, f32[896,128]{1,0:T(8,128)S(1)}) custom-call(s32[2]{0:T(128)S(1)} %pad_add_fusion.where_ref, s32[4]{0:T(128)S(1)} %copy-done.3, f32[448,128]{1,0:T(8,128)S(1)} %get-tuple-element.27.field_ref, ...), custom_call_target="tpu_custom_call" | custom-call | tf_op jit(solution)/shard_map/spread_first/pallas_call | solution.py:532
  50.0 10.2 %all_to_all.30 = f32[16,24,128]{2,1,0:T(8,128)} all-to-all(f32[16,24,128]{2,1,0:T(8,128)S(1)} %bitcast.16), channel_id=1, replica_groups=mesh['tx'=16,'ty'=8] {'tx'}, dimensions={0} | all-to-all | bytes 393216 | tf_op jit(solution)/shard_map/all_to_all | solution.py:551
  60.2 0.6 broadcast_in_dim.3.sums_in_ref
  60.8 18.7 %observe.2 = (f32[16,80,128]{2,1,0:T(8,128)}, f32[128,128]{1,0:T(8,128)}, f32[8,128]{1,0:T(8,128)}) custom-call(s32[1]{0:T(128)S(6)} %copy.12.count_ref, s32[1,128]{1,0:T(1,128)} %bitcast.21, f32[128,128]{1,0:T(8,128)} %weight_ref.5, f32[384,128]{1,0:T(8,128)} %bitcast.18, f32[128,128]{1,0:T(8,128)} %get-tuple-element.33.earlier_ref, ...), custom_call_target="tpu_custom_call" | custom-call | flops 16777216 | bytes 10485760 | tf_op jit(solution)/shard_map/observe/pallas_call | solution.py:201
  79.5 13.8 %all_to_all.31.parts_ref = f32[16,80,128]{2,1,0:T(8,128)S(1)} all-to-all(f32[16,80,128]{2,1,0:T(8,128)} %get-tuple-element.34), channel_id=1, replica_groups=mesh['tx'=16,'ty'=8] {'tx'}, dimensions={0} | all-to-all | bytes 1310720 | tf_op jit(solution)/shard_map/all_to_all | solution.py:551
  93.3 1.8 gather_tile.1
  95.0 3.7 %collective-permute-start.4 = (f32[1,112,128]{2,1,0:T(8,128)S(1)}, f32[1,112,128]{2,1,0:T(8,128)S(1)}, u32[]{:S(2)}, u32[]{:S(2)}) collective-permute-start(f32[1,112,128]{2,1,0:T(8,128)S(1)} %get-tuple-element.37), channel_id=1, source_target_pairs={{0,1},{1,0},{2,3},{3,2},{4,5},{5,4},{6,7},{7,6},{8,9},{9,8},{10,11... | collective-permute-start | bytes 172040 | tf_op jit(solution)/shard_map/ppermute | solution.py:547
  98.8 1.3 collective-permute-start.5
  100.1 2.3 %collective-permute-done.5.far_ref = f32[1,112,128]{2,1,0:T(8,128)S(1)} collective-permute-done((f32[1,112,128]{2,1,0:T(8,128)S(1)}, f32[1,112,128]{2,1,0:T(8,128)S(1)}, u32[]{:S(2)}, u32[]{:S(2)}) %collective-permute-start.5) | collective-permute-done | bytes 57376 | tf_op jit(solution)/shard_map/ppermute | solution.py:547
  102.4 8.8 %spread_next.1 = (f32[384,128]{1,0:T(8,128)S(1)}, f32[4,64,128]{2,1,0:T(8,128)S(1)}) custom-call(s32[2]{0:T(128)S(1)} %pad_add_fusion.where_ref, s32[4]{0:T(128)S(1)} %copy-done.3, f32[448,128]{1,0:T(8,128)S(1)} %get-tuple-element.36.field_ref, f32[1,112,128]{2,1,0:T(8,128)S(1)} %collective-permute-done.4.near_ref, ...), custom_call_target="tpu_custom_call" | custom-call | tf_op jit(solution)/shard_map/spread_next/pallas_call | solution.py:532
  111.2 10.2 %all_to_all.32 = f32[16,24,128]{2,1,0:T(8,128)} all-to-all(f32[16,24,128]{2,1,0:T(8,128)S(1)} %bitcast.17), channel_id=1, replica_groups=mesh['tx'=16,'ty'=8] {'tx'}, dimensions={0} | all-to-all | bytes 393216 | tf_op jit(solution)/shard_map/all_to_all | solution.py:551
  121.4 18.7 %observe.3 = (f32[16,80,128]{2,1,0:T(8,128)}, f32[128,128]{1,0:T(8,128)}, f32[8,128]{1,0:T(8,128)}) custom-call(s32[1]{0:T(128)S(6)} %copy.12.count_ref, s32[1,128]{1,0:T(1,128)} %bitcast.22, f32[128,128]{1,0:T(8,128)} %weight_ref.5, f32[384,128]{1,0:T(8,128)} %bitcast.19, f32[128,128]{1,0:T(8,128)} %get-tuple-element.44.earlier_ref, ...), custom_call_target="tpu_custom_call" | custom-call | flops 16777216 | bytes 10485760 | tf_op jit(solution)/shard_map/observe/pallas_call | solution.py:201
  140.2 13.1 %all_to_all.33.parts_ref = f32[16,80,128]{2,1,0:T(8,128)S(1)} all-to-all(f32[16,80,128]{2,1,0:T(8,128)} %get-tuple-element.46), channel_id=1, replica_groups=mesh['tx'=16,'ty'=8] {'tx'}, dimensions={0} | all-to-all | bytes 1310720 | tf_op jit(solution)/shard_map/all_to_all | solution.py:551
  153.3 1.8 gather_last.1
  155.1 17.6 %all_to_all.34.message_ref = f32[8,56,128]{2,1,0:T(8,128)S(1)} all-to-all(f32[8,56,128]{2,1,0:T(8,128)S(1)} %get-tuple-element.48), channel_id=1, replica_groups=mesh['tx'=16,'ty'=8] {'ty'}, dimensions={0} | all-to-all | bytes 458752 | tf_op jit(solution)/shard_map/all_to_all | solution.py:628
  172.7 5.2 %spread_last.1 = (f32[4,64,128]{2,1,0:T(8,128)}, f32[4,64,128]{2,1,0:T(8,128)}) custom-call(s32[2]{0:T(128)S(1)} %pad_add_fusion.where_ref, s32[4]{0:T(128)S(1)} %copy-done.3, f32[448,128]{1,0:T(8,128)S(1)} %get-tuple-element.47.field_ref, f32[8,56,128]{2,1,0:T(8,128)S(1)} %all_to_all.34.message_ref, f32[896,128]{1,0:T(8,128)S(1)} %get-tuple-element.39.along_ref, ...), custom_call_target="tpu_custom_call" | custom-call | tf_op jit(solution)/shard_map/spread_last/pallas_call | solution.py:532
  (17 shorter events, 0.2 us)
Async XLA Ops:
  0.6 18.0 %copy-start.2 = (f32[4,64,128]{2,1,0:T(8,128)S(1)}, f32[4,64,128]{2,1,0:T(8,128)}, u32[]{:S(2)}) copy-start(f32[4,64,128]{2,1,0:T(8,128)} %diffusivity_ref.1) | copy-start | bytes 393220
  0.6 18.0 %copy-start.1 = (s32[4,64,128]{2,1,0:T(8,128)S(1)}, s32[4,64,128]{2,1,0:T(8,128)}, u32[]{:S(2)}) copy-start(s32[4,64,128]{2,1,0:T(8,128)} %mask_ref.1) | copy-start | bytes 393220
  0.7 18.0 %copy-start = (f32[4,64,128]{2,1,0:T(8,128)S(1)}, f32[4,64,128]{2,1,0:T(8,128)}, u32[]{:S(2)}) copy-start(f32[4,64,128]{2,1,0:T(8,128)} %sigma_ref.5) | copy-start | bytes 393220
  0.7 40.0 %copy-start.3 = (s32[4]{0:T(128)S(1)}, s32[4]{0:T(128)}, u32[]{:S(2)}) copy-start(s32[4]{0:T(128)} %count_ref.8) | copy-start | bytes 52
  10.2 22.8 %all-to-all-start = ((f32[16,80,128]{2,1,0:T(8,128)}), f32[16,80,128]{2,1,0:T(8,128)S(1)}, u32[]{:S(2)}, u32[]{:S(2)}) async-start(f32[16,80,128]{2,1,0:T(8,128)} %get-tuple-element.26), calls=%async_computation | async-start | bytes 1310720 | tf_op jit(solution)/shard_map/all_to_all | solution.py:551
  18.7 14.3 %collective-permute-start.1 = (f32[2,4,24,128]{3,2,1,0:T(8,128)S(1)}, f32[2,4,24,128]{3,2,1,0:T(8,128)S(1)}, u32[]{:S(2)}, u32[]{:S(2)}) collective-permute-start(f32[2,4,24,128]{3,2,1,0:T(8,128)S(1)} %get-tuple-element.50), channel_id=1, source_target_pairs={{0,120},{8,16},{16,8},{24,32},{32,24},{40,48},{48,40},{56,64},{64,... | collective-permute-start | bytes 294920 | tf_op jit(solution)/shard_map/ppermute | solution.py:547
  23.5 9.5 %collective-permute-start = (f32[2,4,24,128]{3,2,1,0:T(8,128)S(1)}, f32[2,4,24,128]{3,2,1,0:T(8,128)S(1)}, u32[]{:S(2)}, u32[]{:S(2)}) collective-permute-start(f32[2,4,24,128]{3,2,1,0:T(8,128)S(1)} %get-tuple-element.51), channel_id=1, source_target_pairs={{0,8},{8,0},{16,24},{24,16},{32,40},{40,32},{48,56},{56,48},{64,72... | collective-permute-start | bytes 294920 | tf_op jit(solution)/shard_map/ppermute | solution.py:547
  34.8 2.6 %collective-permute-start.2 = (f32[2,112,128]{2,1,0:T(8,128)S(1)}, f32[2,112,128]{2,1,0:T(8,128)S(1)}, u32[]{:S(2)}, u32[]{:S(2)}) collective-permute-start(f32[2,112,128]{2,1,0:T(8,128)S(1)} %get-tuple-element.29), channel_id=1, source_target_pairs={{0,1},{1,0},{2,3},{3,2},{4,5},{5,4},{6,7},{7,6},{8,9},{9,8},{10,11... | collective-permute-start | bytes 344072 | tf_op jit(solution)/shard_map/ppermute | solution.py:547
  36.2 4.5 %collective-permute-start.3 = (f32[2,112,128]{2,1,0:T(8,128)S(1)}, f32[2,112,128]{2,1,0:T(8,128)S(1)}, u32[]{:S(2)}, u32[]{:S(2)}) collective-permute-start(f32[2,112,128]{2,1,0:T(8,128)S(1)} %get-tuple-element.30), channel_id=1, source_target_pairs={{0,7},{1,2},{2,1},{3,4},{4,3},{5,6},{6,5},{7,0},{8,15},{9,10},{10,... | collective-permute-start | bytes 344072 | tf_op jit(solution)/shard_map/ppermute | solution.py:547
  95.0 5.0 %collective-permute-start.4 = (f32[1,112,128]{2,1,0:T(8,128)S(1)}, f32[1,112,128]{2,1,0:T(8,128)S(1)}, u32[]{:S(2)}, u32[]{:S(2)}) collective-permute-start(f32[1,112,128]{2,1,0:T(8,128)S(1)} %get-tuple-element.37), channel_id=1, source_target_pairs={{0,1},{1,0},{2,3},{3,2},{4,5},{5,4},{6,7},{7,6},{8,9},{9,8},{10,11... | collective-permute-start | bytes 172040 | tf_op jit(solution)/shard_map/ppermute | solution.py:547
  98.8 3.6 %collective-permute-start.5 = (f32[1,112,128]{2,1,0:T(8,128)S(1)}, f32[1,112,128]{2,1,0:T(8,128)S(1)}, u32[]{:S(2)}, u32[]{:S(2)}) collective-permute-start(f32[1,112,128]{2,1,0:T(8,128)S(1)} %get-tuple-element.38), channel_id=1, source_target_pairs={{0,7},{1,2},{2,1},{3,4},{4,3},{5,6},{6,5},{7,0},{8,15},{9,10},{10,... | collective-permute-start | bytes 172040 | tf_op jit(solution)/shard_map/ppermute | solution.py:547

commit v2 on v1

--- a/solution.py
+++ b/solution.py
@@ -13,6 +13,7 @@
 CY = 128
 NSTEP = 10
 MIN_STEPS = 5
+UNROLL = 5
 HALO = 2 * NSTEP
 SIDE = 24
 EXT = CX + 2 * SIDE
@@ -25,6 +26,7 @@
 LISTED = 3 * CAP
 PART = 80
 GROUP = 16
+GROUPS = OWN // GROUP
 WIDE = 16
 STRIP = 48
 LAST = STRIP + 8
@@ -106,77 +108,123 @@
     return jnp.where(iota((OWN, OWN), 1) < count_ref[0], weighted.T, 0.0)
 
 
-def group_columns(columns_ref, step):
-    turned = pltpu.roll(columns_ref[...], lax.rem(OWN - step * GROUP, OWN), 1)
-    return turned[:, :GROUP]
+def group(number):
+    return pl.ds(pl.multiple_of(number * GROUP, GROUP), GROUP)
+
+
+def load_blocks(operator_ref, blocks_ref, arrived):
+    return lambda number: pltpu.make_async_copy(
+        operator_ref.at[group(number)], blocks_ref.at[group(number)], arrived.at[number]
+    )
+
+
+def start_all(copy_of):
+    for number in range(GROUPS):
+        copy_of(number).start()
 
 
 def first_kernel(
     count_ref, tile_ref, column_ref, innovation_ref, weight_ref, operator_ref,
-    parts_ref, adjoint_ref, columns_ref,
+    parts_ref, adjoint_ref, blocks_ref, repeated_ref, arrived,
 ):
-    step = pl.program_id(0)
-
-    @pl.when(step == 0)
-    def _():
-        columns_ref[...] = live_columns(count_ref, weight_ref[...] * innovation_ref[...])
-
-    columns = group_columns(columns_ref, step)
-    rows = []
-    for k in range(GROUP):
-        rows.append(jnp.sum(operator_ref[k] * columns[:, k : k + 1], axis=0, keepdims=True))
-    adjoint_ref[pl.ds(pl.multiple_of(step * GROUP, GROUP), GROUP), :] = jnp.concatenate(rows, axis=0)
-
-    @pl.when(step == pl.num_programs(0) - 1)
-    def _():
-        tables = slot_tables(tile_ref)
-        write_parts(parts_ref, to_slots(tables, adjoint_ref[...]))
-        listed = listed_columns(tables, column_ref)
-        for tile in range(TX):
-            parts_ref[tile, pl.ds(LISTED, 8), :] = jnp.broadcast_to(listed[tile : tile + 1], (8, 128))
+    copy_of = load_blocks(operator_ref, blocks_ref, arrived)
+    start_all(copy_of)
+    tables = slot_tables(tile_ref)
+    listed = listed_columns(tables, column_ref)
+    for tile in range(TX):
+        parts_ref[tile, pl.ds(LISTED, 8), :] = jnp.broadcast_to(listed[tile : tile + 1], (8, 128))
+    eye = as_onehot(iota((OWN, OWN), 0) == iota((OWN, OWN), 1))
+    ones = jnp.ones((2 * OWN, 128), BF16)
+
+    def one_group(number, carry):
+        here = group(number)
+        live = iota((GROUP, OWN), 0) + number * GROUP < count_ref[0]
+        weighted = jnp.where(live, weight_ref[here, :] * innovation_ref[here, :], 0.0)
+        high, middle, _ = thirds(weighted)
+        diagonals = [
+            jnp.concatenate([eye * high[k : k + 1], eye * middle[k : k + 1]], axis=1)
+            for k in range(GROUP)
+        ]
+        repeated_ref[...] = jnp.dot(
+            jnp.concatenate(diagonals, axis=0), ones, preferred_element_type=F32
+        )
+        copy_of(number).wait()
+        rows = []
+        for k in range(GROUP):
+            column = repeated_ref[pl.ds(k * OWN, OWN), :]
+            block = blocks_ref[number * GROUP + k]
+            rows.append(jnp.sum(block * column, axis=0, keepdims=True))
+        adjoint_ref[here, :] = jnp.concatenate(rows, axis=0)
+        return carry
+
+    lax.fori_loop(0, GROUPS, one_group, 0)
+    write_parts(parts_ref, to_slots(tables, adjoint_ref[...]))
+
+
+def turn_kernel(operator_ref, turned_ref, done_ref, blocks_ref, lanes_ref, arrived, left):
+    done_ref[...] = jnp.zeros((8, 128), F32)
+
+    def copy_of(number):
+        return pltpu.make_async_copy(
+            operator_ref.at[:, group(number), :], blocks_ref.at[number], arrived.at[number]
+        )
+
+    def back(number):
+        return pltpu.make_async_copy(
+            lanes_ref.at[group(number)], turned_ref.at[group(number)], left.at[number]
+        )
+
+    start_all(copy_of)
+
+    def one_group(number, carry):
+        copy_of(number).wait()
+        for k in range(GROUP):
+            lanes_ref[number * GROUP + k] = blocks_ref[number, :, k, :].T
+        back(number).start()
+        return carry
+
+    lax.fori_loop(0, GROUPS, one_group, 0)
+    for number in range(GROUPS):
+        back(number).wait()
 
 
 def middle_kernel(
-    count_ref, tile_ref, weight_ref, returned_ref, earlier_ref, sums_in_ref, operator_ref,
-    parts_ref, adjoint_ref, sums_ref, columns_ref, segments_ref,
+    count_ref, tile_ref, weight_ref, returned_ref, earlier_ref, turned_ref, *refs
 ):
-    step = pl.program_id(0)
-
-    @pl.when(step == 0)
-    def _():
-        columns_ref[...] = live_columns(count_ref, weight_ref[...])
-        segments_ref[...] = from_slots(slot_tables(tile_ref), returned_ref[...])
-
-    columns = group_columns(columns_ref, step)
-    here = pl.ds(pl.multiple_of(step * GROUP, GROUP), GROUP)
-    segments = segments_ref[here, :]
-    rows = []
-    for k in range(GROUP):
-        block = operator_ref[k]
-        observed = jnp.sum(block * segments[k : k + 1], axis=1, keepdims=True)
-        rows.append(jnp.sum(block * (observed * columns[:, k : k + 1]), axis=0, keepdims=True))
-    adjoint_ref[here, :] = jnp.concatenate(rows, axis=0)
-
-    @pl.when(step == pl.num_programs(0) - 1)
-    def _():
-        adjoint = adjoint_ref[...]
-        segments = segments_ref[...]
-        write_parts(parts_ref, to_slots(slot_tables(tile_ref), adjoint))
-        known = jnp.sum(earlier_ref[...] * segments, axis=0, keepdims=True)
-        new = jnp.sum(adjoint * segments, axis=0, keepdims=True)
-        sums = jnp.concatenate([sums_in_ref[2:4], known, new, jnp.zeros((4, 128), F32)], axis=0)
-        sums_ref[...] = sums
-        for tile in range(TX):
-            parts_ref[tile, pl.ds(LISTED, 8), :] = sums
-        adjoint_ref[...] = adjoint + earlier_ref[...]
-
-
-def whole(shape):
-    return pl.BlockSpec(shape, lambda i: (0,) * len(shape))
-
-
+    *sums_in_ref, parts_ref, adjoint_ref, sums_ref, weight_scr = refs
+    tables = slot_tables(tile_ref)
+    weight_scr[...] = live_columns(count_ref, weight_ref[...])
+    own_segments = from_slots(tables, returned_ref[...])
+    segments = own_segments.T
+
+    def one_group(number, total):
+        weight = weight_scr[group(number), :]
+        for k in range(GROUP):
+            block = turned_ref[number * GROUP + k]
+            observed = jnp.sum(block * segments, axis=0, keepdims=True)
+            total = total + block * (observed * weight[k : k + 1])
+        return total
+
+    total = lax.fori_loop(0, GROUPS, one_group, jnp.zeros((OWN, OWN), F32))
+    adjoint = total.T
+    write_parts(parts_ref, to_slots(tables, adjoint))
+    known = jnp.sum(earlier_ref[...] * own_segments, axis=0, keepdims=True)
+    new = jnp.sum(adjoint * own_segments, axis=0, keepdims=True)
+    before = sums_in_ref[0][2:4] if sums_in_ref else jnp.zeros((2, 128), F32)
+    sums = jnp.concatenate([before, known, new, jnp.zeros((4, 128), F32)], axis=0)
+    sums_ref[...] = sums
+    for tile in range(TX):
+        parts_ref[tile, pl.ds(LISTED, 8), :] = sums
+    adjoint_ref[...] = adjoint + earlier_ref[...]
+
+
+VMEM_FIRST = 57 << 20
+VMEM_TURN = 57 << 20
+VMEM_OBSERVE = 16 << 20
 SCALARS = pl.BlockSpec(memory_space=pltpu.SMEM)
-OPERATORS = pl.BlockSpec((GROUP, 128, 128), lambda i: (i, 0, 0))
+HERE = pl.BlockSpec(memory_space=pltpu.VMEM)
+THERE = pl.BlockSpec(memory_space=pltpu.HBM)
+CUBE = (OWN, 128, 128)
 PARTS = jax.ShapeDtypeStruct((TX, PART, 128), F32)
 SQUARE = jax.ShapeDtypeStruct((OWN, 128), F32)
 SUMS = jax.ShapeDtypeStruct((8, 128), F32)
@@ -185,32 +233,49 @@
 def run_first(counts, tile, column, innovation, weight, operator):
     return pl.pallas_call(
         first_kernel,
-        grid=(OWN // GROUP,),
-        in_specs=[
-            SCALARS, whole((1, OWN)), whole((1, OWN)), whole((OWN, 128)), whole((OWN, 128)), OPERATORS,
+        in_specs=[SCALARS, HERE, HERE, HERE, HERE, THERE],
+        out_specs=[HERE, HERE],
+        out_shape=[PARTS, SQUARE],
+        scratch_shapes=[
+            pltpu.VMEM(CUBE, F32),
+            pltpu.VMEM((GROUP * OWN, 128), F32),
+            pltpu.SemaphoreType.DMA((GROUPS,)),
         ],
-        out_specs=[whole((TX, PART, 128)), whole((OWN, 128))],
-        out_shape=[PARTS, SQUARE],
-        scratch_shapes=[pltpu.VMEM((OWN, OWN), F32)],
+        compiler_params=pltpu.CompilerParams(vmem_limit_bytes=VMEM_FIRST),
         cost_estimate=pl.CostEstimate(flops=4 * 128**3, bytes_accessed=9 << 20, transcendentals=0),
         name="first_adjoint",
     )(counts, tile, column, innovation, weight, operator)
 
 
-def run_middle(counts, tile, weight, returned, earlier, sums, operator):
+def run_turn(operator):
+    return pl.pallas_call(
+        turn_kernel,
+        in_specs=[THERE],
+        out_specs=[THERE, HERE],
+        out_shape=[jax.ShapeDtypeStruct(CUBE, F32), SUMS],
+        scratch_shapes=[
+            pltpu.VMEM((GROUPS, OWN, GROUP, 128), F32),
+            pltpu.VMEM(CUBE, F32),
+            pltpu.SemaphoreType.DMA((GROUPS,)),
+            pltpu.SemaphoreType.DMA((GROUPS,)),
+        ],
+        compiler_params=pltpu.CompilerParams(vmem_limit_bytes=VMEM_TURN),
+        cost_estimate=pl.CostEstimate(flops=0, bytes_accessed=16 << 20, transcendentals=0),
+        name="blocks_on_lanes",
+    )(operator)
+
+
+def run_middle(counts, tile, weight, returned, earlier, turned, *sums):
     return pl.pallas_call(
         middle_kernel,
-        grid=(OWN // GROUP,),
-        in_specs=[
-            SCALARS, whole((1, OWN)), whole((OWN, 128)), whole((SLOTS, 128)), whole((OWN, 128)),
-            whole((8, 128)), OPERATORS,
-        ],
-        out_specs=[whole((TX, PART, 128)), whole((OWN, 128)), whole((8, 128))],
+        in_specs=[SCALARS] + [HERE] * (5 + len(sums)),
+        out_specs=[HERE, HERE, HERE],
         out_shape=[PARTS, SQUARE, SUMS],
-        scratch_shapes=[pltpu.VMEM((OWN, OWN), F32), pltpu.VMEM((OWN, 128), F32)],
+        scratch_shapes=[pltpu.VMEM((OWN, OWN), F32)],
+        compiler_params=pltpu.CompilerParams(vmem_limit_bytes=VMEM_OBSERVE),
         cost_estimate=pl.CostEstimate(flops=8 * 128**3, bytes_accessed=10 << 20, transcendentals=0),
         name="observe",
-    )(counts, tile, weight, returned, earlier, sums, operator)
+    )(counts, tile, weight, returned, earlier, turned, *sums)
 
 
 def scatter(parts_ref, listed):
@@ -259,7 +324,7 @@
 
 
 def open_kernel(
-    where_ref, parts_ref, sigma_ref, mask_ref, diffusivity_ref, near_ref, far_ref,
+    where_ref, parts_ref, sigma_ref, mask_ref, diffusivity_ref, near_ref, far_ref, _,
     field_ref, sigma_ext_ref, kappa_ext_ref, pair_ref, other_ref, listed_ref,
 ):
     row_no = where_ref[0]
@@ -284,6 +349,10 @@
     field_ref[...] = field
     pair_ref[0], other_ref[0] = edges(field, even)
     pair_ref[1], other_ref[1] = edges(kappa_ext_ref[...], even)
+
+
+def bring_kernel(listed_ref, _, brought_ref):
+    brought_ref[...] = listed_ref[:8]
 
 
 def gather_kernel(where_ref, parts_ref, sigma_ext_ref, listed_ref, field_ref, pair_ref, other_ref):
@@ -370,8 +439,16 @@
             work_ref[here, :] = now + change
             now = after
 
-    lax.fori_loop(0, MIN_STEPS, lambda n, c: (one(n, False), c)[1], 0)
-    lax.fori_loop(MIN_STEPS, NSTEP, lambda n, c: (one(n, True), c)[1], 0)
+    def run(start, end, masked):
+        def body(index, carry):
+            for k in range(UNROLL):
+                one(start + index * UNROLL + k, masked)
+            return carry
+
+        lax.fori_loop(0, (end - start) // UNROLL, body, 0)
+
+    run(0, MIN_STEPS, False)
+    run(MIN_STEPS, NSTEP, True)
 
 
 def faces(work_ref, along_ref, across_ref):
@@ -424,7 +501,7 @@
 
 
 def spread_first_kernel(
-    where_ref, count_ref, field_ref, kappa_ext_ref, near_ref, far_ref, sigma_ref, listed_ref,
+    where_ref, count_ref, field_ref, kappa_ext_ref, near_ref, far_ref, sigma_ref, listed_ref, _,
     picked_ref, once_ref, twice_ref, along_ref, across_ref, work_ref,
 ):
     band = where_ref[1]
@@ -527,17 +604,16 @@
     return jax.ShapeDtypeStruct((number, EXT, 128), F32)
 
 
-def tile_call(kernel, out_shape, scalars, arrays, name, scratch=()):
-    vmem = pl.BlockSpec(memory_space=pltpu.VMEM)
+def tile_call(kernel, out_shape, scalars, arrays, name, scratch=(), after=()):
     return pl.pallas_call(
         kernel,
-        in_specs=[SCALARS] * len(scalars) + [vmem] * len(arrays),
-        out_specs=[vmem] * len(out_shape),
+        in_specs=[SCALARS] * len(scalars) + [HERE] * len(arrays) + [HERE] * len(after),
+        out_specs=[HERE] * len(out_shape),
         out_shape=list(out_shape),
         scratch_shapes=list(scratch),
-        compiler_params=pltpu.CompilerParams(vmem_limit_bytes=32 << 20),
+        compiler_params=pltpu.CompilerParams(vmem_limit_bytes=16 << 20),
         name=name,
-    )(*scalars, *arrays)
+    )(*scalars, *arrays, *after)
 
 
 def swap_neighbours(for_pair, for_other, axis):
@@ -574,6 +650,8 @@
     near_x, far_x = swap_neighbours(jnp.where(even, high, low), jnp.where(even, low, high), "tx")
 
     parts, adjoint = run_first(owner_counts, tile, column, innovation, obs_weight, obs_operator)
+    parts, near_x, far_x = lax.optimization_barrier((parts, near_x, far_x))
+    turned, done = run_turn(obs_operator)
     parts = exchange(parts)
     field, sigma_ext, kappa_ext, pair, other, listed = tile_call(
         open_kernel,
@@ -581,8 +659,10 @@
         (where,),
         (parts, background_std, sea_mask, diffusivity, near_x, far_x),
         "open_tile",
+        after=(done,),
     )
     near, far = swap_neighbours(pair, other, "ty")
+    brought = tile_call(bring_kernel, (SUMS,), (), (listed, turned), "bring_blocks")
     picked, once, twice, along, across = tile_call(
         spread_first_kernel,
         (PICKED, TILE, TILE, LAID, LAID),
@@ -590,12 +670,10 @@
         (field, kappa_ext, near, far, background_std, listed),
         "spread_first",
         WORK,
+        after=brought,
     )
     returned = exchange(picked.reshape(TX, CAP, 128)).reshape(SLOTS, 128)
-    sums = jnp.zeros((8, 128), F32)
-    parts, adjoint, sums = run_middle(
-        owner_counts, tile, obs_weight, returned, adjoint, sums, obs_operator
-    )
+    parts, adjoint, sums = run_middle(owner_counts, tile, obs_weight, returned, adjoint, turned)
     parts = exchange(parts)
     field, pair, other = tile_call(
         gather_kernel,
@@ -615,7 +693,7 @@
     )
     returned = exchange(picked.reshape(TX, CAP, 128)).reshape(SLOTS, 128)
     parts, adjoint, sums = run_middle(
-        owner_counts, tile, obs_weight, returned, adjoint, sums, obs_operator
+        owner_counts, tile, obs_weight, returned, adjoint, turned, sums
     )
     parts = exchange(parts)
     field, message = tile_call(

time: 179 us -> 139 us (0.78)
  Pallas kernels: 74.9 us -> 42.2 us
  waiting for transfers between devices: 15 us -> 5.26 us
  local copies, waits for them, and re-layouts: 0.63 us -> 4.96 us
    pallas_call x9 -> x11, Pallas kernels: 74.9 us -> 42.2 us  [the longest x7 21.5 us: tile_call(): pl.pallas_call(kernel, in_specs=[SCALARS] * len(scalars) + [HERE] * len(a...]
    ppermute x3, waiting for transfers between devices: 15 us -> 1.88 us  [swap_neighbours(): lax.ppermute(for_other, axis, others)]
    all_to_all x1, starting transfers between devices: 8.43 us -> 3.6 us  [exchange(): return lax.all_to_all(parts, 'tx', split_axis=0, concat_axis=0, tiled=True)]
    unnamed x8 -> x20, local copies, waits for them, and re-layouts: 0.02 us -> 4.11 us
    all_to_all x1, waiting for transfers between devices: 0.01 us -> 3.37 us  [exchange(): return lax.all_to_all(parts, 'tx', split_axis=0, concat_axis=0, tiled=True)]
    ppermute x3, starting transfers between devices: 7.3 us -> 9.86 us  [swap_neighbours(): lax.ppermute(for_other, axis, others)]
  transfers between devices with their start and end apart: 7 -> 7, of which waited for: 3 -> 2; matrix products, arithmetic and copies ran while one was open for 0% -> 0% of each run, Pallas kernels for 0% -> 11%
where the time goes in v2:
time: 139 us
  blocking collectives  63.4 us (46%)
  Pallas kernels  42.2 us (30%)
  starting transfers between devices  20.2 us (15%)
  waiting for transfers between devices  5.26 us (4%)
  local copies, waits for them, and re-layouts  4.96 us (4%)
  between operations  1.5 us (1%)
    all_to_all x4, blocking collectives, exchange(): return lax.all_to_all(parts, 'tx', split_axis=0, concat_axis=0, tiled=True)  46.2 us
    pallas_call x7, Pallas kernels, tile_call(): pl.pallas_call(kernel, in_specs=[SCALARS] * len(scalars) + [HERE] * len(a...  21.5 us
    all_to_all x1, blocking collectives, body(): lax.all_to_all(message, 'ty', split_axis=0, concat_axis=0, tiled=True)  17.1 us
    ppermute x3, starting transfers between devices, swap_neighbours(): lax.ppermute(for_other, axis, others)  9.86 us
    pallas_call x1, Pallas kernels, run_turn(): pl.pallas_call(turn_kernel, in_specs=[THERE], out_specs=[THERE, HERE], ou...  8.07 us
    pallas_call x1, Pallas kernels, run_first(): pl.pallas_call(first_kernel, in_specs=[SCALARS, HERE, HERE, HERE, HERE, T...  7.61 us
    ppermute x3, starting transfers between devices, swap_neighbours(): lax.ppermute(for_pair, axis, pairs)  6.75 us
    pallas_call x2, Pallas kernels, run_middle(): pl.pallas_call(middle_kernel, in_specs=[SCALARS] + [HERE] * (5 + len(sums...  5.09 us
  transfers between devices with their start and end apart: 7, of which 2 were waited for; matrix products, arithmetic and copies ran while one was open for 0% of the time, Pallas kernels for 11%

profile of v2, /device:TPU:1, one launch (start us, length us, event | category | flops | bytes accessed | tf_op | source)
XLA Modules:
  0.0 138.6 jit_solution(10061429987200788784)
XLA Ops:
  2.5 6.9 %collective-permute-start.1 = (f32[2,4,24,128]{3,2,1,0:T(8,128)S(1)}, f32[2,4,24,128]{3,2,1,0:T(8,128)S(1)}, u32[]{:S(2)}, u32[]{:S(2)}) collective-permute-start(f32[2,4,24,128]{3,2,1,0:T(8,128)S(1)} %get-tuple-element.60), channel_id=1, source_target_pairs={{0,120},{8,16},{16,8},{24,32},{32,24},{40,48},{48,40},{56,64},{64,... | collective-permute-start | bytes 294920 | tf_op jit(solution)/shard_map/ppermute | solution.py:623
  10.1 7.6 %first_adjoint.1 = (f32[16,80,128]{2,1,0:T(8,128)}, f32[128,128]{1,0:T(8,128)}) custom-call(s32[1]{0:T(128)S(6)} %copy.12.count_ref, s32[1,128]{1,0:T(1,128)} %bitcast.20, s32[1,128]{1,0:T(1,128)} %bitcast.23, f32[128,128]{1,0:T(8,128)} %innovation_ref.1, f32[128,128]{1,0:T(8,128)} %weight_ref.5, f32[128,128,128]{2,1,0:T(8,128)} %operator_ref.3), custom_call_target="tpu_custom_call" | custom-call | flops 8388608 | bytes 9437184 | tf_op jit(solution)/shard_map/first_adjoint/pallas_call | solution.py:234
  17.7 3.6 %all-to-all-start = ((f32[16,80,128]{2,1,0:T(8,128)}), f32[16,80,128]{2,1,0:T(8,128)S(1)}, u32[]{:S(2)}, u32[]{:S(2)}) async-start(f32[16,80,128]{2,1,0:T(8,128)} %get-tuple-element.32), calls=%async_computation | async-start | bytes 1310720 | tf_op jit(solution)/shard_map/all_to_all | solution.py:627
  21.4 8.1 %blocks_on_lanes.1 = (f32[128,128,128]{2,1,0:T(8,128)}, f32[8,128]{1,0:T(8,128)}) custom-call(f32[128,128,128]{2,1,0:T(8,128)} %operator_ref.3), custom_call_target="tpu_custom_call" | custom-call | bytes 16777216 | tf_op jit(solution)/shard_map/blocks_on_lanes/pallas_call | solution.py:251
  29.5 3.4 %all-to-all-done.parts_ref = f32[16,80,128]{2,1,0:T(8,128)S(1)} async-done(((f32[16,80,128]{2,1,0:T(8,128)}), f32[16,80,128]{2,1,0:T(8,128)S(1)}, u32[]{:S(2)}, u32[]{:S(2)}) %all-to-all-start) | async-done | bytes 655392 | tf_op jit(solution)/shard_map/all_to_all | solution.py:627
  33.6 1.8 %open_tile.1 = (f32[448,128]{1,0:T(8,128)S(1)}, f32[448,128]{1,0:T(8,128)S(1)}, f32[448,128]{1,0:T(8,128)S(1)}, f32[2,112,128]{2,1,0:T(8,128)S(1)}, f32[2,112,128]{2,1,0:T(8,128)S(1)}, /*index=5*/f32[16,128]{1,0:T(8,128)S(1)}) custom-call(s32[2]{0:T(128)S(1)} %pad_add_fusion.where_ref, f32[16,80,128]{2,1,0:T(8,128)S(1)} %all-to-all-done.parts_ref, ...), custom_call_target="tpu_custom_call" | custom-call | tf_op jit(solution)/shard_map/open_tile/pallas_call | solution.py:608
  35.4 2.3 %collective-permute-start.2 = (f32[2,112,128]{2,1,0:T(8,128)S(1)}, f32[2,112,128]{2,1,0:T(8,128)S(1)}, u32[]{:S(2)}, u32[]{:S(2)}) collective-permute-start(f32[2,112,128]{2,1,0:T(8,128)S(1)} %get-tuple-element.38), channel_id=1, source_target_pairs={{0,1},{1,0},{2,3},{3,2},{4,5},{5,4},{6,7},{7,6},{8,9},{9,8},{10,11... | collective-permute-start | bytes 344072 | tf_op jit(solution)/shard_map/ppermute | solution.py:623
  37.7 1.3 collective-permute-start.3
  39.0 3.4 %copy-done = f32[128,128,128]{2,1,0:T(8,128)S(1)} copy-done((f32[128,128,128]{2,1,0:T(8,128)S(1)}, f32[128,128,128]{2,1,0:T(8,128)}, u32[]{:S(2)}) %copy-start) | copy-done | bytes 8388632
  42.4 6.5 %spread_first.1 = (f32[384,128]{1,0:T(8,128)S(1)}, f32[4,64,128]{2,1,0:T(8,128)S(1)}, f32[4,64,128]{2,1,0:T(8,128)S(1)}, f32[896,128]{1,0:T(8,128)S(1)}, f32[896,128]{1,0:T(8,128)S(1)}) custom-call(s32[2]{0:T(128)S(1)} %pad_add_fusion.where_ref, s32[4]{0:T(128)S(1)} %copy-done.8, f32[448,128]{1,0:T(8,128)S(1)} %get-tuple-element.36.field_ref, ...), custom_call_target="tpu_custom_call" | custom-call | tf_op jit(solution)/shard_map/spread_first/pallas_call | solution.py:608
  48.9 10.1 %all_to_all.30 = f32[16,24,128]{2,1,0:T(8,128)S(1)} all-to-all(f32[16,24,128]{2,1,0:T(8,128)S(1)} %bitcast.18), channel_id=1, replica_groups=mesh['tx'=16,'ty'=8] {'tx'}, dimensions={0} | all-to-all | bytes 393216 | tf_op jit(solution)/shard_map/all_to_all | solution.py:627
  59.0 2.3 %observe.2 = (f32[16,80,128]{2,1,0:T(8,128)S(1)}, f32[128,128]{1,0:T(8,128)S(1)}, f32[8,128]{1,0:T(8,128)S(1)}) custom-call(s32[1]{0:T(128)S(6)} %copy.12.count_ref, s32[1,128]{1,0:T(1,128)S(1)} %bitcast.21, f32[128,128]{1,0:T(8,128)S(1)} %copy-done.3, f32[384,128]{1,0:T(8,128)S(1)} %bitcast.17, f32[128,128]{1,0:T(8,128)S(1)} %copy-done.6, ...), custom_call_target="tpu_custom_call" | custom-call | flops 16777216 | bytes 10485760 | tf_op jit(solution)/shard_map/observe/pallas_call | solution.py:269
  61.4 13.0 %all_to_all.31.parts_ref = f32[16,80,128]{2,1,0:T(8,128)S(1)} all-to-all(f32[16,80,128]{2,1,0:T(8,128)S(1)} %get-tuple-element.44), channel_id=1, replica_groups=mesh['tx'=16,'ty'=8] {'tx'}, dimensions={0} | all-to-all | bytes 1310720 | tf_op jit(solution)/shard_map/all_to_all | solution.py:627
  74.3 1.8 %gather_tile.1 = (f32[448,128]{1,0:T(8,128)S(1)}, f32[1,112,128]{2,1,0:T(8,128)S(1)}, f32[1,112,128]{2,1,0:T(8,128)S(1)}) custom-call(s32[2]{0:T(128)S(1)} %pad_add_fusion.where_ref, f32[16,80,128]{2,1,0:T(8,128)S(1)} %all_to_all.31.parts_ref, f32[448,128]{1,0:T(8,128)S(1)} %get-tuple-element.45.sigma_ext_ref, f32[16,128]{1,0:T(8,128)S(1)} %get-tuple-element.40.listed_ref), custom_call_target="tpu_custom_call" | custom-call | tf_op jit(solution)/shard_map/gather_tile/pallas_call | solution.py:608
  76.1 4.4 %collective-permute-start.4 = (f32[1,112,128]{2,1,0:T(8,128)S(1)}, f32[1,112,128]{2,1,0:T(8,128)S(1)}, u32[]{:S(2)}, u32[]{:S(2)}) collective-permute-start(f32[1,112,128]{2,1,0:T(8,128)S(1)} %get-tuple-element.47), channel_id=1, source_target_pairs={{0,1},{1,0},{2,3},{3,2},{4,5},{5,4},{6,7},{7,6},{8,9},{9,8},{10,11... | collective-permute-start | bytes 172040 | tf_op jit(solution)/shard_map/ppermute | solution.py:623
  80.6 1.7 %collective-permute-start.5 = (f32[1,112,128]{2,1,0:T(8,128)S(1)}, f32[1,112,128]{2,1,0:T(8,128)S(1)}, u32[]{:S(2)}, u32[]{:S(2)}) collective-permute-start(f32[1,112,128]{2,1,0:T(8,128)S(1)} %get-tuple-element.48), channel_id=1, source_target_pairs={{0,7},{1,2},{2,1},{3,4},{4,3},{5,6},{6,5},{7,0},{8,15},{9,10},{10,... | collective-permute-start | bytes 172040 | tf_op jit(solution)/shard_map/ppermute | solution.py:623
  82.3 1.9 %collective-permute-done.5.far_ref = f32[1,112,128]{2,1,0:T(8,128)S(1)} collective-permute-done((f32[1,112,128]{2,1,0:T(8,128)S(1)}, f32[1,112,128]{2,1,0:T(8,128)S(1)}, u32[]{:S(2)}, u32[]{:S(2)}) %collective-permute-start.5) | collective-permute-done | bytes 57376 | tf_op jit(solution)/shard_map/ppermute | solution.py:623
  84.2 5.8 %spread_next.1 = (f32[384,128]{1,0:T(8,128)S(1)}, f32[4,64,128]{2,1,0:T(8,128)S(1)}) custom-call(s32[2]{0:T(128)S(1)} %pad_add_fusion.where_ref, s32[4]{0:T(128)S(1)} %copy-done.8, f32[448,128]{1,0:T(8,128)S(1)} %get-tuple-element.46.field_ref, f32[1,112,128]{2,1,0:T(8,128)S(1)} %collective-permute-done.4.near_ref, ...), custom_call_target="tpu_custom_call" | custom-call | tf_op jit(solution)/shard_map/spread_next/pallas_call | solution.py:608
  90.0 10.1 %all_to_all.32 = f32[16,24,128]{2,1,0:T(8,128)S(1)} all-to-all(f32[16,24,128]{2,1,0:T(8,128)S(1)} %bitcast.19), channel_id=1, replica_groups=mesh['tx'=16,'ty'=8] {'tx'}, dimensions={0} | all-to-all | bytes 393216 | tf_op jit(solution)/shard_map/all_to_all | solution.py:627
  100.1 2.7 %observe.3 = (f32[16,80,128]{2,1,0:T(8,128)S(1)}, f32[128,128]{1,0:T(8,128)}, f32[8,128]{1,0:T(8,128)}) custom-call(s32[1]{0:T(128)S(6)} %copy.12.count_ref, s32[1,128]{1,0:T(1,128)S(1)} %bitcast.22, f32[128,128]{1,0:T(8,128)S(1)} %copy-done.3, f32[384,128]{1,0:T(8,128)S(1)} %bitcast.16, f32[128,128]{1,0:T(8,128)S(1)} %get-tuple-element.54.earlier_ref, ...), custom_call_target="tpu_custom_call" | custom-call | flops 16777216 | bytes 10485760 | tf_op jit(solution)/shard_map/observe/pallas_call | solution.py:269
  102.8 13.1 %all_to_all.33.parts_ref = f32[16,80,128]{2,1,0:T(8,128)S(1)} all-to-all(f32[16,80,128]{2,1,0:T(8,128)S(1)} %get-tuple-element.56), channel_id=1, replica_groups=mesh['tx'=16,'ty'=8] {'tx'}, dimensions={0} | all-to-all | bytes 1310720 | tf_op jit(solution)/shard_map/all_to_all | solution.py:627
  115.9 1.8 %gather_last.1 = (f32[448,128]{1,0:T(8,128)S(1)}, f32[8,56,128]{2,1,0:T(8,128)S(1)}) custom-call(s32[2]{0:T(128)S(1)} %pad_add_fusion.where_ref, f32[16,80,128]{2,1,0:T(8,128)S(1)} %all_to_all.33.parts_ref, f32[448,128]{1,0:T(8,128)S(1)} %get-tuple-element.45.sigma_ext_ref, f32[16,128]{1,0:T(8,128)S(1)} %get-tuple-element.40.listed_ref), custom_call_target="tpu_custom_call" | custom-call | tf_op jit(solution)/shard_map/gather_last/pallas_call | solution.py:608
  117.7 17.1 %all_to_all.34.message_ref = f32[8,56,128]{2,1,0:T(8,128)S(1)} all-to-all(f32[8,56,128]{2,1,0:T(8,128)S(1)} %get-tuple-element.58), channel_id=1, replica_groups=mesh['tx'=16,'ty'=8] {'ty'}, dimensions={0} | all-to-all | bytes 458752 | tf_op jit(solution)/shard_map/all_to_all | solution.py:706
  134.8 3.8 %spread_last.1 = (f32[4,64,128]{2,1,0:T(8,128)}, f32[4,64,128]{2,1,0:T(8,128)}) custom-call(s32[2]{0:T(128)S(1)} %pad_add_fusion.where_ref, s32[4]{0:T(128)S(1)} %copy-done.8, f32[448,128]{1,0:T(8,128)S(1)} %get-tuple-element.57.field_ref, f32[8,56,128]{2,1,0:T(8,128)S(1)} %all_to_all.34.message_ref, f32[896,128]{1,0:T(8,128)S(1)} %get-tuple-element.49.along_ref, ...), custom_call_target="tpu_custom_call" | custom-call | tf_op jit(solution)/shard_map/spread_last/pallas_call | solution.py:608
  (30 shorter events, 2.7 us)
Async XLA Ops:
  2.5 15.2 %collective-permute-start.1 = (f32[2,4,24,128]{3,2,1,0:T(8,128)S(1)}, f32[2,4,24,128]{3,2,1,0:T(8,128)S(1)}, u32[]{:S(2)}, u32[]{:S(2)}) collective-permute-start(f32[2,4,24,128]{3,2,1,0:T(8,128)S(1)} %get-tuple-element.60), channel_id=1, source_target_pairs={{0,120},{8,16},{16,8},{24,32},{32,24},{40,48},{48,40},{56,64},{64,... | collective-permute-start | bytes 294920 | tf_op jit(solution)/shard_map/ppermute | solution.py:623
  9.4 8.3 %collective-permute-start = (f32[2,4,24,128]{3,2,1,0:T(8,128)S(1)}, f32[2,4,24,128]{3,2,1,0:T(8,128)S(1)}, u32[]{:S(2)}, u32[]{:S(2)}) collective-permute-start(f32[2,4,24,128]{3,2,1,0:T(8,128)S(1)} %get-tuple-element.61), channel_id=1, source_target_pairs={{0,8},{8,0},{16,24},{24,16},{32,40},{40,32},{48,56},{56,48},{64,72... | collective-permute-start | bytes 294920 | tf_op jit(solution)/shard_map/ppermute | solution.py:623
  10.0 22.9 %copy-start.2 = (f32[4,64,128]{2,1,0:T(8,128)S(1)}, f32[4,64,128]{2,1,0:T(8,128)}, u32[]{:S(2)}) copy-start(f32[4,64,128]{2,1,0:T(8,128)} %sigma_ref.5) | copy-start | bytes 393220
  10.0 22.9 %copy-start.4 = (s32[4,64,128]{2,1,0:T(8,128)S(1)}, s32[4,64,128]{2,1,0:T(8,128)}, u32[]{:S(2)}) copy-start(s32[4,64,128]{2,1,0:T(8,128)} %mask_ref.1) | copy-start | bytes 393220
  10.0 22.8 %copy-start.5 = (f32[4,64,128]{2,1,0:T(8,128)S(1)}, f32[4,64,128]{2,1,0:T(8,128)}, u32[]{:S(2)}) copy-start(f32[4,64,128]{2,1,0:T(8,128)} %diffusivity_ref.1) | copy-start | bytes 393220
  17.7 15.2 %all-to-all-start = ((f32[16,80,128]{2,1,0:T(8,128)}), f32[16,80,128]{2,1,0:T(8,128)S(1)}, u32[]{:S(2)}, u32[]{:S(2)}) async-start(f32[16,80,128]{2,1,0:T(8,128)} %get-tuple-element.32), calls=%async_computation | async-start | bytes 1310720 | tf_op jit(solution)/shard_map/all_to_all | solution.py:627
  21.3 21.1 %copy-start.8 = (s32[4]{0:T(128)S(1)}, s32[4]{0:T(128)}, u32[]{:S(2)}) copy-start(s32[4]{0:T(128)} %count_ref.8) | copy-start | bytes 52
  21.3 37.7 %copy-start.3 = (f32[128,128]{1,0:T(8,128)S(1)}, f32[128,128]{1,0:T(8,128)}, u32[]{:S(2)}) copy-start(f32[128,128]{1,0:T(8,128)} %weight_ref.5) | copy-start | bytes 196612
  21.3 37.6 %copy-start.6 = (f32[128,128]{1,0:T(8,128)S(1)}, f32[128,128]{1,0:T(8,128)}, u32[]{:S(2)}) copy-start(f32[128,128]{1,0:T(8,128)} %get-tuple-element.43.earlier_ref) | copy-start | bytes 196612
  21.3 37.6 %copy-start.7 = (s32[128,1]{0,1:T(1,128)S(1)}, s32[128,1]{0,1:T(1,128)}, u32[]{:S(2)}) copy-start(s32[128,1]{0,1:T(1,128)} %param.13) | copy-start | bytes 1540
  32.9 0.7 copy-start.9
  35.4 7.0 %collective-permute-start.2 = (f32[2,112,128]{2,1,0:T(8,128)S(1)}, f32[2,112,128]{2,1,0:T(8,128)S(1)}, u32[]{:S(2)}, u32[]{:S(2)}) collective-permute-start(f32[2,112,128]{2,1,0:T(8,128)S(1)} %get-tuple-element.38), channel_id=1, source_target_pairs={{0,1},{1,0},{2,3},{3,2},{4,5},{5,4},{6,7},{7,6},{8,9},{9,8},{10,11... | collective-permute-start | bytes 344072 | tf_op jit(solution)/shard_map/ppermute | solution.py:623
  37.7 4.7 %collective-permute-start.3 = (f32[2,112,128]{2,1,0:T(8,128)S(1)}, f32[2,112,128]{2,1,0:T(8,128)S(1)}, u32[]{:S(2)}, u32[]{:S(2)}) collective-permute-start(f32[2,112,128]{2,1,0:T(8,128)S(1)} %get-tuple-element.39), channel_id=1, source_target_pairs={{0,7},{1,2},{2,1},{3,4},{4,3},{5,6},{6,5},{7,0},{8,15},{9,10},{10,... | collective-permute-start | bytes 344072 | tf_op jit(solution)/shard_map/ppermute | solution.py:623
  39.0 3.4 %copy-start = (f32[128,128,128]{2,1,0:T(8,128)S(1)}, f32[128,128,128]{2,1,0:T(8,128)}, u32[]{:S(2)}) copy-start(f32[128,128,128]{2,1,0:T(8,128)} %get-tuple-element.41._.turned_ref) | copy-start | bytes 25165828
  42.4 16.6 %copy-start.1 = (f32[128,128,128]{2,1,0:T(8,128)S(1)}, f32[128,128,128]{2,1,0:T(8,128)}, u32[]{:S(2)}) copy-start(f32[128,128,128]{2,1,0:T(8,128)} %get-tuple-element.41._.turned_ref) | copy-start | bytes 25165828
  76.1 6.2 %collective-permute-start.4 = (f32[1,112,128]{2,1,0:T(8,128)S(1)}, f32[1,112,128]{2,1,0:T(8,128)S(1)}, u32[]{:S(2)}, u32[]{:S(2)}) collective-permute-start(f32[1,112,128]{2,1,0:T(8,128)S(1)} %get-tuple-element.47), channel_id=1, source_target_pairs={{0,1},{1,0},{2,3},{3,2},{4,5},{5,4},{6,7},{7,6},{8,9},{9,8},{10,11... | collective-permute-start | bytes 172040 | tf_op jit(solution)/shard_map/ppermute | solution.py:623
  80.6 3.6 %collective-permute-start.5 = (f32[1,112,128]{2,1,0:T(8,128)S(1)}, f32[1,112,128]{2,1,0:T(8,128)S(1)}, u32[]{:S(2)}, u32[]{:S(2)}) collective-permute-start(f32[1,112,128]{2,1,0:T(8,128)S(1)} %get-tuple-element.48), channel_id=1, source_target_pairs={{0,7},{1,2},{2,1},{3,4},{4,3},{5,6},{6,5},{7,0},{8,15},{9,10},{10,... | collective-permute-start | bytes 172040 | tf_op jit(solution)/shard_map/ppermute | solution.py:623

commit v3 on v2

--- a/solution.py
+++ b/solution.py
@@ -27,27 +27,20 @@
 PART = 80
 GROUP = 16
 GROUPS = OWN // GROUP
-WIDE = 16
-STRIP = 48
-LAST = STRIP + 8
 
 
 def iota(shape, dim):
     return lax.broadcasted_iota(jnp.int32, shape, dim)
 
 
-def thirds(values):
+def pieces(values):
     high = values.astype(BF16)
-    rest = values - high.astype(F32)
-    middle = rest.astype(BF16)
-    low = (rest - middle.astype(F32)).astype(BF16)
-    return high, middle, low
+    return high, (values - high.astype(F32)).astype(BF16)
 
 
 def pick(onehot, values):
-    high, middle, low = thirds(values)
+    high, low = pieces(values)
     total = jnp.dot(onehot, high, preferred_element_type=F32)
-    total = total + jnp.dot(onehot, middle, preferred_element_type=F32)
     return total + jnp.dot(onehot, low, preferred_element_type=F32)
 
 
@@ -125,7 +118,7 @@
 
 def first_kernel(
     count_ref, tile_ref, column_ref, innovation_ref, weight_ref, operator_ref,
-    parts_ref, adjoint_ref, blocks_ref, repeated_ref, arrived,
+    parts_ref, adjoint_ref, blocks_ref, arrived,
 ):
     copy_of = load_blocks(operator_ref, blocks_ref, arrived)
     start_all(copy_of)
@@ -133,27 +126,24 @@
     listed = listed_columns(tables, column_ref)
     for tile in range(TX):
         parts_ref[tile, pl.ds(LISTED, 8), :] = jnp.broadcast_to(listed[tile : tile + 1], (8, 128))
-    eye = as_onehot(iota((OWN, OWN), 0) == iota((OWN, OWN), 1))
-    ones = jnp.ones((2 * OWN, 128), BF16)
+    down = iota((8, 128), 0)
 
     def one_group(number, carry):
         here = group(number)
         live = iota((GROUP, OWN), 0) + number * GROUP < count_ref[0]
         weighted = jnp.where(live, weight_ref[here, :] * innovation_ref[here, :], 0.0)
-        high, middle, _ = thirds(weighted)
-        diagonals = [
-            jnp.concatenate([eye * high[k : k + 1], eye * middle[k : k + 1]], axis=1)
-            for k in range(GROUP)
-        ]
-        repeated_ref[...] = jnp.dot(
-            jnp.concatenate(diagonals, axis=0), ones, preferred_element_type=F32
-        )
+        high = weighted.astype(BF16).astype(F32)
+        low = weighted - high
         copy_of(number).wait()
         rows = []
         for k in range(GROUP):
-            column = repeated_ref[pl.ds(k * OWN, OWN), :]
-            block = blocks_ref[number * GROUP + k]
-            rows.append(jnp.sum(block * column, axis=0, keepdims=True))
+            wide = jnp.broadcast_to(high[k : k + 1], (8, 128))
+            narrow = jnp.broadcast_to(low[k : k + 1], (8, 128))
+            first = jnp.where(down == 0, wide, 0.0)
+            left = jnp.concatenate([jnp.where(down == 1, narrow, first), first], axis=1).astype(BF16)
+            right = jnp.concatenate(pieces(blocks_ref[number * GROUP + k]), axis=0)
+            product = jnp.dot(left, right, preferred_element_type=F32)
+            rows.append(jnp.sum(product, axis=0, keepdims=True))
         adjoint_ref[here, :] = jnp.concatenate(rows, axis=0)
         return carry
 
@@ -213,8 +203,9 @@
     before = sums_in_ref[0][2:4] if sums_in_ref else jnp.zeros((2, 128), F32)
     sums = jnp.concatenate([before, known, new, jnp.zeros((4, 128), F32)], axis=0)
     sums_ref[...] = sums
-    for tile in range(TX):
-        parts_ref[tile, pl.ds(LISTED, 8), :] = sums
+    if sums_in_ref:
+        for tile in range(TX):
+            parts_ref[tile, pl.ds(LISTED, 8), :] = sums
     adjoint_ref[...] = adjoint + earlier_ref[...]
 
 
@@ -225,6 +216,7 @@
 HERE = pl.BlockSpec(memory_space=pltpu.VMEM)
 THERE = pl.BlockSpec(memory_space=pltpu.HBM)
 CUBE = (OWN, 128, 128)
+PLAIN_PARTS = jax.ShapeDtypeStruct((TX, LISTED, 128), F32)
 PARTS = jax.ShapeDtypeStruct((TX, PART, 128), F32)
 SQUARE = jax.ShapeDtypeStruct((OWN, 128), F32)
 SUMS = jax.ShapeDtypeStruct((8, 128), F32)
@@ -238,7 +230,6 @@
         out_shape=[PARTS, SQUARE],
         scratch_shapes=[
             pltpu.VMEM(CUBE, F32),
-            pltpu.VMEM((GROUP * OWN, 128), F32),
             pltpu.SemaphoreType.DMA((GROUPS,)),
         ],
         compiler_params=pltpu.CompilerParams(vmem_limit_bytes=VMEM_FIRST),
@@ -270,7 +261,7 @@
         middle_kernel,
         in_specs=[SCALARS] + [HERE] * (5 + len(sums)),
         out_specs=[HERE, HERE, HERE],
-        out_shape=[PARTS, SQUARE, SUMS],
+        out_shape=[PARTS if sums else PLAIN_PARTS, SQUARE, SUMS],
         scratch_shapes=[pltpu.VMEM((OWN, OWN), F32)],
         compiler_params=pltpu.CompilerParams(vmem_limit_bytes=VMEM_OBSERVE),
         cost_estimate=pl.CostEstimate(flops=8 * 128**3, bytes_accessed=10 << 20, transcendentals=0),
@@ -278,32 +269,43 @@
     )(counts, tile, weight, returned, earlier, turned, *sums)
 
 
-def scatter(parts_ref, listed):
-    column = listed.astype(jnp.int32)
-    level = column >> 6
-    cell = column & (CX - 1)
-    lane = iota((TX, 128), 1)
-    left = lane < CAP
-    right = lane >= 2 * CAP
-    place = jnp.where(left, cell - (CX - SIDE), jnp.where(right, cell + CX + SIDE, cell + SIDE))
-    good = (lane < LISTED) & (place >= 0) & (place < EXT)
-    row = jnp.where(good, level * EXT + place, -1)
-    turned = pltpu.roll(row, PART, 1)
-    one = jnp.where(lane < PART, row, turned)
-    two = jnp.where(
-        lane < 2 * PART - 128,
-        turned,
-        jnp.where(lane < 3 * PART - 128, pltpu.roll(row, 2 * PART - 128, 1), -1),
-    )
-    triple = jnp.concatenate([one, two], axis=1)
-    down = iota((ROWS, 256), 0)
-    total = jnp.zeros((ROWS, 128), F32)
-    blank = jnp.zeros((256 - 3 * PART, 128), BF16)
+def flat_list(listed, part):
+    lane = iota((1, 128), 1)
+    words = [jnp.zeros((1, 128), F32)] * (SLOTS // 128)
     for source in range(TX):
-        onehot = as_onehot(down == triple[source : source + 1])
-        stacked = jnp.concatenate([*thirds(parts_ref[source]), blank], axis=0)
-        total = total + jnp.dot(onehot, stacked, preferred_element_type=F32)
-    return total
+        start = CAP * source
+        turned = pltpu.roll(listed[source : source + 1], (start - CAP * part) % 128, 1)
+        for word in range(start // 128, (start + CAP - 1) // 128 + 1):
+            here = (lane + 128 * word >= start) & (lane + 128 * word < start + CAP)
+            words[word] = jnp.where(here, turned, words[word])
+    return jnp.concatenate(words, axis=1).astype(jnp.int32)
+
+
+def target_rows(listed):
+    west, own, east = (flat_list(listed, part) for part in range(3))
+    cell = west & (CX - 1)
+    west = jnp.where(cell >= CX - SIDE, (west >> 6) * SIDE + cell - (CX - SIDE), -1)
+    cell = east & (CX - 1)
+    east = jnp.where(cell < SIDE, (east >> 6) * SIDE + cell, -1)
+    return jnp.concatenate([west, own, east, jnp.zeros((5, SLOTS), jnp.int32)], axis=0)
+
+
+def scatter(field_ref, parts_ref, rows_ref, sigma_ext_ref):
+    at = 0
+    for part, width in ((0, SIDE), (1, CX), (2, SIDE)):
+        values = jnp.concatenate(
+            [parts_ref[source, pl.ds(part * CAP, CAP), :] for source in range(TX)], axis=0
+        )
+        onehot = as_onehot(iota((LEV * width, SLOTS), 0) == rows_ref[part : part + 1, :])
+        total = jnp.dot(
+            jnp.concatenate([onehot, onehot], axis=1),
+            jnp.concatenate(pieces(values), axis=0),
+            preferred_element_type=F32,
+        )
+        for level in range(LEV):
+            here = pl.ds(level * EXT + at, width)
+            field_ref[here, :] = total[level * width : (level + 1) * width] * sigma_ext_ref[here, :]
+        at += width
 
 
 def edges(field, even):
@@ -323,13 +325,24 @@
     return lax.axis_index(axis) % 2 == 0
 
 
+def prepare_kernel(mask_ref, diffusivity_ref, sigma_ref, kappa_ref, pair_ref, other_ref):
+    even = parity("tx")
+    for level in range(LEV):
+        kappa = diffusivity_ref[level] * mask_ref[level].astype(F32)
+        kappa_ref[level] = kappa
+        for number, values in ((0, kappa), (1, sigma_ref[level])):
+            low, high = values[:SIDE], values[CX - SIDE :]
+            pair_ref[number, level] = jnp.where(even, high, low)
+            other_ref[number, level] = jnp.where(even, low, high)
+
+
 def open_kernel(
-    where_ref, parts_ref, sigma_ref, mask_ref, diffusivity_ref, near_ref, far_ref, _,
-    field_ref, sigma_ext_ref, kappa_ext_ref, pair_ref, other_ref, listed_ref,
+    parts_ref, sigma_ref, kappa_ref, near_ref, far_ref, _,
+    field_ref, sigma_ext_ref, kappa_ext_ref, pair_ref, other_ref, listed_ref, rows_ref,
 ):
-    row_no = where_ref[0]
-    even_row = row_no % 2 == 0
-    even = where_ref[1] % 2 == 0
+    row_no = lax.axis_index("tx")
+    even_row = parity("tx")
+    even = parity("ty")
     not_first = jnp.where(row_no > 0, 1.0, 0.0)
     not_last = jnp.where(row_no < TX - 1, 1.0, 0.0)
     for level in range(LEV):
@@ -337,7 +350,7 @@
         near_k, far_k = near_ref[0, level], far_ref[0, level]
         near_s, far_s = near_ref[1, level], far_ref[1, level]
         kappa_ext_ref[pl.ds(base, SIDE), :] = jnp.where(even_row, far_k, near_k) * not_first
-        kappa_ext_ref[pl.ds(base + SIDE, CX), :] = diffusivity_ref[level] * mask_ref[level].astype(F32)
+        kappa_ext_ref[pl.ds(base + SIDE, CX), :] = kappa_ref[level]
         kappa_ext_ref[pl.ds(base + SIDE + CX, SIDE), :] = jnp.where(even_row, near_k, far_k) * not_last
         sigma_ext_ref[pl.ds(base, SIDE), :] = jnp.where(even_row, far_s, near_s)
         sigma_ext_ref[pl.ds(base + SIDE, CX), :] = sigma_ref[level]
@@ -345,9 +358,9 @@
     sigma_ext_ref[...] = jnp.where(kappa_ext_ref[...] > 0.0, sigma_ext_ref[...], 0.0)
     listed = jnp.concatenate([parts_ref[k, pl.ds(LISTED, 1), :] for k in range(TX)], axis=0)
     listed_ref[...] = listed
-    field = scatter(parts_ref, listed) * sigma_ext_ref[...]
-    field_ref[...] = field
-    pair_ref[0], other_ref[0] = edges(field, even)
+    rows_ref[...] = target_rows(listed)
+    scatter(field_ref, parts_ref, rows_ref, sigma_ext_ref)
+    pair_ref[0], other_ref[0] = edges(field_ref[...], even)
     pair_ref[1], other_ref[1] = edges(kappa_ext_ref[...], even)
 
 
@@ -355,47 +368,37 @@
     brought_ref[...] = listed_ref[:8]
 
 
-def gather_kernel(where_ref, parts_ref, sigma_ext_ref, listed_ref, field_ref, pair_ref, other_ref):
-    field = scatter(parts_ref, listed_ref[...]) * sigma_ext_ref[...]
-    field_ref[...] = field
-    pair_ref[0], other_ref[0] = edges(field, where_ref[1] % 2 == 0)
-
-
-FIRST_ROW = SIDE - NSTEP - 6
-
-
-def last_gather_kernel(where_ref, parts_ref, sigma_ext_ref, listed_ref, field_ref, message_ref):
-    field = scatter(parts_ref, listed_ref[...]) * sigma_ext_ref[...]
-    field_ref[...] = field
-    lane = iota((STRIP, 128), 1)
-    west = jnp.zeros((STRIP, 128), F32)
-    east = jnp.zeros((STRIP, 128), F32)
-    for level in range(LEV):
-        for half in range(2):
-            start = level * EXT + FIRST_ROW + half * STRIP
-            part = field[start : start + STRIP]
-            at = WIDE * (2 * level + half)
-            here = (lane >= at) & (lane < at + NSTEP)
-            west = jnp.where(here, pltpu.roll(part, at, 1) if at else part, west)
-            east = jnp.where(here, pltpu.roll(part, (at + NSTEP) % 128, 1), east)
+def gather_kernel(parts_ref, sigma_ext_ref, rows_ref, field_ref, pair_ref, other_ref):
+    scatter(field_ref, parts_ref, rows_ref, sigma_ext_ref)
+    pair_ref[0], other_ref[0] = edges(field_ref[...], parity("ty"))
+
+
+def last_gather_kernel(parts_ref, sigma_ext_ref, rows_ref, field_ref, pair_ref, other_ref, sums_ref):
+    scatter(field_ref, parts_ref, rows_ref, sigma_ext_ref)
+    pair_ref[0, pl.ds(0, EXT), :], other_ref[0, pl.ds(0, EXT), :] = edges(field_ref[...], parity("ty"))
     sums = parts_ref[0, pl.ds(LISTED, 8), :]
     for source in range(1, TX):
         sums = sums + parts_ref[source, pl.ds(LISTED, 8), :]
-    me = where_ref[1]
-    for band in range(TY):
-        message_ref[band, pl.ds(0, STRIP), :] = jnp.where(band == me + 1, east, west)
-        message_ref[band, pl.ds(STRIP, 8), :] = sums
-
-
-def widen(work_ref, field_ref, west_of, east_of, reach):
+    pair_ref[0, pl.ds(EXT, 8), :] = sums
+    other_ref[0, pl.ds(EXT, 8), :] = sums
+    sums_ref[...] = sums
+
+
+def meet_kernel(sums_ref, near_ref, far_ref, three_ref, two_ref):
+    near, far = near_ref[0, pl.ds(EXT, 8), :], far_ref[0, pl.ds(EXT, 8), :]
+    two_ref[...] = sums_ref[...] + jnp.where(parity("ty"), far, near)
+    three_ref[...] = sums_ref[...] + near + far
+
+
+def widen(work_ref, field_ref, west_of, east_of):
     lane = iota((EXT, 128), 1)
     for level in range(LEV):
         part = field_ref[pl.ds(level * EXT, EXT), :]
         first = jnp.where(
-            (lane >= HALO - reach) & (lane < HALO), west_of(level), pltpu.roll(part, HALO, 1)
+            lane < HALO, west_of(level), pltpu.roll(part, HALO, 1)
         )
         second = jnp.where(
-            (lane >= 128 - HALO) & (lane < 128 - HALO + reach),
+            lane >= 128 - HALO,
             east_of(level),
             pltpu.roll(part, 128 - HALO, 1),
         )
@@ -419,7 +422,7 @@
 
 
 def sweeps(work_ref, along_ref, across_ref, counts, first_row, end_row):
-    def one(number, masked):
+    def one(number, masked, first_row, end_row):
         active = counts > number
         flux = None
         now = work_ref[pl.ds(first_row * 8, 8), :]
@@ -439,16 +442,16 @@
             work_ref[here, :] = now + change
             now = after
 
-    def run(start, end, masked):
+    def run(start, end, masked, *rows):
         def body(index, carry):
             for k in range(UNROLL):
-                one(start + index * UNROLL + k, masked)
+                one(start + index * UNROLL + k, masked, *rows)
             return carry
 
         lax.fori_loop(0, (end - start) // UNROLL, body, 0)
 
-    run(0, MIN_STEPS, False)
-    run(MIN_STEPS, NSTEP, True)
+    run(0, MIN_STEPS, False, first_row, end_row)
+    run(MIN_STEPS, NSTEP, True, first_row + MIN_STEPS, end_row - MIN_STEPS)
 
 
 def faces(work_ref, along_ref, across_ref):
@@ -480,8 +483,9 @@
     return west_of, east_of
 
 
-def from_pairs(near_ref, far_ref, which, even):
-    near, far = near_ref[which], far_ref[which]
+def from_pairs(near_ref, far_ref, which):
+    near, far = near_ref[which, pl.ds(0, EXT), :], far_ref[which, pl.ds(0, EXT), :]
+    even = parity("ty")
     return jnp.where(even, far, near), jnp.where(even, near, far)
 
 
@@ -501,17 +505,16 @@
 
 
 def spread_first_kernel(
-    where_ref, count_ref, field_ref, kappa_ext_ref, near_ref, far_ref, sigma_ref, listed_ref, _,
+    count_ref, field_ref, kappa_ext_ref, near_ref, far_ref, sigma_ref, listed_ref, _,
     picked_ref, once_ref, twice_ref, along_ref, across_ref, work_ref,
 ):
-    band = where_ref[1]
-    even = band % 2 == 0
-    west, east = from_pairs(near_ref, far_ref, 1, even)
+    band = lax.axis_index("ty")
+    west, east = from_pairs(near_ref, far_ref, 1)
     west = west * jnp.where(band > 0, 1.0, 0.0)
     east = east * jnp.where(band < TY - 1, 1.0, 0.0)
-    widen(work_ref, kappa_ext_ref, *strips((west, east)), HALO)
+    widen(work_ref, kappa_ext_ref, *strips((west, east)))
     faces(work_ref, along_ref, across_ref)
-    widen(work_ref, field_ref, *strips(from_pairs(near_ref, far_ref, 0, even)), HALO)
+    widen(work_ref, field_ref, *strips(from_pairs(near_ref, far_ref, 0)))
     counts = level_counts(count_ref)
     sweeps(work_ref, along_ref, across_ref, counts, *OUTER)
     for level in range(LEV):
@@ -526,12 +529,11 @@
 
 
 def spread_next_kernel(
-    where_ref, count_ref, field_ref, near_ref, far_ref, sigma_ref, listed_ref, along_ref, across_ref,
+    count_ref, field_ref, near_ref, far_ref, sigma_ref, listed_ref, along_ref, across_ref,
     once_ref, twice_ref,
     picked_ref, image_ref, work_ref,
 ):
-    even = where_ref[1] % 2 == 0
-    widen(work_ref, field_ref, *strips(from_pairs(near_ref, far_ref, 0, even)), HALO)
+    widen(work_ref, field_ref, *strips(from_pairs(near_ref, far_ref, 0)))
     counts = level_counts(count_ref)
     sweeps(work_ref, along_ref, across_ref, counts, *OUTER)
     for level in range(LEV):
@@ -543,32 +545,17 @@
     send_segments(picked_ref, listed_ref, jnp.concatenate(parts, axis=0))
 
 
-def spread_last_kernel(
-    where_ref, count_ref, field_ref, message_ref, along_ref, across_ref, start_ref, image_ref,
-    control_ref, residual_ref, work_ref,
+def spread_last_kernel(count_ref, field_ref, near_ref, far_ref, along_ref, across_ref, last_ref, work_ref):
+    widen(work_ref, field_ref, *strips(from_pairs(near_ref, far_ref, 0)))
+    sweeps(work_ref, along_ref, across_ref, level_counts(count_ref), *INNER)
+    for level in range(LEV):
+        last_ref[level] = tile_part(work_ref, level)
+
+
+def finish_kernel(
+    last_ref, three_ref, next_ref, previous_ref, start_ref, image_ref, control_ref, residual_ref
 ):
-    band = where_ref[1]
-    west = message_ref[jnp.maximum(band - 1, 0), pl.ds(0, STRIP), :]
-    east = message_ref[jnp.minimum(band + 1, TY - 1), pl.ds(0, STRIP), :]
-    blank = jnp.zeros((FIRST_ROW, 128), F32)
-
-    def side_of(packed, shift):
-        def of(level):
-            halves = [
-                pltpu.roll(packed, (2 * 128 + shift - WIDE * (2 * level + half)) % 128, 1)
-                for half in range(2)
-            ]
-            return jnp.concatenate([blank, *halves, blank], axis=0)
-
-        return of
-
-    widen(work_ref, field_ref, side_of(west, HALO - NSTEP), side_of(east, 128 - HALO), NSTEP)
-    counts = level_counts(count_ref)
-    sweeps(work_ref, along_ref, across_ref, counts, *INNER)
-
-    sums = message_ref[0, pl.ds(STRIP, 8), :]
-    for source in range(1, TY):
-        sums = sums + message_ref[source, pl.ds(STRIP, 8), :]
+    sums = three_ref[...] + next_ref[...] + previous_ref[...]
     sums = jnp.sum(sums, axis=1, keepdims=True)
     start_start = sums[0:1]
     start_image = sums[0:1] + sums[1:2]
@@ -584,7 +571,7 @@
     for level in range(LEV):
         start = start_ref[level]
         image = image_ref[level]
-        twice = image + tile_part(work_ref, level)
+        twice = image + last_ref[level]
         remainder = start - step * image
         direction = remainder + ratio * start
         curved = (1.0 + ratio) * image - step * twice
@@ -596,12 +583,13 @@
 TILE = jax.ShapeDtypeStruct((LEV, CX, CY), F32)
 WIDENED = jax.ShapeDtypeStruct((ROWS, 128), F32)
 LAID = jax.ShapeDtypeStruct((EXT * 8, 128), F32)
+TARGETS = jax.ShapeDtypeStruct((8, SLOTS), jnp.int32)
 LISTS = jax.ShapeDtypeStruct((TX, 128), F32)
 PICKED = jax.ShapeDtypeStruct((SLOTS, 128), F32)
 
 
-def edge_shape(number):
-    return jax.ShapeDtypeStruct((number, EXT, 128), F32)
+def edge_shape(number, more=0):
+    return jax.ShapeDtypeStruct((number, EXT + more, 128), F32)
 
 
 def tile_call(kernel, out_shape, scalars, arrays, name, scratch=(), after=()):
@@ -639,25 +627,26 @@
     background_std,
     step_counts,
 ):
-    where = jnp.stack([lax.axis_index("tx"), lax.axis_index("ty")]).astype(jnp.int32)
     tile = block_tile.reshape(1, OWN)
     column = block_column.reshape(1, OWN)
 
-    masked = diffusivity * sea_mask.astype(F32)
-    low = jnp.stack([masked[:, :SIDE], background_std[:, :SIDE]])
-    high = jnp.stack([masked[:, CX - SIDE :], background_std[:, CX - SIDE :]])
-    even = parity("tx")
-    near_x, far_x = swap_neighbours(jnp.where(even, high, low), jnp.where(even, low, high), "tx")
-
+    rows_shape = jax.ShapeDtypeStruct((2, LEV, SIDE, 128), F32)
+    kappa, pair, other = tile_call(
+        prepare_kernel,
+        (TILE, rows_shape, rows_shape),
+        (),
+        (sea_mask, diffusivity, background_std),
+        "prepare",
+    )
+    near_x, far_x = swap_neighbours(pair, other, "tx")
     parts, adjoint = run_first(owner_counts, tile, column, innovation, obs_weight, obs_operator)
-    parts, near_x, far_x = lax.optimization_barrier((parts, near_x, far_x))
     turned, done = run_turn(obs_operator)
     parts = exchange(parts)
-    field, sigma_ext, kappa_ext, pair, other, listed = tile_call(
+    field, sigma_ext, kappa_ext, pair, other, listed, rows = tile_call(
         open_kernel,
-        (WIDENED, WIDENED, WIDENED, edge_shape(2), edge_shape(2), LISTS),
-        (where,),
-        (parts, background_std, sea_mask, diffusivity, near_x, far_x),
+        (WIDENED, WIDENED, WIDENED, edge_shape(2), edge_shape(2), LISTS, TARGETS),
+        (),
+        (parts, background_std, kappa, near_x, far_x),
         "open_tile",
         after=(done,),
     )
@@ -666,7 +655,7 @@
     picked, once, twice, along, across = tile_call(
         spread_first_kernel,
         (PICKED, TILE, TILE, LAID, LAID),
-        (where, step_counts),
+        (step_counts,),
         (field, kappa_ext, near, far, background_std, listed),
         "spread_first",
         WORK,
@@ -678,15 +667,15 @@
     field, pair, other = tile_call(
         gather_kernel,
         (WIDENED, edge_shape(1), edge_shape(1)),
-        (where,),
-        (parts, sigma_ext, listed),
+        (),
+        (parts, sigma_ext, rows),
         "gather_tile",
     )
     near, far = swap_neighbours(pair, other, "ty")
     picked, image = tile_call(
         spread_next_kernel,
         (PICKED, TILE),
-        (where, step_counts),
+        (step_counts,),
         (field, near, far, background_std, listed, along, across, once, twice),
         "spread_next",
         WORK,
@@ -696,21 +685,28 @@
         owner_counts, tile, obs_weight, returned, adjoint, turned, sums
     )
     parts = exchange(parts)
-    field, message = tile_call(
+    field, pair, other, sums = tile_call(
         last_gather_kernel,
-        (WIDENED, jax.ShapeDtypeStruct((TY, LAST, 128), F32)),
-        (where,),
-        (parts, sigma_ext, listed),
+        (WIDENED, edge_shape(1, 8), edge_shape(1, 8), SUMS),
+        (),
+        (parts, sigma_ext, rows),
         "gather_last",
     )
-    message = lax.all_to_all(message, "ty", split_axis=0, concat_axis=0, tiled=True)
-    control_field, residual = tile_call(
+    near, far = swap_neighbours(pair, other, "ty")
+    three, two = tile_call(meet_kernel, (SUMS, SUMS), (), (sums, near, far), "meet")
+    bands = lax.axis_size("ty")
+    after = lax.ppermute(three, "ty", [(i, (i - 3) % bands) for i in range(bands)])
+    before = lax.ppermute(two, "ty", [(i, (i + 2) % bands) for i in range(bands)])
+    last = tile_call(
         spread_last_kernel,
-        (TILE, TILE),
-        (where, step_counts),
-        (field, message, along, across, once, image),
+        (TILE,),
+        (step_counts,),
+        (field, near, far, along, across),
         "spread_last",
         WORK,
+    )[0]
+    control_field, residual = tile_call(
+        finish_kernel, (TILE, TILE), (), (last, three, after, before, once, image), "finish"
     )
     return control_field, residual
 

time: 139 us -> 127 us (0.914)
  blocking collectives: 63.4 us -> 45.9 us
  starting transfers between devices: 20.2 us -> 34.1 us
  Pallas kernels: 42.2 us -> 35.4 us
    all_to_all x1 -> x0, blocking collectives: 17.1 us -> none  [body(): lax.all_to_all(message, 'ty', split_axis=0, concat_axis=0, tiled=True)]
    ppermute x0 -> x2, starting transfers between devices: none -> 6.34 us  [the longest x1 5.37 us: body(): lax.ppermute(three, 'ty', [(i, (i - 3) % bands) for i in range(bands)])]
    ppermute x3 -> x4, starting transfers between devices: 6.75 us -> 11.8 us  [swap_neighbours(): lax.ppermute(for_pair, axis, pairs)]
    all_to_all x1, starting transfers between devices: 3.6 us -> 8.44 us  [exchange(): return lax.all_to_all(parts, 'tx', split_axis=0, concat_axis=0, tiled=True)]
    pallas_call x7 -> x10, Pallas kernels: 21.5 us -> 16.6 us  [tile_call(): pl.pallas_call(kernel, in_specs=[SCALARS] * len(scalars) + [HERE] * len(a...]
    ppermute x3 -> x4, waiting for transfers between devices: 1.88 us -> 5.8 us  [swap_neighbours(): lax.ppermute(for_other, axis, others)]
    all_to_all x1, waiting for transfers between devices: 3.37 us -> 0.01 us  [exchange(): return lax.all_to_all(parts, 'tx', split_axis=0, concat_axis=0, tiled=True)]
    ppermute x3 -> x4, starting transfers between devices: 9.86 us -> 7.55 us  [swap_neighbours(): lax.ppermute(for_other, axis, others)]
  transfers between devices with their start and end apart: 7 -> 11, of which waited for: 2 -> 3; matrix products, arithmetic and copies ran while one was open for 0% -> 0% of each run, Pallas kernels for 11% -> 9%
where the time goes in v3:
time: 127 us
  blocking collectives  45.9 us (36%)
  Pallas kernels  35.4 us (28%)
  starting transfers between devices  34.1 us (27%)
  waiting for transfers between devices  5.82 us (5%)
  local copies, waits for them, and re-layouts  4.1 us (3%)
  between operations  1.5 us (1%)
    all_to_all x4, blocking collectives, exchange(): return lax.all_to_all(parts, 'tx', split_axis=0, concat_axis=0, tiled=True)  45.9 us
    pallas_call x10, Pallas kernels, tile_call(): pl.pallas_call(kernel, in_specs=[SCALARS] * len(scalars) + [HERE] * len(a...  16.6 us
    ppermute x4, starting transfers between devices, swap_neighbours(): lax.ppermute(for_pair, axis, pairs)  11.8 us
    all_to_all x1, starting transfers between devices, exchange(): return lax.all_to_all(parts, 'tx', split_axis=0, concat_axis=0, tiled=True)  8.44 us
    pallas_call x1, Pallas kernels, run_turn(): pl.pallas_call(turn_kernel, in_specs=[THERE], out_specs=[THERE, HERE], ou...  8 us
    ppermute x4, starting transfers between devices, swap_neighbours(): lax.ppermute(for_other, axis, others)  7.55 us
    ppermute x4, waiting for transfers between devices, swap_neighbours(): lax.ppermute(for_other, axis, others)  5.8 us
    pallas_call x1, Pallas kernels, run_first(): pl.pallas_call(first_kernel, in_specs=[SCALARS, HERE, HERE, HERE, HERE, T...  5.77 us
  transfers between devices with their start and end apart: 11, of which 3 were waited for; matrix products, arithmetic and copies ran while one was open for 0% of the time, Pallas kernels for 9%

profile of v3, /device:TPU:1, one launch (start us, length us, event | category | flops | bytes accessed | tf_op | source)
XLA Modules:
  0.0 126.9 jit_solution(4970536302650441884)
XLA Ops:
  1.4 5.8 %first_adjoint.1 = (f32[16,80,128]{2,1,0:T(8,128)}, f32[128,128]{1,0:T(8,128)}) custom-call(s32[1]{0:T(128)S(6)} %copy.12.count_ref, s32[1,128]{1,0:T(1,128)} %bitcast.10, s32[1,128]{1,0:T(1,128)} %bitcast.13, f32[128,128]{1,0:T(8,128)} %innovation_ref.1, f32[128,128]{1,0:T(8,128)} %weight_ref.5, f32[128,128,128]{2,1,0:T(8,128)} %operator_ref.3), custom_call_target="tpu_custom_call" | custom-call | flops 8388608 | bytes 9437184 | tf_op jit(solution)/shard_map/first_adjoint/pallas_call | solution.py:226
  7.1 8.4 %all-to-all-start = ((f32[16,80,128]{2,1,0:T(8,128)}), f32[16,80,128]{2,1,0:T(8,128)S(1)}, u32[]{:S(2)}, u32[]{:S(2)}) async-start(f32[16,80,128]{2,1,0:T(8,128)} %get-tuple-element.36), calls=%async_computation | async-start | bytes 1310720 | tf_op jit(solution)/shard_map/all_to_all | solution.py:615
  15.7 1.4 %collective-permute-start = (f32[2,4,24,128]{3,2,1,0:T(8,128)S(1)}, f32[2,4,24,128]{3,2,1,0:T(8,128)S(1)}, u32[]{:S(2)}, u32[]{:S(2)}) collective-permute-start(f32[2,4,24,128]{3,2,1,0:T(8,128)S(1)} %get-tuple-element.38), channel_id=1, source_target_pairs={{0,8},{8,0},{16,24},{24,16},{32,40},{40,32},{48,56},{56,48},{64,72... | collective-permute-start | bytes 294920 | tf_op jit(solution)/shard_map/ppermute | solution.py:611
  17.1 4.0 %collective-permute-start.1 = (f32[2,4,24,128]{3,2,1,0:T(8,128)S(1)}, f32[2,4,24,128]{3,2,1,0:T(8,128)S(1)}, u32[]{:S(2)}, u32[]{:S(2)}) collective-permute-start(f32[2,4,24,128]{3,2,1,0:T(8,128)S(1)} %get-tuple-element.39), channel_id=1, source_target_pairs={{0,120},{8,16},{16,8},{24,32},{32,24},{40,48},{48,40},{56,64},{64,... | collective-permute-start | bytes 294920 | tf_op jit(solution)/shard_map/ppermute | solution.py:611
  21.1 8.0 %blocks_on_lanes.1 = (f32[128,128,128]{2,1,0:T(8,128)}, f32[8,128]{1,0:T(8,128)}) custom-call(f32[128,128,128]{2,1,0:T(8,128)} %operator_ref.3), custom_call_target="tpu_custom_call" | custom-call | bytes 16777216 | tf_op jit(solution)/shard_map/blocks_on_lanes/pallas_call | solution.py:242
  31.3 1.4 %collective-permute-start.2 = (f32[2,112,128]{2,1,0:T(8,128)S(1)}, f32[2,112,128]{2,1,0:T(8,128)S(1)}, u32[]{:S(2)}, u32[]{:S(2)}) collective-permute-start(f32[2,112,128]{2,1,0:T(8,128)S(1)} %get-tuple-element.43), channel_id=1, source_target_pairs={{0,1},{1,0},{2,3},{3,2},{4,5},{5,4},{6,7},{7,6},{8,9},{9,8},{10,11... | collective-permute-start | bytes 344072 | tf_op jit(solution)/shard_map/ppermute | solution.py:611
  32.6 1.3 %collective-permute-start.3 = (f32[2,112,128]{2,1,0:T(8,128)S(1)}, f32[2,112,128]{2,1,0:T(8,128)S(1)}, u32[]{:S(2)}, u32[]{:S(2)}) collective-permute-start(f32[2,112,128]{2,1,0:T(8,128)S(1)} %get-tuple-element.44), channel_id=1, source_target_pairs={{0,7},{1,2},{2,1},{3,4},{4,3},{5,6},{6,5},{7,0},{8,15},{9,10},{10,... | collective-permute-start | bytes 344072 | tf_op jit(solution)/shard_map/ppermute | solution.py:611
  33.9 3.4 %copy-done = f32[128,128,128]{2,1,0:T(8,128)S(1)} copy-done((f32[128,128,128]{2,1,0:T(8,128)S(1)}, f32[128,128,128]{2,1,0:T(8,128)}, u32[]{:S(2)}) %copy-start) | copy-done | bytes 8388632
  37.3 5.9 %spread_first.1 = (f32[384,128]{1,0:T(8,128)S(1)}, f32[4,64,128]{2,1,0:T(8,128)S(1)}, f32[4,64,128]{2,1,0:T(8,128)S(1)}, f32[896,128]{1,0:T(8,128)S(1)}, f32[896,128]{1,0:T(8,128)S(1)}) custom-call(s32[4]{0:T(128)S(1)} %copy-done.7, f32[448,128]{1,0:T(8,128)S(1)} %get-tuple-element.41.field_ref, f32[448,128]{1,0:T(8,128)S(1)} %get-tuple-element.42.kappa_ext_ref, ...), custom_call_target="tpu_custom_call" | custom-call | tf_op jit(solution)/shard_map/spread_first/pallas_call | solution.py:596
  43.2 10.2 %all_to_all.25 = f32[16,24,128]{2,1,0:T(8,128)S(1)} all-to-all(f32[16,24,128]{2,1,0:T(8,128)S(1)} %bitcast.8), channel_id=1, replica_groups=mesh['tx'=16,'ty'=8] {'tx'}, dimensions={0} | all-to-all | bytes 393216 | tf_op jit(solution)/shard_map/all_to_all | solution.py:615
  53.5 2.3 %observe.2 = (f32[16,72,128]{2,1,0:T(8,128)S(1)}, f32[128,128]{1,0:T(8,128)S(1)}, f32[8,128]{1,0:T(8,128)S(1)}) custom-call(s32[1]{0:T(128)S(6)} %copy.12.count_ref, s32[1,128]{1,0:T(1,128)S(1)} %bitcast.11, f32[128,128]{1,0:T(8,128)S(1)} %copy-done.3, f32[384,128]{1,0:T(8,128)S(1)} %bitcast.7, f32[128,128]{1,0:T(8,128)S(1)} %copy-done.6, ...), custom_call_target="tpu_custom_call" | custom-call | flops 16777216 | bytes 10485760 | tf_op jit(solution)/shard_map/observe/pallas_call | solution.py:260
  55.8 12.8 %all_to_all.26.parts_ref = f32[16,72,128]{2,1,0:T(8,128)S(1)} all-to-all(f32[16,72,128]{2,1,0:T(8,128)S(1)} %get-tuple-element.49), channel_id=1, replica_groups=mesh['tx'=16,'ty'=8] {'tx'}, dimensions={0} | all-to-all | bytes 1179648 | tf_op jit(solution)/shard_map/all_to_all | solution.py:615
  69.0 4.5 %collective-permute-start.4 = (f32[1,112,128]{2,1,0:T(8,128)S(1)}, f32[1,112,128]{2,1,0:T(8,128)S(1)}, u32[]{:S(2)}, u32[]{:S(2)}) collective-permute-start(f32[1,112,128]{2,1,0:T(8,128)S(1)} %get-tuple-element.53), channel_id=1, source_target_pairs={{0,1},{1,0},{2,3},{3,2},{4,5},{5,4},{6,7},{7,6},{8,9},{9,8},{10,11... | collective-permute-start | bytes 172040 | tf_op jit(solution)/shard_map/ppermute | solution.py:611
  73.4 1.4 %collective-permute-start.5 = (f32[1,112,128]{2,1,0:T(8,128)S(1)}, f32[1,112,128]{2,1,0:T(8,128)S(1)}, u32[]{:S(2)}, u32[]{:S(2)}) collective-permute-start(f32[1,112,128]{2,1,0:T(8,128)S(1)} %get-tuple-element.54), channel_id=1, source_target_pairs={{0,7},{1,2},{2,1},{3,4},{4,3},{5,6},{6,5},{7,0},{8,15},{9,10},{10,... | collective-permute-start | bytes 172040 | tf_op jit(solution)/shard_map/ppermute | solution.py:611
  74.8 2.2 %collective-permute-done.5.far_ref = f32[1,112,128]{2,1,0:T(8,128)S(1)} collective-permute-done((f32[1,112,128]{2,1,0:T(8,128)S(1)}, f32[1,112,128]{2,1,0:T(8,128)S(1)}, u32[]{:S(2)}, u32[]{:S(2)}) %collective-permute-start.5) | collective-permute-done | bytes 57376 | tf_op jit(solution)/shard_map/ppermute | solution.py:611
  77.0 5.5 %spread_next.1 = (f32[384,128]{1,0:T(8,128)S(1)}, f32[4,64,128]{2,1,0:T(8,128)S(1)}) custom-call(s32[4]{0:T(128)S(1)} %copy-done.7, f32[448,128]{1,0:T(8,128)S(1)} %get-tuple-element.52.field_ref, f32[1,112,128]{2,1,0:T(8,128)S(1)} %collective-permute-done.4.near_ref, f32[1,112,128]{2,1,0:T(8,128)S(1)} %collective-permute-done.5.far_ref, ...), custom_call_target="tpu_custom_call" | custom-call | tf_op jit(solution)/shard_map/spread_next/pallas_call | solution.py:596
  82.6 10.0 %all_to_all.27 = f32[16,24,128]{2,1,0:T(8,128)S(1)} all-to-all(f32[16,24,128]{2,1,0:T(8,128)S(1)} %bitcast.9), channel_id=1, replica_groups=mesh['tx'=16,'ty'=8] {'tx'}, dimensions={0} | all-to-all | bytes 393216 | tf_op jit(solution)/shard_map/all_to_all | solution.py:615
  92.6 2.7 %observe.3 = (f32[16,80,128]{2,1,0:T(8,128)S(1)}, f32[128,128]{1,0:T(8,128)}, f32[8,128]{1,0:T(8,128)}) custom-call(s32[1]{0:T(128)S(6)} %copy.12.count_ref, s32[1,128]{1,0:T(1,128)S(1)} %bitcast.12, f32[128,128]{1,0:T(8,128)S(1)} %copy-done.3, f32[384,128]{1,0:T(8,128)S(1)} %bitcast.6, f32[128,128]{1,0:T(8,128)S(1)} %get-tuple-element.60.earlier_ref, ...), custom_call_target="tpu_custom_call" | custom-call | flops 16777216 | bytes 10485760 | tf_op jit(solution)/shard_map/observe/pallas_call | solution.py:260
  95.3 12.9 %all_to_all.28.parts_ref = f32[16,80,128]{2,1,0:T(8,128)S(1)} all-to-all(f32[16,80,128]{2,1,0:T(8,128)S(1)} %get-tuple-element.62), channel_id=1, replica_groups=mesh['tx'=16,'ty'=8] {'tx'}, dimensions={0} | all-to-all | bytes 1310720 | tf_op jit(solution)/shard_map/all_to_all | solution.py:615
  108.7 4.5 %collective-permute-start.6 = (f32[1,120,128]{2,1,0:T(8,128)S(1)}, f32[1,120,128]{2,1,0:T(8,128)S(1)}, u32[]{:S(2)}, u32[]{:S(2)}) collective-permute-start(f32[1,120,128]{2,1,0:T(8,128)S(1)} %get-tuple-element.64), channel_id=1, source_target_pairs={{0,1},{1,0},{2,3},{3,2},{4,5},{5,4},{6,7},{7,6},{8,9},{9,8},{10,11... | collective-permute-start | bytes 184328 | tf_op jit(solution)/shard_map/ppermute | solution.py:611
  114.1 2.7 %collective-permute-done.7.far_ref = f32[1,120,128]{2,1,0:T(8,128)S(1)} collective-permute-done((f32[1,120,128]{2,1,0:T(8,128)S(1)}, f32[1,120,128]{2,1,0:T(8,128)S(1)}, u32[]{:S(2)}, u32[]{:S(2)}) %collective-permute-start.7) | collective-permute-done | bytes 61472 | tf_op jit(solution)/shard_map/ppermute | solution.py:611
  116.9 1.0 collective-permute-start.9
  117.8 5.4 %collective-permute-start.8 = (f32[8,128]{1,0:T(8,128)S(1)}, f32[8,128]{1,0:T(8,128)S(1)}, u32[]{:S(2)}, u32[]{:S(2)}) collective-permute-start(f32[8,128]{1,0:T(8,128)S(1)} %get-tuple-element.67.three_ref), channel_id=1, source_target_pairs={{0,5},{1,6},{2,7},{3,0},{4,1},{5,2},{6,3},{7,4},{8,13},{9,14},{10,... | collective-permute-start | bytes 12296 | tf_op jit(solution)/shard_map/ppermute | solution.py:698
  123.2 2.8 %spread_last.1.last_ref = f32[4,64,128]{2,1,0:T(8,128)S(1)} custom-call(s32[4]{0:T(128)S(1)} %copy-done.7, f32[448,128]{1,0:T(8,128)S(1)} %get-tuple-element.63.field_ref, f32[1,120,128]{2,1,0:T(8,128)S(1)} %collective-permute-done.6.near_ref, f32[1,120,128]{2,1,0:T(8,128)S(1)} %collective-permute-done.7.far_ref, ...), custom_call_target="tpu_custom_call" | custom-call | tf_op jit(solution)/shard_map/spread_last/pallas_call | solution.py:596
  (36 shorter events, 4.9 us)
Async XLA Ops:
  0.6 15.0 %copy-start.2 = (f32[4,64,128]{2,1,0:T(8,128)S(1)}, f32[4,64,128]{2,1,0:T(8,128)}, u32[]{:S(2)}) copy-start(f32[4,64,128]{2,1,0:T(8,128)} %sigma_ref.7) | copy-start | bytes 393220
  0.6 15.0 %copy-start.5 = (f32[4,64,128]{2,1,0:T(8,128)S(1)}, f32[4,64,128]{2,1,0:T(8,128)}, u32[]{:S(2)}) copy-start(f32[4,64,128]{2,1,0:T(8,128)} %diffusivity_ref.1) | copy-start | bytes 393220
  0.7 15.0 %copy-start.4 = (s32[4,64,128]{2,1,0:T(8,128)S(1)}, s32[4,64,128]{2,1,0:T(8,128)}, u32[]{:S(2)}) copy-start(s32[4,64,128]{2,1,0:T(8,128)} %mask_ref.1) | copy-start | bytes 393220
  7.1 22.8 %all-to-all-start = ((f32[16,80,128]{2,1,0:T(8,128)}), f32[16,80,128]{2,1,0:T(8,128)S(1)}, u32[]{:S(2)}, u32[]{:S(2)}) async-start(f32[16,80,128]{2,1,0:T(8,128)} %get-tuple-element.36), calls=%async_computation | async-start | bytes 1310720 | tf_op jit(solution)/shard_map/all_to_all | solution.py:615
  15.7 13.4 %collective-permute-start = (f32[2,4,24,128]{3,2,1,0:T(8,128)S(1)}, f32[2,4,24,128]{3,2,1,0:T(8,128)S(1)}, u32[]{:S(2)}, u32[]{:S(2)}) collective-permute-start(f32[2,4,24,128]{3,2,1,0:T(8,128)S(1)} %get-tuple-element.38), channel_id=1, source_target_pairs={{0,8},{8,0},{16,24},{24,16},{32,40},{40,32},{48,56},{56,48},{64,72... | collective-permute-start | bytes 294920 | tf_op jit(solution)/shard_map/ppermute | solution.py:611
  17.1 20.2 %copy-start.7 = (s32[4]{0:T(128)S(1)}, s32[4]{0:T(128)}, u32[]{:S(2)}) copy-start(s32[4]{0:T(128)} %count_ref.8) | copy-start | bytes 52
  17.1 36.3 %copy-start.3 = (f32[128,128]{1,0:T(8,128)S(1)}, f32[128,128]{1,0:T(8,128)}, u32[]{:S(2)}) copy-start(f32[128,128]{1,0:T(8,128)} %weight_ref.5) | copy-start | bytes 196612
  17.1 36.3 %copy-start.6 = (f32[128,128]{1,0:T(8,128)S(1)}, f32[128,128]{1,0:T(8,128)}, u32[]{:S(2)}) copy-start(f32[128,128]{1,0:T(8,128)} %get-tuple-element.48.earlier_ref) | copy-start | bytes 196612
  17.1 36.3 %copy-start.8 = (s32[128,1]{0,1:T(1,128)S(1)}, s32[128,1]{0,1:T(1,128)}, u32[]{:S(2)}) copy-start(s32[128,1]{0,1:T(1,128)} %param.13) | copy-start | bytes 1540
  17.1 12.9 %collective-permute-start.1 = (f32[2,4,24,128]{3,2,1,0:T(8,128)S(1)}, f32[2,4,24,128]{3,2,1,0:T(8,128)S(1)}, u32[]{:S(2)}, u32[]{:S(2)}) collective-permute-start(f32[2,4,24,128]{3,2,1,0:T(8,128)S(1)} %get-tuple-element.39), channel_id=1, source_target_pairs={{0,120},{8,16},{16,8},{24,32},{32,24},{40,48},{48,40},{56,64},{64,... | collective-permute-start | bytes 294920 | tf_op jit(solution)/shard_map/ppermute | solution.py:611
  30.0 0.7 copy-start.9
  31.3 6.0 %collective-permute-start.2 = (f32[2,112,128]{2,1,0:T(8,128)S(1)}, f32[2,112,128]{2,1,0:T(8,128)S(1)}, u32[]{:S(2)}, u32[]{:S(2)}) collective-permute-start(f32[2,112,128]{2,1,0:T(8,128)S(1)} %get-tuple-element.43), channel_id=1, source_target_pairs={{0,1},{1,0},{2,3},{3,2},{4,5},{5,4},{6,7},{7,6},{8,9},{9,8},{10,11... | collective-permute-start | bytes 344072 | tf_op jit(solution)/shard_map/ppermute | solution.py:611
  32.6 4.7 %collective-permute-start.3 = (f32[2,112,128]{2,1,0:T(8,128)S(1)}, f32[2,112,128]{2,1,0:T(8,128)S(1)}, u32[]{:S(2)}, u32[]{:S(2)}) collective-permute-start(f32[2,112,128]{2,1,0:T(8,128)S(1)} %get-tuple-element.44), channel_id=1, source_target_pairs={{0,7},{1,2},{2,1},{3,4},{4,3},{5,6},{6,5},{7,0},{8,15},{9,10},{10,... | collective-permute-start | bytes 344072 | tf_op jit(solution)/shard_map/ppermute | solution.py:611
  33.9 3.4 %copy-start = (f32[128,128,128]{2,1,0:T(8,128)S(1)}, f32[128,128,128]{2,1,0:T(8,128)}, u32[]{:S(2)}) copy-start(f32[128,128,128]{2,1,0:T(8,128)} %get-tuple-element.46._.turned_ref) | copy-start | bytes 25165828
  37.3 16.2 %copy-start.1 = (f32[128,128,128]{2,1,0:T(8,128)S(1)}, f32[128,128,128]{2,1,0:T(8,128)}, u32[]{:S(2)}) copy-start(f32[128,128,128]{2,1,0:T(8,128)} %get-tuple-element.46._.turned_ref) | copy-start | bytes 25165828
  69.0 5.8 %collective-permute-start.4 = (f32[1,112,128]{2,1,0:T(8,128)S(1)}, f32[1,112,128]{2,1,0:T(8,128)S(1)}, u32[]{:S(2)}, u32[]{:S(2)}) collective-permute-start(f32[1,112,128]{2,1,0:T(8,128)S(1)} %get-tuple-element.53), channel_id=1, source_target_pairs={{0,1},{1,0},{2,3},{3,2},{4,5},{5,4},{6,7},{7,6},{8,9},{9,8},{10,11... | collective-permute-start | bytes 172040 | tf_op jit(solution)/shard_map/ppermute | solution.py:611
  73.4 3.6 %collective-permute-start.5 = (f32[1,112,128]{2,1,0:T(8,128)S(1)}, f32[1,112,128]{2,1,0:T(8,128)S(1)}, u32[]{:S(2)}, u32[]{:S(2)}) collective-permute-start(f32[1,112,128]{2,1,0:T(8,128)S(1)} %get-tuple-element.54), channel_id=1, source_target_pairs={{0,7},{1,2},{2,1},{3,4},{4,3},{5,6},{6,5},{7,0},{8,15},{9,10},{10,... | collective-permute-start | bytes 172040 | tf_op jit(solution)/shard_map/ppermute | solution.py:611
  108.7 5.5 %collective-permute-start.6 = (f32[1,120,128]{2,1,0:T(8,128)S(1)}, f32[1,120,128]{2,1,0:T(8,128)S(1)}, u32[]{:S(2)}, u32[]{:S(2)}) collective-permute-start(f32[1,120,128]{2,1,0:T(8,128)S(1)} %get-tuple-element.64), channel_id=1, source_target_pairs={{0,1},{1,0},{2,3},{3,2},{4,5},{5,4},{6,7},{7,6},{8,9},{9,8},{10,11... | collective-permute-start | bytes 184328 | tf_op jit(solution)/shard_map/ppermute | solution.py:611
  113.2 3.6 %collective-permute-start.7 = (f32[1,120,128]{2,1,0:T(8,128)S(1)}, f32[1,120,128]{2,1,0:T(8,128)S(1)}, u32[]{:S(2)}, u32[]{:S(2)}) collective-permute-start(f32[1,120,128]{2,1,0:T(8,128)S(1)} %get-tuple-element.65), channel_id=1, source_target_pairs={{0,7},{1,2},{2,1},{3,4},{4,3},{5,6},{6,5},{7,0},{8,15},{9,10},{10,... | collective-permute-start | bytes 184328 | tf_op jit(solution)/shard_map/ppermute | solution.py:611
  116.9 9.2 %collective-permute-start.9 = (f32[8,128]{1,0:T(8,128)S(1)}, f32[8,128]{1,0:T(8,128)S(1)}, u32[]{:S(2)}, u32[]{:S(2)}) collective-permute-start(f32[8,128]{1,0:T(8,128)S(1)} %get-tuple-element.68), channel_id=1, source_target_pairs={{0,2},{1,3},{2,4},{3,5},{4,6},{5,7},{6,0},{7,1},{8,10},{9,11},{10,... | collective-permute-start | bytes 12296 | tf_op jit(solution)/shard_map/ppermute | solution.py:699
  117.8 8.2 %collective-permute-start.8 = (f32[8,128]{1,0:T(8,128)S(1)}, f32[8,128]{1,0:T(8,128)S(1)}, u32[]{:S(2)}, u32[]{:S(2)}) collective-permute-start(f32[8,128]{1,0:T(8,128)S(1)} %get-tuple-element.67.three_ref), channel_id=1, source_target_pairs={{0,5},{1,6},{2,7},{3,0},{4,1},{5,2},{6,3},{7,4},{8,13},{9,14},{10,... | collective-permute-start | bytes 12296 | tf_op jit(solution)/shard_map/ppermute | solution.py:698

commit v4 on v3

--- a/solution.py
+++ b/solution.py
@@ -13,7 +13,6 @@
 CY = 128
 NSTEP = 10
 MIN_STEPS = 5
-UNROLL = 5
 HALO = 2 * NSTEP
 SIDE = 24
 EXT = CX + 2 * SIDE
@@ -151,9 +150,7 @@
     write_parts(parts_ref, to_slots(tables, adjoint_ref[...]))
 
 
-def turn_kernel(operator_ref, turned_ref, done_ref, blocks_ref, lanes_ref, arrived, left):
-    done_ref[...] = jnp.zeros((8, 128), F32)
-
+def turn_kernel(operator_ref, turned_ref, blocks_ref, lanes_ref, arrived, left):
     def copy_of(number):
         return pltpu.make_async_copy(
             operator_ref.at[:, group(number), :], blocks_ref.at[number], arrived.at[number]
@@ -242,8 +239,8 @@
     return pl.pallas_call(
         turn_kernel,
         in_specs=[THERE],
-        out_specs=[THERE, HERE],
-        out_shape=[jax.ShapeDtypeStruct(CUBE, F32), SUMS],
+        out_specs=THERE,
+        out_shape=jax.ShapeDtypeStruct(CUBE, F32),
         scratch_shapes=[
             pltpu.VMEM((GROUPS, OWN, GROUP, 128), F32),
             pltpu.VMEM(CUBE, F32),
@@ -337,7 +334,7 @@
 
 
 def open_kernel(
-    parts_ref, sigma_ref, kappa_ref, near_ref, far_ref, _,
+    parts_ref, sigma_ref, kappa_ref, near_ref, far_ref,
     field_ref, sigma_ext_ref, kappa_ext_ref, pair_ref, other_ref, listed_ref, rows_ref,
 ):
     row_no = lax.axis_index("tx")
@@ -384,10 +381,8 @@
     sums_ref[...] = sums
 
 
-def meet_kernel(sums_ref, near_ref, far_ref, three_ref, two_ref):
-    near, far = near_ref[0, pl.ds(EXT, 8), :], far_ref[0, pl.ds(EXT, 8), :]
-    two_ref[...] = sums_ref[...] + jnp.where(parity("ty"), far, near)
-    three_ref[...] = sums_ref[...] + near + far
+def meet_kernel(sums_ref, near_ref, pair_ref):
+    pair_ref[...] = sums_ref[...] + near_ref[0, pl.ds(EXT, 8), :]
 
 
 def widen(work_ref, field_ref, west_of, east_of):
@@ -442,16 +437,8 @@
             work_ref[here, :] = now + change
             now = after
 
-    def run(start, end, masked, *rows):
-        def body(index, carry):
-            for k in range(UNROLL):
-                one(start + index * UNROLL + k, masked, *rows)
-            return carry
-
-        lax.fori_loop(0, (end - start) // UNROLL, body, 0)
-
-    run(0, MIN_STEPS, False, first_row, end_row)
-    run(MIN_STEPS, NSTEP, True, first_row + MIN_STEPS, end_row - MIN_STEPS)
+    for number in range(NSTEP):
+        one(number, number >= MIN_STEPS, first_row + number, end_row - number)
 
 
 def faces(work_ref, along_ref, across_ref):
@@ -553,9 +540,9 @@
 
 
 def finish_kernel(
-    last_ref, three_ref, next_ref, previous_ref, start_ref, image_ref, control_ref, residual_ref
+    last_ref, here_ref, one_ref, two_ref, three_ref, start_ref, image_ref, control_ref, residual_ref
 ):
-    sums = three_ref[...] + next_ref[...] + previous_ref[...]
+    sums = (here_ref[...] + one_ref[...]) + (two_ref[...] + three_ref[...])
     sums = jnp.sum(sums, axis=1, keepdims=True)
     start_start = sums[0:1]
     start_image = sums[0:1] + sums[1:2]
@@ -640,15 +627,14 @@
     )
     near_x, far_x = swap_neighbours(pair, other, "tx")
     parts, adjoint = run_first(owner_counts, tile, column, innovation, obs_weight, obs_operator)
-    turned, done = run_turn(obs_operator)
-    parts = exchange(parts)
+    turned = run_turn(obs_operator)
+    parts, turned = lax.optimization_barrier((exchange(parts), turned))
     field, sigma_ext, kappa_ext, pair, other, listed, rows = tile_call(
         open_kernel,
         (WIDENED, WIDENED, WIDENED, edge_shape(2), edge_shape(2), LISTS, TARGETS),
         (),
         (parts, background_std, kappa, near_x, far_x),
         "open_tile",
-        after=(done,),
     )
     near, far = swap_neighbours(pair, other, "ty")
     brought = tile_call(bring_kernel, (SUMS,), (), (listed, turned), "bring_blocks")
@@ -693,10 +679,10 @@
         "gather_last",
     )
     near, far = swap_neighbours(pair, other, "ty")
-    three, two = tile_call(meet_kernel, (SUMS, SUMS), (), (sums, near, far), "meet")
-    bands = lax.axis_size("ty")
-    after = lax.ppermute(three, "ty", [(i, (i - 3) % bands) for i in range(bands)])
-    before = lax.ppermute(two, "ty", [(i, (i + 2) % bands) for i in range(bands)])
+    chip = tile_call(meet_kernel, (SUMS,), (), (sums, near), "meet")[0]
+    chips = [
+        lax.ppermute(chip, "ty", [(i, i ^ k) for i in range(lax.axis_size("ty"))]) for k in (2, 4, 6)
+    ]
     last = tile_call(
         spread_last_kernel,
         (TILE,),
@@ -706,7 +692,7 @@
         WORK,
     )[0]
     control_field, residual = tile_call(
-        finish_kernel, (TILE, TILE), (), (last, three, after, before, once, image), "finish"
+        finish_kernel, (TILE, TILE), (), (last, chip, *chips, once, image), "finish"
     )
     return control_field, residual
 

time: 127 us -> 124 us (0.976)
  waiting for transfers between devices: 5.82 us -> 4.25 us
    ppermute x4, waiting for transfers between devices: 5.8 us -> 3.7 us  [swap_neighbours(): lax.ppermute(for_other, axis, others)]
    ppermute x2 -> x3, starting transfers between devices: 6.34 us -> 5.36 us  [body(): lax.ppermute(chip, 'ty', [(i, i ^ k) for i in range(lax.axis_size('ty'))])]
    unnamed x20 -> x18, local copies, waits for them, and re-layouts: 4.1 us -> 3.42 us
  transfers between devices with their start and end apart: 11 -> 12, of which waited for: 3 -> 3; matrix products, arithmetic and copies ran while one was open for 0% -> 0% of each run, Pallas kernels for 9% -> 8%
where the time goes in v4:
time: 124 us; the launch traced here: 123 us
  blocking collectives  45.9 us (37%)
  Pallas kernels  34.6 us (28%)
  starting transfers between devices  33.1 us (27%)
  waiting for transfers between devices  4.25 us (3%)
  local copies, waits for them, and re-layouts  3.42 us (3%)
  between operations  1.55 us (1%)
    all_to_all x4, blocking collectives, exchange(): return lax.all_to_all(parts, 'tx', split_axis=0, concat_axis=0, tiled=True)  45.9 us
    pallas_call x10, Pallas kernels, tile_call(): pl.pallas_call(kernel, in_specs=[SCALARS] * len(scalars) + [HERE] * len(a...  16.7 us
    ppermute x4, starting transfers between devices, swap_neighbours(): lax.ppermute(for_pair, axis, pairs)  11.8 us
    all_to_all x1, starting transfers between devices, exchange(): return lax.all_to_all(parts, 'tx', split_axis=0, concat_axis=0, tiled=True)  8.44 us
    ppermute x4, starting transfers between devices, swap_neighbours(): lax.ppermute(for_other, axis, others)  7.5 us
    pallas_call x1, Pallas kernels, run_turn(): pl.pallas_call(turn_kernel, in_specs=[THERE], out_specs=THERE, out_shape=...  7.42 us
    pallas_call x1, Pallas kernels, run_first(): pl.pallas_call(first_kernel, in_specs=[SCALARS, HERE, HERE, HERE, HERE, T...  5.77 us
    ppermute x3, starting transfers between devices, body(): lax.ppermute(chip, 'ty', [(i, i ^ k) for i in range(lax.axis_size('ty'))])  5.36 us
  transfers between devices with their start and end apart: 12, of which 3 were waited for; matrix products, arithmetic and copies ran while one was open for 0% of the time, Pallas kernels for 8%

profile of v4, /device:TPU:1, one launch (start us, length us, event | category | flops | bytes accessed | tf_op | source)
XLA Modules:
  0.0 122.9 jit_solution(8375178872981396508)
XLA Ops:
  1.4 5.8 %first_adjoint.1 = (f32[16,80,128]{2,1,0:T(8,128)}, f32[128,128]{1,0:T(8,128)}) custom-call(s32[1]{0:T(128)S(6)} %copy.12.count_ref, s32[1,128]{1,0:T(1,128)} %bitcast.10, s32[1,128]{1,0:T(1,128)} %bitcast.13, f32[128,128]{1,0:T(8,128)} %innovation_ref.1, f32[128,128]{1,0:T(8,128)} %weight_ref.5, f32[128,128,128]{2,1,0:T(8,128)} %operator_ref.3), custom_call_target="tpu_custom_call" | custom-call | flops 8388608 | bytes 9437184 | tf_op jit(solution)/shard_map/first_adjoint/pallas_call | solution.py:223
  7.1 8.4 %all-to-all-start = ((f32[16,80,128]{2,1,0:T(8,128)}), f32[16,80,128]{2,1,0:T(8,128)S(1)}, u32[]{:S(2)}, u32[]{:S(2)}) async-start(f32[16,80,128]{2,1,0:T(8,128)} %get-tuple-element.34), calls=%async_computation | async-start | bytes 1310720 | tf_op jit(solution)/shard_map/all_to_all | solution.py:602
  15.7 1.4 %collective-permute-start = (f32[2,4,24,128]{3,2,1,0:T(8,128)S(1)}, f32[2,4,24,128]{3,2,1,0:T(8,128)S(1)}, u32[]{:S(2)}, u32[]{:S(2)}) collective-permute-start(f32[2,4,24,128]{3,2,1,0:T(8,128)S(1)} %get-tuple-element.37), channel_id=1, source_target_pairs={{0,8},{8,0},{16,24},{24,16},{32,40},{40,32},{48,56},{56,48},{64,72... | collective-permute-start | bytes 294920 | tf_op jit(solution)/shard_map/ppermute | solution.py:598
  17.1 3.9 %collective-permute-start.1 = (f32[2,4,24,128]{3,2,1,0:T(8,128)S(1)}, f32[2,4,24,128]{3,2,1,0:T(8,128)S(1)}, u32[]{:S(2)}, u32[]{:S(2)}) collective-permute-start(f32[2,4,24,128]{3,2,1,0:T(8,128)S(1)} %get-tuple-element.38), channel_id=1, source_target_pairs={{0,120},{8,16},{16,8},{24,32},{32,24},{40,48},{48,40},{56,64},{64,... | collective-permute-start | bytes 294920 | tf_op jit(solution)/shard_map/ppermute | solution.py:598
  21.0 7.4 %blocks_on_lanes.1._.turned_ref = f32[128,128,128]{2,1,0:T(8,128)} custom-call(f32[128,128,128]{2,1,0:T(8,128)} %operator_ref.3), custom_call_target="tpu_custom_call" | custom-call | bytes 16777216 | tf_op jit(solution)/shard_map/blocks_on_lanes/pallas_call | solution.py:239
  28.5 1.5 %collective-permute-done.1.far_ref = f32[2,4,24,128]{3,2,1,0:T(8,128)S(1)} collective-permute-done((f32[2,4,24,128]{3,2,1,0:T(8,128)S(1)}, f32[2,4,24,128]{3,2,1,0:T(8,128)S(1)}, u32[]{:S(2)}, u32[]{:S(2)}) %collective-permute-start.1) | collective-permute-done | bytes 98336 | tf_op jit(solution)/shard_map/ppermute | solution.py:598
  30.6 1.4 %collective-permute-start.2 = (f32[2,112,128]{2,1,0:T(8,128)S(1)}, f32[2,112,128]{2,1,0:T(8,128)S(1)}, u32[]{:S(2)}, u32[]{:S(2)}) collective-permute-start(f32[2,112,128]{2,1,0:T(8,128)S(1)} %get-tuple-element.41), channel_id=1, source_target_pairs={{0,1},{1,0},{2,3},{3,2},{4,5},{5,4},{6,7},{7,6},{8,9},{9,8},{10,11... | collective-permute-start | bytes 344072 | tf_op jit(solution)/shard_map/ppermute | solution.py:598
  31.9 1.3 %collective-permute-start.3 = (f32[2,112,128]{2,1,0:T(8,128)S(1)}, f32[2,112,128]{2,1,0:T(8,128)S(1)}, u32[]{:S(2)}, u32[]{:S(2)}) collective-permute-start(f32[2,112,128]{2,1,0:T(8,128)S(1)} %get-tuple-element.42), channel_id=1, source_target_pairs={{0,7},{1,2},{2,1},{3,4},{4,3},{5,6},{6,5},{7,0},{8,15},{9,10},{10,... | collective-permute-start | bytes 344072 | tf_op jit(solution)/shard_map/ppermute | solution.py:598
  33.2 3.4 %copy-done = f32[128,128,128]{2,1,0:T(8,128)S(1)} copy-done((f32[128,128,128]{2,1,0:T(8,128)S(1)}, f32[128,128,128]{2,1,0:T(8,128)}, u32[]{:S(2)}) %copy-start) | copy-done | bytes 8388632
  36.6 6.0 %spread_first.1 = (f32[384,128]{1,0:T(8,128)S(1)}, f32[4,64,128]{2,1,0:T(8,128)S(1)}, f32[4,64,128]{2,1,0:T(8,128)S(1)}, f32[896,128]{1,0:T(8,128)S(1)}, f32[896,128]{1,0:T(8,128)S(1)}) custom-call(s32[4]{0:T(128)S(1)} %copy-done.7, f32[448,128]{1,0:T(8,128)S(1)} %get-tuple-element.39.field_ref, f32[448,128]{1,0:T(8,128)S(1)} %get-tuple-element.40.kappa_ext_ref, ...), custom_call_target="tpu_custom_call" | custom-call | tf_op jit(solution)/shard_map/spread_first/pallas_call | solution.py:583
  42.6 10.2 %all_to_all.25 = f32[16,24,128]{2,1,0:T(8,128)S(1)} all-to-all(f32[16,24,128]{2,1,0:T(8,128)S(1)} %bitcast.8), channel_id=1, replica_groups=mesh['tx'=16,'ty'=8] {'tx'}, dimensions={0} | all-to-all | bytes 393216 | tf_op jit(solution)/shard_map/all_to_all | solution.py:602
  52.9 2.2 %observe.2 = (f32[16,72,128]{2,1,0:T(8,128)S(1)}, f32[128,128]{1,0:T(8,128)S(1)}, f32[8,128]{1,0:T(8,128)S(1)}) custom-call(s32[1]{0:T(128)S(6)} %copy.12.count_ref, s32[1,128]{1,0:T(1,128)S(1)} %bitcast.11, f32[128,128]{1,0:T(8,128)S(1)} %copy-done.3, f32[384,128]{1,0:T(8,128)S(1)} %bitcast.7, f32[128,128]{1,0:T(8,128)S(1)} %copy-done.6, ...), custom_call_target="tpu_custom_call" | custom-call | flops 16777216 | bytes 10485760 | tf_op jit(solution)/shard_map/observe/pallas_call | solution.py:257
  55.0 12.8 %all_to_all.26.parts_ref = f32[16,72,128]{2,1,0:T(8,128)S(1)} all-to-all(f32[16,72,128]{2,1,0:T(8,128)S(1)} %get-tuple-element.47), channel_id=1, replica_groups=mesh['tx'=16,'ty'=8] {'tx'}, dimensions={0} | all-to-all | bytes 1179648 | tf_op jit(solution)/shard_map/all_to_all | solution.py:602
  68.2 4.5 %collective-permute-start.4 = (f32[1,112,128]{2,1,0:T(8,128)S(1)}, f32[1,112,128]{2,1,0:T(8,128)S(1)}, u32[]{:S(2)}, u32[]{:S(2)}) collective-permute-start(f32[1,112,128]{2,1,0:T(8,128)S(1)} %get-tuple-element.51), channel_id=1, source_target_pairs={{0,1},{1,0},{2,3},{3,2},{4,5},{5,4},{6,7},{7,6},{8,9},{9,8},{10,11... | collective-permute-start | bytes 172040 | tf_op jit(solution)/shard_map/ppermute | solution.py:598
  72.7 1.4 %collective-permute-start.5 = (f32[1,112,128]{2,1,0:T(8,128)S(1)}, f32[1,112,128]{2,1,0:T(8,128)S(1)}, u32[]{:S(2)}, u32[]{:S(2)}) collective-permute-start(f32[1,112,128]{2,1,0:T(8,128)S(1)} %get-tuple-element.52), channel_id=1, source_target_pairs={{0,7},{1,2},{2,1},{3,4},{4,3},{5,6},{6,5},{7,0},{8,15},{9,10},{10,... | collective-permute-start | bytes 172040 | tf_op jit(solution)/shard_map/ppermute | solution.py:598
  74.0 2.2 %collective-permute-done.5.far_ref = f32[1,112,128]{2,1,0:T(8,128)S(1)} collective-permute-done((f32[1,112,128]{2,1,0:T(8,128)S(1)}, f32[1,112,128]{2,1,0:T(8,128)S(1)}, u32[]{:S(2)}, u32[]{:S(2)}) %collective-permute-start.5) | collective-permute-done | bytes 57376 | tf_op jit(solution)/shard_map/ppermute | solution.py:598
  76.3 5.5 %spread_next.1 = (f32[384,128]{1,0:T(8,128)S(1)}, f32[4,64,128]{2,1,0:T(8,128)S(1)}) custom-call(s32[4]{0:T(128)S(1)} %copy-done.7, f32[448,128]{1,0:T(8,128)S(1)} %get-tuple-element.50.field_ref, f32[1,112,128]{2,1,0:T(8,128)S(1)} %collective-permute-done.4.near_ref, f32[1,112,128]{2,1,0:T(8,128)S(1)} %collective-permute-done.5.far_ref, ...), custom_call_target="tpu_custom_call" | custom-call | tf_op jit(solution)/shard_map/spread_next/pallas_call | solution.py:583
  81.8 10.0 %all_to_all.27 = f32[16,24,128]{2,1,0:T(8,128)S(1)} all-to-all(f32[16,24,128]{2,1,0:T(8,128)S(1)} %bitcast.9), channel_id=1, replica_groups=mesh['tx'=16,'ty'=8] {'tx'}, dimensions={0} | all-to-all | bytes 393216 | tf_op jit(solution)/shard_map/all_to_all | solution.py:602
  91.8 2.6 %observe.3 = (f32[16,80,128]{2,1,0:T(8,128)S(1)}, f32[128,128]{1,0:T(8,128)}, f32[8,128]{1,0:T(8,128)}) custom-call(s32[1]{0:T(128)S(6)} %copy.12.count_ref, s32[1,128]{1,0:T(1,128)S(1)} %bitcast.12, f32[128,128]{1,0:T(8,128)S(1)} %copy-done.3, f32[384,128]{1,0:T(8,128)S(1)} %bitcast.6, f32[128,128]{1,0:T(8,128)S(1)} %get-tuple-element.58.earlier_ref, ...), custom_call_target="tpu_custom_call" | custom-call | flops 16777216 | bytes 10485760 | tf_op jit(solution)/shard_map/observe/pallas_call | solution.py:257
  94.4 12.9 %all_to_all.28.parts_ref = f32[16,80,128]{2,1,0:T(8,128)S(1)} all-to-all(f32[16,80,128]{2,1,0:T(8,128)S(1)} %get-tuple-element.60), channel_id=1, replica_groups=mesh['tx'=16,'ty'=8] {'tx'}, dimensions={0} | all-to-all | bytes 1310720 | tf_op jit(solution)/shard_map/all_to_all | solution.py:602
  107.7 4.5 %collective-permute-start.6 = (f32[1,120,128]{2,1,0:T(8,128)S(1)}, f32[1,120,128]{2,1,0:T(8,128)S(1)}, u32[]{:S(2)}, u32[]{:S(2)}) collective-permute-start(f32[1,120,128]{2,1,0:T(8,128)S(1)} %get-tuple-element.62), channel_id=1, source_target_pairs={{0,1},{1,0},{2,3},{3,2},{4,5},{5,4},{6,7},{7,6},{8,9},{9,8},{10,11... | collective-permute-start | bytes 184328 | tf_op jit(solution)/shard_map/ppermute | solution.py:598
  112.3 1.0 collective-permute-start.7
  113.2 4.8 %collective-permute-start.10 = (f32[8,128]{1,0:T(8,128)S(1)}, f32[8,128]{1,0:T(8,128)S(1)}, u32[]{:S(2)}, u32[]{:S(2)}) collective-permute-start(f32[8,128]{1,0:T(8,128)S(1)} %meet.1.here_ref), channel_id=1, source_target_pairs={{0,6},{1,7},{2,4},{3,5},{4,2},{5,3},{6,0},{7,1},{8,14},{9,15},{10,... | collective-permute-start | bytes 12296 | tf_op jit(solution)/shard_map/ppermute | solution.py:684
  118.6 2.8 %spread_last.1.last_ref = f32[4,64,128]{2,1,0:T(8,128)S(1)} custom-call(s32[4]{0:T(128)S(1)} %copy-done.7, f32[448,128]{1,0:T(8,128)S(1)} %get-tuple-element.61.field_ref, f32[1,120,128]{2,1,0:T(8,128)S(1)} %collective-permute-done.6.near_ref, f32[1,120,128]{2,1,0:T(8,128)S(1)} %collective-permute-done.7.far_ref, ...), custom_call_target="tpu_custom_call" | custom-call | tf_op jit(solution)/shard_map/spread_last/pallas_call | solution.py:583
  (36 shorter events, 3.5 us)
Async XLA Ops:
  0.6 15.0 %copy-start.2 = (f32[4,64,128]{2,1,0:T(8,128)S(1)}, f32[4,64,128]{2,1,0:T(8,128)}, u32[]{:S(2)}) copy-start(f32[4,64,128]{2,1,0:T(8,128)} %sigma_ref.7) | copy-start | bytes 393220
  0.6 15.0 %copy-start.5 = (f32[4,64,128]{2,1,0:T(8,128)S(1)}, f32[4,64,128]{2,1,0:T(8,128)}, u32[]{:S(2)}) copy-start(f32[4,64,128]{2,1,0:T(8,128)} %diffusivity_ref.1) | copy-start | bytes 393220
  0.7 15.0 %copy-start.4 = (s32[4,64,128]{2,1,0:T(8,128)S(1)}, s32[4,64,128]{2,1,0:T(8,128)}, u32[]{:S(2)}) copy-start(s32[4,64,128]{2,1,0:T(8,128)} %mask_ref.1) | copy-start | bytes 393220
  7.1 21.3 %all-to-all-start = ((f32[16,80,128]{2,1,0:T(8,128)}), f32[16,80,128]{2,1,0:T(8,128)S(1)}, u32[]{:S(2)}, u32[]{:S(2)}) async-start(f32[16,80,128]{2,1,0:T(8,128)} %get-tuple-element.34), calls=%async_computation | async-start | bytes 1310720 | tf_op jit(solution)/shard_map/all_to_all | solution.py:602
  15.7 12.8 %collective-permute-start = (f32[2,4,24,128]{3,2,1,0:T(8,128)S(1)}, f32[2,4,24,128]{3,2,1,0:T(8,128)S(1)}, u32[]{:S(2)}, u32[]{:S(2)}) collective-permute-start(f32[2,4,24,128]{3,2,1,0:T(8,128)S(1)} %get-tuple-element.37), channel_id=1, source_target_pairs={{0,8},{8,0},{16,24},{24,16},{32,40},{40,32},{48,56},{56,48},{64,72... | collective-permute-start | bytes 294920 | tf_op jit(solution)/shard_map/ppermute | solution.py:598
  17.1 12.9 %collective-permute-start.1 = (f32[2,4,24,128]{3,2,1,0:T(8,128)S(1)}, f32[2,4,24,128]{3,2,1,0:T(8,128)S(1)}, u32[]{:S(2)}, u32[]{:S(2)}) collective-permute-start(f32[2,4,24,128]{3,2,1,0:T(8,128)S(1)} %get-tuple-element.38), channel_id=1, source_target_pairs={{0,120},{8,16},{16,8},{24,32},{32,24},{40,48},{48,40},{56,64},{64,... | collective-permute-start | bytes 294920 | tf_op jit(solution)/shard_map/ppermute | solution.py:598
  28.4 8.2 %copy-start.7 = (s32[4]{0:T(128)S(1)}, s32[4]{0:T(128)}, u32[]{:S(2)}) copy-start(s32[4]{0:T(128)} %count_ref.8) | copy-start | bytes 52
  28.4 24.4 %copy-start.3 = (f32[128,128]{1,0:T(8,128)S(1)}, f32[128,128]{1,0:T(8,128)}, u32[]{:S(2)}) copy-start(f32[128,128]{1,0:T(8,128)} %weight_ref.5) | copy-start | bytes 196612
  28.4 24.4 %copy-start.6 = (f32[128,128]{1,0:T(8,128)S(1)}, f32[128,128]{1,0:T(8,128)}, u32[]{:S(2)}) copy-start(f32[128,128]{1,0:T(8,128)} %get-tuple-element.46.earlier_ref) | copy-start | bytes 196612
  28.5 24.4 %copy-start.8 = (s32[128,1]{0,1:T(1,128)S(1)}, s32[128,1]{0,1:T(1,128)}, u32[]{:S(2)}) copy-start(s32[128,1]{0,1:T(1,128)} %param.13) | copy-start | bytes 1540
  30.6 6.0 %collective-permute-start.2 = (f32[2,112,128]{2,1,0:T(8,128)S(1)}, f32[2,112,128]{2,1,0:T(8,128)S(1)}, u32[]{:S(2)}, u32[]{:S(2)}) collective-permute-start(f32[2,112,128]{2,1,0:T(8,128)S(1)} %get-tuple-element.41), channel_id=1, source_target_pairs={{0,1},{1,0},{2,3},{3,2},{4,5},{5,4},{6,7},{7,6},{8,9},{9,8},{10,11... | collective-permute-start | bytes 344072 | tf_op jit(solution)/shard_map/ppermute | solution.py:598
  31.9 4.7 %collective-permute-start.3 = (f32[2,112,128]{2,1,0:T(8,128)S(1)}, f32[2,112,128]{2,1,0:T(8,128)S(1)}, u32[]{:S(2)}, u32[]{:S(2)}) collective-permute-start(f32[2,112,128]{2,1,0:T(8,128)S(1)} %get-tuple-element.42), channel_id=1, source_target_pairs={{0,7},{1,2},{2,1},{3,4},{4,3},{5,6},{6,5},{7,0},{8,15},{9,10},{10,... | collective-permute-start | bytes 344072 | tf_op jit(solution)/shard_map/ppermute | solution.py:598
  33.2 3.4 %copy-start = (f32[128,128,128]{2,1,0:T(8,128)S(1)}, f32[128,128,128]{2,1,0:T(8,128)}, u32[]{:S(2)}) copy-start(f32[128,128,128]{2,1,0:T(8,128)} %blocks_on_lanes.1._.turned_ref) | copy-start | bytes 25165828
  36.6 16.3 %copy-start.1 = (f32[128,128,128]{2,1,0:T(8,128)S(1)}, f32[128,128,128]{2,1,0:T(8,128)}, u32[]{:S(2)}) copy-start(f32[128,128,128]{2,1,0:T(8,128)} %blocks_on_lanes.1._.turned_ref) | copy-start | bytes 25165828
  68.2 5.8 %collective-permute-start.4 = (f32[1,112,128]{2,1,0:T(8,128)S(1)}, f32[1,112,128]{2,1,0:T(8,128)S(1)}, u32[]{:S(2)}, u32[]{:S(2)}) collective-permute-start(f32[1,112,128]{2,1,0:T(8,128)S(1)} %get-tuple-element.51), channel_id=1, source_target_pairs={{0,1},{1,0},{2,3},{3,2},{4,5},{5,4},{6,7},{7,6},{8,9},{9,8},{10,11... | collective-permute-start | bytes 172040 | tf_op jit(solution)/shard_map/ppermute | solution.py:598
  72.7 3.6 %collective-permute-start.5 = (f32[1,112,128]{2,1,0:T(8,128)S(1)}, f32[1,112,128]{2,1,0:T(8,128)S(1)}, u32[]{:S(2)}, u32[]{:S(2)}) collective-permute-start(f32[1,112,128]{2,1,0:T(8,128)S(1)} %get-tuple-element.52), channel_id=1, source_target_pairs={{0,7},{1,2},{2,1},{3,4},{4,3},{5,6},{6,5},{7,0},{8,15},{9,10},{10,... | collective-permute-start | bytes 172040 | tf_op jit(solution)/shard_map/ppermute | solution.py:598
  107.7 5.5 %collective-permute-start.6 = (f32[1,120,128]{2,1,0:T(8,128)S(1)}, f32[1,120,128]{2,1,0:T(8,128)S(1)}, u32[]{:S(2)}, u32[]{:S(2)}) collective-permute-start(f32[1,120,128]{2,1,0:T(8,128)S(1)} %get-tuple-element.62), channel_id=1, source_target_pairs={{0,1},{1,0},{2,3},{3,2},{4,5},{5,4},{6,7},{7,6},{8,9},{9,8},{10,11... | collective-permute-start | bytes 184328 | tf_op jit(solution)/shard_map/ppermute | solution.py:598
  112.3 6.3 %collective-permute-start.7 = (f32[1,120,128]{2,1,0:T(8,128)S(1)}, f32[1,120,128]{2,1,0:T(8,128)S(1)}, u32[]{:S(2)}, u32[]{:S(2)}) collective-permute-start(f32[1,120,128]{2,1,0:T(8,128)S(1)} %get-tuple-element.63), channel_id=1, source_target_pairs={{0,7},{1,2},{2,1},{3,4},{4,3},{5,6},{6,5},{7,0},{8,15},{9,10},{10,... | collective-permute-start | bytes 184328 | tf_op jit(solution)/shard_map/ppermute | solution.py:598
  113.2 8.2 %collective-permute-start.10 = (f32[8,128]{1,0:T(8,128)S(1)}, f32[8,128]{1,0:T(8,128)S(1)}, u32[]{:S(2)}, u32[]{:S(2)}) collective-permute-start(f32[8,128]{1,0:T(8,128)S(1)} %meet.1.here_ref), channel_id=1, source_target_pairs={{0,6},{1,7},{2,4},{3,5},{4,2},{5,3},{6,0},{7,1},{8,14},{9,15},{10,... | collective-permute-start | bytes 12296 | tf_op jit(solution)/shard_map/ppermute | solution.py:684
  118.0 4.0 %collective-permute-start.9 = (f32[8,128]{1,0:T(8,128)S(1)}, f32[8,128]{1,0:T(8,128)S(1)}, u32[]{:S(2)}, u32[]{:S(2)}) collective-permute-start(f32[8,128]{1,0:T(8,128)S(1)} %meet.1.here_ref), channel_id=1, source_target_pairs={{0,4},{1,5},{2,6},{3,7},{4,0},{5,1},{6,2},{7,3},{8,12},{9,13},{10,... | collective-permute-start | bytes 12296 | tf_op jit(solution)/shard_map/ppermute | solution.py:684
  118.4 3.6 %collective-permute-start.8 = (f32[8,128]{1,0:T(8,128)S(1)}, f32[8,128]{1,0:T(8,128)S(1)}, u32[]{:S(2)}, u32[]{:S(2)}) collective-permute-start(f32[8,128]{1,0:T(8,128)S(1)} %meet.1.here_ref), channel_id=1, source_target_pairs={{0,2},{1,3},{2,0},{3,1},{4,6},{5,7},{6,4},{7,5},{8,10},{9,11},{10,... | collective-permute-start | bytes 12296 | tf_op jit(solution)/shard_map/ppermute | solution.py:684

commit v5 on v4

--- a/solution.py
+++ b/solution.py
@@ -242,7 +242,7 @@
         out_specs=THERE,
         out_shape=jax.ShapeDtypeStruct(CUBE, F32),
         scratch_shapes=[
-            pltpu.VMEM((GROUPS, OWN, GROUP, 128), F32),
+            pltpu.VMEM((GROUPS + 1, OWN, GROUP, 128), F32),
             pltpu.VMEM(CUBE, F32),
             pltpu.SemaphoreType.DMA((GROUPS,)),
             pltpu.SemaphoreType.DMA((GROUPS,)),
@@ -566,7 +566,7 @@
         residual_ref[level] = remainder - second * curved
 
 
-WORK = [pltpu.VMEM((EXT * 8, 128), F32)]
+WORK = [pltpu.VMEM((EXT * 8 + 8, 128), F32)]
 TILE = jax.ShapeDtypeStruct((LEV, CX, CY), F32)
 WIDENED = jax.ShapeDtypeStruct((ROWS, 128), F32)
 LAID = jax.ShapeDtypeStruct((EXT * 8, 128), F32)

time: 124 us -> 124 us (level)
  no operation moved by 1% of the time
where the time goes in v5:
time: 124 us; the launch traced here: 123 us
  blocking collectives  45.9 us (37%)
  Pallas kernels  34.6 us (28%)
  starting transfers between devices  33.1 us (27%)
  waiting for transfers between devices  4.25 us (3%)
  local copies, waits for them, and re-layouts  3.42 us (3%)
  between operations  1.55 us (1%)
    all_to_all x4, blocking collectives, exchange(): return lax.all_to_all(parts, 'tx', split_axis=0, concat_axis=0, tiled=True)  45.9 us
    pallas_call x10, Pallas kernels, tile_call(): pl.pallas_call(kernel, in_specs=[SCALARS] * len(scalars) + [HERE] * len(a...  16.7 us
    ppermute x4, starting transfers between devices, swap_neighbours(): lax.ppermute(for_pair, axis, pairs)  11.8 us
    all_to_all x1, starting transfers between devices, exchange(): return lax.all_to_all(parts, 'tx', split_axis=0, concat_axis=0, tiled=True)  8.44 us
    ppermute x4, starting transfers between devices, swap_neighbours(): lax.ppermute(for_other, axis, others)  7.49 us
    pallas_call x1, Pallas kernels, run_turn(): pl.pallas_call(turn_kernel, in_specs=[THERE], out_specs=THERE, out_shape=...  7.42 us
    pallas_call x1, Pallas kernels, run_first(): pl.pallas_call(first_kernel, in_specs=[SCALARS, HERE, HERE, HERE, HERE, T...  5.77 us
    ppermute x3, starting transfers between devices, body(): lax.ppermute(chip, 'ty', [(i, i ^ k) for i in range(lax.axis_size('ty'))])  5.38 us
  transfers between devices with their start and end apart: 12, of which 3 were waited for; matrix products, arithmetic and copies ran while one was open for 0% of the time, Pallas kernels for 8%

profile of v5, /device:TPU:1, one launch (start us, length us, event | category | flops | bytes accessed | tf_op | source)
XLA Modules:
  0.0 122.9 jit_solution(17584617027553720467)
XLA Ops:
  1.4 5.8 %first_adjoint.1 = (f32[16,80,128]{2,1,0:T(8,128)}, f32[128,128]{1,0:T(8,128)}) custom-call(s32[1]{0:T(128)S(6)} %copy.12.count_ref, s32[1,128]{1,0:T(1,128)} %bitcast.10, s32[1,128]{1,0:T(1,128)} %bitcast.13, f32[128,128]{1,0:T(8,128)} %innovation_ref.1, f32[128,128]{1,0:T(8,128)} %weight_ref.5, f32[128,128,128]{2,1,0:T(8,128)} %operator_ref.3), custom_call_target="tpu_custom_call" | custom-call | flops 8388608 | bytes 9437184 | tf_op jit(solution)/shard_map/first_adjoint/pallas_call | solution.py:223
  7.1 8.4 %all-to-all-start = ((f32[16,80,128]{2,1,0:T(8,128)}), f32[16,80,128]{2,1,0:T(8,128)S(1)}, u32[]{:S(2)}, u32[]{:S(2)}) async-start(f32[16,80,128]{2,1,0:T(8,128)} %get-tuple-element.34), calls=%async_computation | async-start | bytes 1310720 | tf_op jit(solution)/shard_map/all_to_all | solution.py:602
  15.7 1.4 %collective-permute-start = (f32[2,4,24,128]{3,2,1,0:T(8,128)S(1)}, f32[2,4,24,128]{3,2,1,0:T(8,128)S(1)}, u32[]{:S(2)}, u32[]{:S(2)}) collective-permute-start(f32[2,4,24,128]{3,2,1,0:T(8,128)S(1)} %get-tuple-element.37), channel_id=1, source_target_pairs={{0,8},{8,0},{16,24},{24,16},{32,40},{40,32},{48,56},{56,48},{64,72... | collective-permute-start | bytes 294920 | tf_op jit(solution)/shard_map/ppermute | solution.py:598
  17.1 3.9 %collective-permute-start.1 = (f32[2,4,24,128]{3,2,1,0:T(8,128)S(1)}, f32[2,4,24,128]{3,2,1,0:T(8,128)S(1)}, u32[]{:S(2)}, u32[]{:S(2)}) collective-permute-start(f32[2,4,24,128]{3,2,1,0:T(8,128)S(1)} %get-tuple-element.38), channel_id=1, source_target_pairs={{0,120},{8,16},{16,8},{24,32},{32,24},{40,48},{48,40},{56,64},{64,... | collective-permute-start | bytes 294920 | tf_op jit(solution)/shard_map/ppermute | solution.py:598
  21.0 7.4 %blocks_on_lanes.1._.turned_ref = f32[128,128,128]{2,1,0:T(8,128)} custom-call(f32[128,128,128]{2,1,0:T(8,128)} %operator_ref.3), custom_call_target="tpu_custom_call" | custom-call | bytes 16777216 | tf_op jit(solution)/shard_map/blocks_on_lanes/pallas_call | solution.py:239
  28.5 1.5 %collective-permute-done.1.far_ref = f32[2,4,24,128]{3,2,1,0:T(8,128)S(1)} collective-permute-done((f32[2,4,24,128]{3,2,1,0:T(8,128)S(1)}, f32[2,4,24,128]{3,2,1,0:T(8,128)S(1)}, u32[]{:S(2)}, u32[]{:S(2)}) %collective-permute-start.1) | collective-permute-done | bytes 98336 | tf_op jit(solution)/shard_map/ppermute | solution.py:598
  30.6 1.4 %collective-permute-start.2 = (f32[2,112,128]{2,1,0:T(8,128)S(1)}, f32[2,112,128]{2,1,0:T(8,128)S(1)}, u32[]{:S(2)}, u32[]{:S(2)}) collective-permute-start(f32[2,112,128]{2,1,0:T(8,128)S(1)} %get-tuple-element.41), channel_id=1, source_target_pairs={{0,1},{1,0},{2,3},{3,2},{4,5},{5,4},{6,7},{7,6},{8,9},{9,8},{10,11... | collective-permute-start | bytes 344072 | tf_op jit(solution)/shard_map/ppermute | solution.py:598
  31.9 1.3 %collective-permute-start.3 = (f32[2,112,128]{2,1,0:T(8,128)S(1)}, f32[2,112,128]{2,1,0:T(8,128)S(1)}, u32[]{:S(2)}, u32[]{:S(2)}) collective-permute-start(f32[2,112,128]{2,1,0:T(8,128)S(1)} %get-tuple-element.42), channel_id=1, source_target_pairs={{0,7},{1,2},{2,1},{3,4},{4,3},{5,6},{6,5},{7,0},{8,15},{9,10},{10,... | collective-permute-start | bytes 344072 | tf_op jit(solution)/shard_map/ppermute | solution.py:598
  33.2 3.4 %copy-done = f32[128,128,128]{2,1,0:T(8,128)S(1)} copy-done((f32[128,128,128]{2,1,0:T(8,128)S(1)}, f32[128,128,128]{2,1,0:T(8,128)}, u32[]{:S(2)}) %copy-start) | copy-done | bytes 8388632
  36.6 6.0 %spread_first.1 = (f32[384,128]{1,0:T(8,128)S(1)}, f32[4,64,128]{2,1,0:T(8,128)S(1)}, f32[4,64,128]{2,1,0:T(8,128)S(1)}, f32[896,128]{1,0:T(8,128)S(1)}, f32[896,128]{1,0:T(8,128)S(1)}) custom-call(s32[4]{0:T(128)S(1)} %copy-done.7, f32[448,128]{1,0:T(8,128)S(1)} %get-tuple-element.39.field_ref, f32[448,128]{1,0:T(8,128)S(1)} %get-tuple-element.40.kappa_ext_ref, ...), custom_call_target="tpu_custom_call" | custom-call | tf_op jit(solution)/shard_map/spread_first/pallas_call | solution.py:583
  42.6 10.2 %all_to_all.25 = f32[16,24,128]{2,1,0:T(8,128)S(1)} all-to-all(f32[16,24,128]{2,1,0:T(8,128)S(1)} %bitcast.8), channel_id=1, replica_groups=mesh['tx'=16,'ty'=8] {'tx'}, dimensions={0} | all-to-all | bytes 393216 | tf_op jit(solution)/shard_map/all_to_all | solution.py:602
  52.8 2.2 %observe.2 = (f32[16,72,128]{2,1,0:T(8,128)S(1)}, f32[128,128]{1,0:T(8,128)S(1)}, f32[8,128]{1,0:T(8,128)S(1)}) custom-call(s32[1]{0:T(128)S(6)} %copy.12.count_ref, s32[1,128]{1,0:T(1,128)S(1)} %bitcast.11, f32[128,128]{1,0:T(8,128)S(1)} %copy-done.3, f32[384,128]{1,0:T(8,128)S(1)} %bitcast.7, f32[128,128]{1,0:T(8,128)S(1)} %copy-done.6, ...), custom_call_target="tpu_custom_call" | custom-call | flops 16777216 | bytes 10485760 | tf_op jit(solution)/shard_map/observe/pallas_call | solution.py:257
  55.0 12.8 %all_to_all.26.parts_ref = f32[16,72,128]{2,1,0:T(8,128)S(1)} all-to-all(f32[16,72,128]{2,1,0:T(8,128)S(1)} %get-tuple-element.47), channel_id=1, replica_groups=mesh['tx'=16,'ty'=8] {'tx'}, dimensions={0} | all-to-all | bytes 1179648 | tf_op jit(solution)/shard_map/all_to_all | solution.py:602
  68.2 4.5 %collective-permute-start.4 = (f32[1,112,128]{2,1,0:T(8,128)S(1)}, f32[1,112,128]{2,1,0:T(8,128)S(1)}, u32[]{:S(2)}, u32[]{:S(2)}) collective-permute-start(f32[1,112,128]{2,1,0:T(8,128)S(1)} %get-tuple-element.51), channel_id=1, source_target_pairs={{0,1},{1,0},{2,3},{3,2},{4,5},{5,4},{6,7},{7,6},{8,9},{9,8},{10,11... | collective-permute-start | bytes 172040 | tf_op jit(solution)/shard_map/ppermute | solution.py:598
  72.7 1.4 %collective-permute-start.5 = (f32[1,112,128]{2,1,0:T(8,128)S(1)}, f32[1,112,128]{2,1,0:T(8,128)S(1)}, u32[]{:S(2)}, u32[]{:S(2)}) collective-permute-start(f32[1,112,128]{2,1,0:T(8,128)S(1)} %get-tuple-element.52), channel_id=1, source_target_pairs={{0,7},{1,2},{2,1},{3,4},{4,3},{5,6},{6,5},{7,0},{8,15},{9,10},{10,... | collective-permute-start | bytes 172040 | tf_op jit(solution)/shard_map/ppermute | solution.py:598
  74.0 2.2 %collective-permute-done.5.far_ref = f32[1,112,128]{2,1,0:T(8,128)S(1)} collective-permute-done((f32[1,112,128]{2,1,0:T(8,128)S(1)}, f32[1,112,128]{2,1,0:T(8,128)S(1)}, u32[]{:S(2)}, u32[]{:S(2)}) %collective-permute-start.5) | collective-permute-done | bytes 57376 | tf_op jit(solution)/shard_map/ppermute | solution.py:598
  76.3 5.5 %spread_next.1 = (f32[384,128]{1,0:T(8,128)S(1)}, f32[4,64,128]{2,1,0:T(8,128)S(1)}) custom-call(s32[4]{0:T(128)S(1)} %copy-done.7, f32[448,128]{1,0:T(8,128)S(1)} %get-tuple-element.50.field_ref, f32[1,112,128]{2,1,0:T(8,128)S(1)} %collective-permute-done.4.near_ref, f32[1,112,128]{2,1,0:T(8,128)S(1)} %collective-permute-done.5.far_ref, ...), custom_call_target="tpu_custom_call" | custom-call | tf_op jit(solution)/shard_map/spread_next/pallas_call | solution.py:583
  81.8 10.0 %all_to_all.27 = f32[16,24,128]{2,1,0:T(8,128)S(1)} all-to-all(f32[16,24,128]{2,1,0:T(8,128)S(1)} %bitcast.9), channel_id=1, replica_groups=mesh['tx'=16,'ty'=8] {'tx'}, dimensions={0} | all-to-all | bytes 393216 | tf_op jit(solution)/shard_map/all_to_all | solution.py:602
  91.8 2.6 %observe.3 = (f32[16,80,128]{2,1,0:T(8,128)S(1)}, f32[128,128]{1,0:T(8,128)}, f32[8,128]{1,0:T(8,128)}) custom-call(s32[1]{0:T(128)S(6)} %copy.12.count_ref, s32[1,128]{1,0:T(1,128)S(1)} %bitcast.12, f32[128,128]{1,0:T(8,128)S(1)} %copy-done.3, f32[384,128]{1,0:T(8,128)S(1)} %bitcast.6, f32[128,128]{1,0:T(8,128)S(1)} %get-tuple-element.58.earlier_ref, ...), custom_call_target="tpu_custom_call" | custom-call | flops 16777216 | bytes 10485760 | tf_op jit(solution)/shard_map/observe/pallas_call | solution.py:257
  94.4 12.9 %all_to_all.28.parts_ref = f32[16,80,128]{2,1,0:T(8,128)S(1)} all-to-all(f32[16,80,128]{2,1,0:T(8,128)S(1)} %get-tuple-element.60), channel_id=1, replica_groups=mesh['tx'=16,'ty'=8] {'tx'}, dimensions={0} | all-to-all | bytes 1310720 | tf_op jit(solution)/shard_map/all_to_all | solution.py:602
  107.7 4.5 %collective-permute-start.6 = (f32[1,120,128]{2,1,0:T(8,128)S(1)}, f32[1,120,128]{2,1,0:T(8,128)S(1)}, u32[]{:S(2)}, u32[]{:S(2)}) collective-permute-start(f32[1,120,128]{2,1,0:T(8,128)S(1)} %get-tuple-element.62), channel_id=1, source_target_pairs={{0,1},{1,0},{2,3},{3,2},{4,5},{5,4},{6,7},{7,6},{8,9},{9,8},{10,11... | collective-permute-start | bytes 184328 | tf_op jit(solution)/shard_map/ppermute | solution.py:598
  112.3 0.9 collective-permute-start.7
  113.2 4.8 %collective-permute-start.10 = (f32[8,128]{1,0:T(8,128)S(1)}, f32[8,128]{1,0:T(8,128)S(1)}, u32[]{:S(2)}, u32[]{:S(2)}) collective-permute-start(f32[8,128]{1,0:T(8,128)S(1)} %meet.1.here_ref), channel_id=1, source_target_pairs={{0,6},{1,7},{2,4},{3,5},{4,2},{5,3},{6,0},{7,1},{8,14},{9,15},{10,... | collective-permute-start | bytes 12296 | tf_op jit(solution)/shard_map/ppermute | solution.py:684
  118.6 2.8 %spread_last.1.last_ref = f32[4,64,128]{2,1,0:T(8,128)S(1)} custom-call(s32[4]{0:T(128)S(1)} %copy-done.7, f32[448,128]{1,0:T(8,128)S(1)} %get-tuple-element.61.field_ref, f32[1,120,128]{2,1,0:T(8,128)S(1)} %collective-permute-done.6.near_ref, f32[1,120,128]{2,1,0:T(8,128)S(1)} %collective-permute-done.7.far_ref, ...), custom_call_target="tpu_custom_call" | custom-call | tf_op jit(solution)/shard_map/spread_last/pallas_call | solution.py:583
  (36 shorter events, 3.5 us)
Async XLA Ops:
  0.6 15.0 %copy-start.2 = (f32[4,64,128]{2,1,0:T(8,128)S(1)}, f32[4,64,128]{2,1,0:T(8,128)}, u32[]{:S(2)}) copy-start(f32[4,64,128]{2,1,0:T(8,128)} %sigma_ref.7) | copy-start | bytes 393220
  0.6 15.0 %copy-start.5 = (f32[4,64,128]{2,1,0:T(8,128)S(1)}, f32[4,64,128]{2,1,0:T(8,128)}, u32[]{:S(2)}) copy-start(f32[4,64,128]{2,1,0:T(8,128)} %diffusivity_ref.1) | copy-start | bytes 393220
  0.7 15.0 %copy-start.4 = (s32[4,64,128]{2,1,0:T(8,128)S(1)}, s32[4,64,128]{2,1,0:T(8,128)}, u32[]{:S(2)}) copy-start(s32[4,64,128]{2,1,0:T(8,128)} %mask_ref.1) | copy-start | bytes 393220
  7.1 21.3 %all-to-all-start = ((f32[16,80,128]{2,1,0:T(8,128)}), f32[16,80,128]{2,1,0:T(8,128)S(1)}, u32[]{:S(2)}, u32[]{:S(2)}) async-start(f32[16,80,128]{2,1,0:T(8,128)} %get-tuple-element.34), calls=%async_computation | async-start | bytes 1310720 | tf_op jit(solution)/shard_map/all_to_all | solution.py:602
  15.7 12.8 %collective-permute-start = (f32[2,4,24,128]{3,2,1,0:T(8,128)S(1)}, f32[2,4,24,128]{3,2,1,0:T(8,128)S(1)}, u32[]{:S(2)}, u32[]{:S(2)}) collective-permute-start(f32[2,4,24,128]{3,2,1,0:T(8,128)S(1)} %get-tuple-element.37), channel_id=1, source_target_pairs={{0,8},{8,0},{16,24},{24,16},{32,40},{40,32},{48,56},{56,48},{64,72... | collective-permute-start | bytes 294920 | tf_op jit(solution)/shard_map/ppermute | solution.py:598
  17.1 12.9 %collective-permute-start.1 = (f32[2,4,24,128]{3,2,1,0:T(8,128)S(1)}, f32[2,4,24,128]{3,2,1,0:T(8,128)S(1)}, u32[]{:S(2)}, u32[]{:S(2)}) collective-permute-start(f32[2,4,24,128]{3,2,1,0:T(8,128)S(1)} %get-tuple-element.38), channel_id=1, source_target_pairs={{0,120},{8,16},{16,8},{24,32},{32,24},{40,48},{48,40},{56,64},{64,... | collective-permute-start | bytes 294920 | tf_op jit(solution)/shard_map/ppermute | solution.py:598
  28.4 8.2 %copy-start.7 = (s32[4]{0:T(128)S(1)}, s32[4]{0:T(128)}, u32[]{:S(2)}) copy-start(s32[4]{0:T(128)} %count_ref.8) | copy-start | bytes 52
  28.4 24.4 %copy-start.3 = (f32[128,128]{1,0:T(8,128)S(1)}, f32[128,128]{1,0:T(8,128)}, u32[]{:S(2)}) copy-start(f32[128,128]{1,0:T(8,128)} %weight_ref.5) | copy-start | bytes 196612
  28.4 24.4 %copy-start.6 = (f32[128,128]{1,0:T(8,128)S(1)}, f32[128,128]{1,0:T(8,128)}, u32[]{:S(2)}) copy-start(f32[128,128]{1,0:T(8,128)} %get-tuple-element.46.earlier_ref) | copy-start | bytes 196612
  28.5 24.4 %copy-start.8 = (s32[128,1]{0,1:T(1,128)S(1)}, s32[128,1]{0,1:T(1,128)}, u32[]{:S(2)}) copy-start(s32[128,1]{0,1:T(1,128)} %param.13) | copy-start | bytes 1540
  30.6 6.0 %collective-permute-start.2 = (f32[2,112,128]{2,1,0:T(8,128)S(1)}, f32[2,112,128]{2,1,0:T(8,128)S(1)}, u32[]{:S(2)}, u32[]{:S(2)}) collective-permute-start(f32[2,112,128]{2,1,0:T(8,128)S(1)} %get-tuple-element.41), channel_id=1, source_target_pairs={{0,1},{1,0},{2,3},{3,2},{4,5},{5,4},{6,7},{7,6},{8,9},{9,8},{10,11... | collective-permute-start | bytes 344072 | tf_op jit(solution)/shard_map/ppermute | solution.py:598
  31.9 4.7 %collective-permute-start.3 = (f32[2,112,128]{2,1,0:T(8,128)S(1)}, f32[2,112,128]{2,1,0:T(8,128)S(1)}, u32[]{:S(2)}, u32[]{:S(2)}) collective-permute-start(f32[2,112,128]{2,1,0:T(8,128)S(1)} %get-tuple-element.42), channel_id=1, source_target_pairs={{0,7},{1,2},{2,1},{3,4},{4,3},{5,6},{6,5},{7,0},{8,15},{9,10},{10,... | collective-permute-start | bytes 344072 | tf_op jit(solution)/shard_map/ppermute | solution.py:598
  33.2 3.4 %copy-start = (f32[128,128,128]{2,1,0:T(8,128)S(1)}, f32[128,128,128]{2,1,0:T(8,128)}, u32[]{:S(2)}) copy-start(f32[128,128,128]{2,1,0:T(8,128)} %blocks_on_lanes.1._.turned_ref) | copy-start | bytes 25165828
  36.6 16.2 %copy-start.1 = (f32[128,128,128]{2,1,0:T(8,128)S(1)}, f32[128,128,128]{2,1,0:T(8,128)}, u32[]{:S(2)}) copy-start(f32[128,128,128]{2,1,0:T(8,128)} %blocks_on_lanes.1._.turned_ref) | copy-start | bytes 25165828
  68.2 5.8 %collective-permute-start.4 = (f32[1,112,128]{2,1,0:T(8,128)S(1)}, f32[1,112,128]{2,1,0:T(8,128)S(1)}, u32[]{:S(2)}, u32[]{:S(2)}) collective-permute-start(f32[1,112,128]{2,1,0:T(8,128)S(1)} %get-tuple-element.51), channel_id=1, source_target_pairs={{0,1},{1,0},{2,3},{3,2},{4,5},{5,4},{6,7},{7,6},{8,9},{9,8},{10,11... | collective-permute-start | bytes 172040 | tf_op jit(solution)/shard_map/ppermute | solution.py:598
  72.7 3.6 %collective-permute-start.5 = (f32[1,112,128]{2,1,0:T(8,128)S(1)}, f32[1,112,128]{2,1,0:T(8,128)S(1)}, u32[]{:S(2)}, u32[]{:S(2)}) collective-permute-start(f32[1,112,128]{2,1,0:T(8,128)S(1)} %get-tuple-element.52), channel_id=1, source_target_pairs={{0,7},{1,2},{2,1},{3,4},{4,3},{5,6},{6,5},{7,0},{8,15},{9,10},{10,... | collective-permute-start | bytes 172040 | tf_op jit(solution)/shard_map/ppermute | solution.py:598
  107.7 5.5 %collective-permute-start.6 = (f32[1,120,128]{2,1,0:T(8,128)S(1)}, f32[1,120,128]{2,1,0:T(8,128)S(1)}, u32[]{:S(2)}, u32[]{:S(2)}) collective-permute-start(f32[1,120,128]{2,1,0:T(8,128)S(1)} %get-tuple-element.62), channel_id=1, source_target_pairs={{0,1},{1,0},{2,3},{3,2},{4,5},{5,4},{6,7},{7,6},{8,9},{9,8},{10,11... | collective-permute-start | bytes 184328 | tf_op jit(solution)/shard_map/ppermute | solution.py:598
  112.3 6.3 %collective-permute-start.7 = (f32[1,120,128]{2,1,0:T(8,128)S(1)}, f32[1,120,128]{2,1,0:T(8,128)S(1)}, u32[]{:S(2)}, u32[]{:S(2)}) collective-permute-start(f32[1,120,128]{2,1,0:T(8,128)S(1)} %get-tuple-element.63), channel_id=1, source_target_pairs={{0,7},{1,2},{2,1},{3,4},{4,3},{5,6},{6,5},{7,0},{8,15},{9,10},{10,... | collective-permute-start | bytes 184328 | tf_op jit(solution)/shard_map/ppermute | solution.py:598
  113.2 8.2 %collective-permute-start.10 = (f32[8,128]{1,0:T(8,128)S(1)}, f32[8,128]{1,0:T(8,128)S(1)}, u32[]{:S(2)}, u32[]{:S(2)}) collective-permute-start(f32[8,128]{1,0:T(8,128)S(1)} %meet.1.here_ref), channel_id=1, source_target_pairs={{0,6},{1,7},{2,4},{3,5},{4,2},{5,3},{6,0},{7,1},{8,14},{9,15},{10,... | collective-permute-start | bytes 12296 | tf_op jit(solution)/shard_map/ppermute | solution.py:684
  118.0 4.0 %collective-permute-start.9 = (f32[8,128]{1,0:T(8,128)S(1)}, f32[8,128]{1,0:T(8,128)S(1)}, u32[]{:S(2)}, u32[]{:S(2)}) collective-permute-start(f32[8,128]{1,0:T(8,128)S(1)} %meet.1.here_ref), channel_id=1, source_target_pairs={{0,4},{1,5},{2,6},{3,7},{4,0},{5,1},{6,2},{7,3},{8,12},{9,13},{10,... | collective-permute-start | bytes 12296 | tf_op jit(solution)/shard_map/ppermute | solution.py:684
  118.4 3.6 %collective-permute-start.8 = (f32[8,128]{1,0:T(8,128)S(1)}, f32[8,128]{1,0:T(8,128)S(1)}, u32[]{:S(2)}, u32[]{:S(2)}) collective-permute-start(f32[8,128]{1,0:T(8,128)S(1)} %meet.1.here_ref), channel_id=1, source_target_pairs={{0,2},{1,3},{2,0},{3,1},{4,6},{5,7},{6,4},{7,5},{8,10},{9,11},{10,... | collective-permute-start | bytes 12296 | tf_op jit(solution)/shard_map/ppermute | solution.py:684
